TPU v7x, 32 devices: a whole 2x2x4 slice. The times are simulated.
32 devices in a mesh: replica: 8 (over z, x), fsdp: 4 (over y, core).
Axes of the slice: x: 2, y: 2, z: 4, core: 2. Of those that a mesh axis runs over, the one named last changes fastest.
Arguments:
- hidden_in: bfloat16 [2, 32, 256, 2048], P(None, ('replica', 'fsdp')), may hold values from -6 to 6
- segment_ids: int32 [2, 32, 256], P(None, ('replica', 'fsdp')), may hold values from 0 to 15, never falling along the last dimension, each value on 1 to 128 neighbouring positions
- cotangent: bfloat16 [2, 32, 256, 2048], P(None, ('replica', 'fsdp')), may hold values from -6 to 6
- norm_gain: bfloat16 [2048], P('fsdp'), may hold values from 0.099609375 to 1.8984375
- w_in: bfloat16 [2048, 8512], P('fsdp'), may hold values from -0.125 to 0.125
- conv_weight: bfloat16 [4, 4352], P(None, 'fsdp'), may hold values from -3 to 3
- conv_bias: bfloat16 [4352], P('fsdp'), may hold values from -0.5 to 0.5
- dt_bias: bfloat16 [64], P('fsdp'), may hold values from -6 to -2
- a_log: bfloat16 [64], P('fsdp'), may hold values from 0 to 2
- skip_gain: bfloat16 [64], P('fsdp'), may hold values from 0.5 to 1.5
- gate_gain: bfloat16 [4096], P('fsdp'), may hold values from 0.099609375 to 1.8984375
- w_out: bfloat16 [4096, 2048], P('fsdp'), may hold values from -0.09375 to 0.09375
Outputs:
- block_out: bfloat16 [2, 32, 256, 2048], P(None, ('replica', 'fsdp'))
- grad_in: float32 [2, 32, 256, 2048], P(None, ('replica', 'fsdp'))
- grad_norm_gain: float32 [2048], P('fsdp')
- grad_w_in: float32 [2048, 8512], P('fsdp')
- grad_conv_weight: float32 [4, 4352], P(None, 'fsdp')
- grad_conv_bias: float32 [4352], P('fsdp')
- grad_dt_bias: float32 [64], P('fsdp')
- grad_a_log: float32 [64], P('fsdp')
- grad_skip_gain: float32 [64], P('fsdp')
- grad_gate_gain: float32 [4096], P('fsdp')
- grad_w_out: float32 [4096, 2048], P('fsdp')
Inputs may be any that keep to these rules, and one draw needn't show every extreme that they name: `segment_ids`: along each sequence the numbers never fall; each document has 1 to 128 tokens.
All inputs are finite; a program needn't handle non-finite values.
Results may differ from a plain program's by a relative error of at most 0.0077.
Values may be sent and summed in bfloat16 or wider, within the bound.
A program may use at most 384 MiB of HBM per device.

v0:
```python
import jax
import jax.numpy as jnp
from jax import lax
from jax.sharding import PartitionSpec as P

EPS = 1e-05
HIGHEST = lax.Precision.HIGHEST


def pre_norm(inputs, gain):
    square_mean = jnp.mean(inputs * inputs, -1, keepdims=True)
    return inputs * lax.rsqrt(square_mean + EPS) * gain


def mixer(projected, conv_weight, conv_bias, dt_bias, a_log, skip_gain, gate_gain, segments):
    length = projected.shape[0]
    inner_width = gate_gain.shape[0]
    head_count = dt_bias.shape[0]
    conv_width = conv_bias.shape[0]
    state_width = (conv_width - inner_width) // 2
    head_width = inner_width // head_count
    kernel_width = conv_weight.shape[0]
    gate_part = projected[:, :inner_width]
    conv_input = projected[:, inner_width : inner_width + conv_width]
    step_raw = projected[:, inner_width + conv_width :]
    convolved = conv_bias + conv_weight[0] * conv_input
    for offset in range(1, kernel_width):
        prior = jnp.concatenate(
            [jnp.zeros((offset, conv_width), projected.dtype), conv_input[:-offset]], 0
        )
        same_doc = jnp.concatenate(
            [
                jnp.zeros((offset,), projected.dtype),
                (segments[offset:] == segments[:-offset]).astype(projected.dtype),
            ],
            0,
        )
        convolved = convolved + conv_weight[offset] * prior * same_doc[:, None]
    activated = jax.nn.silu(convolved)
    values_in = activated[:, :inner_width].reshape(length, head_count, head_width)
    state_in = activated[:, inner_width : inner_width + state_width]
    state_out = activated[:, inner_width + state_width :]
    step_size = jax.nn.softplus(step_raw + dt_bias)
    log_decay = -jnp.exp(a_log) * step_size
    cumulative = jnp.cumsum(log_decay, 0)
    position = jnp.arange(length)
    visible = (position[:, None] >= position[None, :]) & (segments[:, None] == segments[None, :])
    distance = jnp.where(visible[:, :, None], cumulative[:, None, :] - cumulative[None, :, :], 0.0)
    decays = jnp.where(visible[:, :, None], jnp.exp(distance), 0.0)
    affinity = jnp.dot(state_out, state_in.T, precision=HIGHEST)
    weights_ts = affinity[:, :, None] * decays * step_size[None, :, :]
    output_sum = (
        jnp.einsum("tsh,shp->thp", weights_ts, values_in, precision=HIGHEST)
        + skip_gain[:, None] * values_in
    )
    output_sum = output_sum.reshape(length, inner_width)
    gated_out = output_sum * jax.nn.silu(gate_part)
    square_mean = jnp.mean(gated_out * gated_out, -1, keepdims=True)
    return gated_out * lax.rsqrt(square_mean + EPS) * gate_gain


def contract_rows(left, right):
    return lax.dot_general(
        left, right, (((0,), (0,)), ((), ())), preferred_element_type=jnp.float32
    )


def contract_cols(left, right):
    return lax.dot_general(
        left, right, (((1,), (1,)), ((), ())), preferred_element_type=jnp.float32
    )


def on_device(
    hidden_in,
    segment_ids,
    cotangent,
    norm_gain,
    w_in,
    conv_weight,
    conv_bias,
    dt_bias,
    a_log,
    skip_gain,
    gate_gain,
    w_out,
):
    micro_count, seq_count, seq_length, width = hidden_in.shape
    row_count = seq_count * seq_length
    outputs = []
    grad_rows = []
    accum = None
    for micro in range(micro_count):
        gathered = (
            lax.all_gather(norm_gain, "fsdp", axis=0, tiled=True),
            lax.all_gather(w_in, "fsdp", axis=0, tiled=True),
            lax.all_gather(conv_weight, "fsdp", axis=1, tiled=True),
            lax.all_gather(conv_bias, "fsdp", axis=0, tiled=True),
            lax.all_gather(dt_bias, "fsdp", axis=0, tiled=True),
            lax.all_gather(a_log, "fsdp", axis=0, tiled=True),
            lax.all_gather(skip_gain, "fsdp", axis=0, tiled=True),
            lax.all_gather(gate_gain, "fsdp", axis=0, tiled=True),
            lax.all_gather(w_out, "fsdp", axis=0, tiled=True),
        )
        full_norm, full_in, full_cw, full_cb, full_dt, full_al, full_sk, full_gg, full_out = (
            gathered
        )
        small_params = tuple(
            (
                weight.astype(jnp.float32)
                for weight in (full_cw, full_cb, full_dt, full_al, full_sk, full_gg)
            )
        )
        inputs_now = hidden_in[micro].reshape(row_count, width).astype(jnp.float32)
        segments_now = segment_ids[micro]
        scaled, norm_back = jax.vjp(pre_norm, inputs_now, full_norm.astype(jnp.float32))
        scaled_low = scaled.astype(jnp.bfloat16)
        projected = jnp.dot(scaled_low, full_in, preferred_element_type=jnp.float32)

        def mix_all(projected_all, cw_now, cb_now, dt_now, al_now, sk_now, gg_now):
            per_seq = projected_all.reshape(seq_count, seq_length, projected_all.shape[1])
            mixed_seq = jax.vmap(mixer, in_axes=(0, None, None, None, None, None, None, 0))(
                per_seq, cw_now, cb_now, dt_now, al_now, sk_now, gg_now, segments_now
            )
            return mixed_seq.reshape(row_count, mixed_seq.shape[2])

        normed, mix_back = jax.vjp(mix_all, projected, *small_params)
        normed_low = normed.astype(jnp.bfloat16)
        branch_out = jnp.dot(normed_low, full_out, preferred_element_type=jnp.float32)
        outputs.append(
            (inputs_now + branch_out).astype(jnp.bfloat16).reshape(seq_count, seq_length, width)
        )
        back_in, back_out = (
            lax.all_gather(w_in, "fsdp", axis=0, tiled=True),
            lax.all_gather(w_out, "fsdp", axis=0, tiled=True),
        )
        cotan_now = cotangent[micro].reshape(row_count, width)
        grad_normed = contract_cols(cotan_now, back_out)
        grad_w_out = contract_rows(normed_low, cotan_now)
        mix_grads = mix_back(grad_normed)
        grad_projected_low = mix_grads[0].astype(jnp.bfloat16)
        grad_w_in = contract_rows(scaled_low, grad_projected_low)
        grad_scaled = contract_cols(grad_projected_low, back_in)
        grad_inputs, grad_norm = norm_back(grad_scaled)
        grad_rows.append(
            (cotan_now.astype(jnp.float32) + grad_inputs).reshape(seq_count, seq_length, width)
        )
        owned = (
            grad_norm,
            grad_w_in,
            mix_grads[1],
            mix_grads[2],
            mix_grads[3],
            mix_grads[4],
            mix_grads[5],
            mix_grads[6],
            grad_w_out,
        )
        if accum is None:
            accum = tuple((jnp.zeros(term.shape, jnp.float32) for term in owned))
        accum = tuple((carried + added for carried, added in zip(accum, owned)))
    shards = (
        lax.psum_scatter(accum[0], "fsdp", scatter_dimension=0, tiled=True),
        lax.psum_scatter(accum[1], "fsdp", scatter_dimension=0, tiled=True),
        lax.psum_scatter(accum[2], "fsdp", scatter_dimension=1, tiled=True),
        lax.psum_scatter(accum[3], "fsdp", scatter_dimension=0, tiled=True),
        lax.psum_scatter(accum[4], "fsdp", scatter_dimension=0, tiled=True),
        lax.psum_scatter(accum[5], "fsdp", scatter_dimension=0, tiled=True),
        lax.psum_scatter(accum[6], "fsdp", scatter_dimension=0, tiled=True),
        lax.psum_scatter(accum[7], "fsdp", scatter_dimension=0, tiled=True),
        lax.psum_scatter(accum[8], "fsdp", scatter_dimension=0, tiled=True),
    )
    totals = lax.psum(
        (
            shards[0],
            shards[1],
            shards[2],
            shards[3],
            shards[4],
            shards[5],
            shards[6],
            shards[7],
            shards[8],
        ),
        "replica",
    )
    block_out = jnp.stack(outputs, 0)
    grad_in = jnp.stack(grad_rows, 0)
    return (
        block_out,
        grad_in,
        totals[0],
        totals[1],
        totals[2],
        totals[3],
        totals[4],
        totals[5],
        totals[6],
        totals[7],
        totals[8],
    )


def solution(mesh):
    placed = (
        P(None, ("replica", "fsdp"), None, None),
        P(None, ("replica", "fsdp"), None),
        P(None, ("replica", "fsdp"), None, None),
        P("fsdp"),
        P("fsdp", None),
        P(None, "fsdp"),
        P("fsdp"),
        P("fsdp"),
        P("fsdp"),
        P("fsdp"),
        P("fsdp"),
        P("fsdp", None),
    )
    return jax.shard_map(
        on_device,
        mesh=mesh,
        in_specs=placed,
        out_specs=(
            P(None, ("replica", "fsdp"), None, None),
            P(None, ("replica", "fsdp"), None, None),
            P("fsdp"),
            P("fsdp", None),
            P(None, "fsdp"),
            P("fsdp"),
            P("fsdp"),
            P("fsdp"),
            P("fsdp"),
            P("fsdp"),
            P("fsdp", None),
        ),
        check_vma=False,
    )
```

profile of v0, /device:TPU:0, one launch (start us, length us, event | category | flops | bytes accessed | tf_op | source)
XLA Modules:
  0.0 1998.6 jit_solution(15459266687203980493)
XLA Ops:
  23.6 12.0 all-reduce.49
  43.1 180.6 %all-gather.5.cloned.1.call-done = bf16[2048,8512]{0,1:T(8,128)(2,1)} async-done(((bf16[512,8512]{0,1:T(8,128)(2,1)}), bf16[2048,8512]{0,1:T(8,128)(2,1)}) %all-gather.5.cloned.1.call-update) | async-done | bytes 34865168 | tf_op jit(solution)/shard_map/all_gather | solution.py:96
  223.7 17.8 convolution_bitcast_fusion.1
  249.4 16.3 convolution_bitcast_fusion
  273.7 19.3 fusion.41
  306.7 22.4 %bitcast_add_fusion.2 = f32[1,256,64,64]{1,3,2,0:T(8,128)S(1)} fusion(f32[1,256,64,64]{1,3,2,0:T(8,128)} %bitcast.415, f32[256,64,64]{0,2,1:T(8,128)} %bitcast.416, f32[256,64]{0,1:T(8,128)S(1)} %get-tuple-element.133, f32[256,64]{0,1:T(8,128)S(1)} %bitcast.445, f32[256,256]{1,0:T(8,128)S(1)} %fusion.125, pred[256,256]{1,0:T(8,128)(4,1)S(1)} %fusion.122, ...), kind=kOutput, calls=%fused_computation.95 | convolution fusion | flops 3244294144 | bytes 13041920 | tf_op jit(solution)/shard_map/jvp(vmap(tsh,shp->thp))/dot_general | solution.py:53
  336.1 19.4 bitcast_add_fusion.3
  360.7 13.2 fusion.102
  373.9 25.0 %convolution_add_fusion.1 = f32[4096,2048]{1,0:T(8,128)} fusion(f32[4096,2048]{1,0:T(8,128)} %fusion.102, bf16[2,1,256,2048]{3,2,1,0:T(8,128)(2,1)} %param.15, f32[1,256,4096]{1,2,0:T(8,128)S(1)} %get-tuple-element.95, f32[256]{0:T(256)S(1)} %fusion.139, f32[4096]{0:T(1024)S(1)} %convert_element_type.117), kind=kOutput, calls=%fused_computation.21 | convolution fusion | flops 4306501632 | bytes 72369152 | tf_op jit(solution)/shard_map/dot_general | solution.py:63
  399.1 13.8 fusion.100
  412.9 18.3 fusion.49
  432.5 21.4 %multiply_reduce_fusion.11 = (f32[4096]{0:T(1024)}, f32[1,256,4096]{1,2,0:T(8,128)S(1)}, f32[1,256,4096]{1,2,0:T(8,128)}, f32[1,256,4096]{1,2,0:T(8,128)}, f32[4096]{0:T(1024)}, /*index=5*/f32[1,256,4096]{1,2,0:T(8,128)}) fusion(f32[1,256,4352]{1,2,0:T(8,128)S(1)} %bitcast.409, f32[1,256,8512]{1,2,0:T(8,128)} %copy-done, f32[1,256,4096]{1,2,0:T(8,128)S(1)} %copy-done.5, ...), kind=kLoop, calls=%fused_computation.110 | loop fusion | flops 39837696 | bytes 58773504 | tf_op jit(solution)/shard_map/transpose(jvp(vmap()))/reduce_sum | solution.py:54
  454.0 26.8 %fusion.9 = (f32[256,64]{0,1:T(8,128)S(1)}, f32[256,64]{0,1:T(8,128)S(1)}, f32[256,64]{0,1:T(8,128)S(1)}, f32[256,256]{1,0:T(8,128)S(1)}) fusion(f32[256,64]{0,1:T(8,128)S(1)} %copy-done.52, f32[256,64]{0,1:T(8,128)S(1)} %bitcast.449, f32[256,256]{1,0:T(8,128)S(1)} %copy-done.27, pred[256,256]{1,0:T(8,128)(4,1)S(1)} %fusion.123, ...), kind=kOutput, calls=%fused_computation.25 | convolution fusion | flops 3284025344 | bytes 9306112 | tf_op jit(solution)/shard_map/transpose(jvp(vmap(tsh,shp->thp)))/dot_general | solution.py:53
  484.0 28.4 %fusion.11 = (f32[256,64]{0,1:T(8,128)S(1)}, f32[256,64]{0,1:T(8,128)S(1)}, f32[256,64]{0,1:T(8,128)S(1)}, f32[256,256]{1,0:T(8,128)S(1)}) fusion(f32[256,64]{0,1:T(8,128)S(1)} %copy-done.50, f32[256,64]{0,1:T(8,128)S(1)} %bitcast.446, f32[256,256]{1,0:T(8,128)S(1)} %copy-done.25, pred[256,256]{1,0:T(8,128)(4,1)S(1)} %fusion.122, ...), kind=kOutput, calls=%fused_computation.27 | convolution fusion | flops 3284025344 | bytes 9306112 | tf_op jit(solution)/shard_map/transpose(jvp(vmap(tsh,shp->thp)))/dot_general | solution.py:53
  523.1 17.7 bitcast_add_fusion.1
  540.8 8.3 multiply_reduce_fusion.9
  549.1 9.4 multiply_reduce_fusion.8
  558.6 16.1 bitcast_add_fusion
  574.7 8.3 multiply_reduce_fusion.5
  607.8 8.7 fusion.157
  616.5 8.7 fusion.158
  625.2 27.7 %fusion.95 = f32[2048,8512]{0,1:T(8,128)} fusion(f32[2048]{0:T(1024)S(1)} %bitcast.441, f32[256]{0:T(256)S(1)} %copy-done.82, bf16[2,1,256,2048]{3,2,1,0:T(8,128)(2,1)S(1)} %copy-done.8, f32[1,256,4096]{1,2,0:T(8,128)} %get-tuple-element.98, f32[1,256,4352]{1,2,0:T(8,128)} %get-tuple-element.109, f32[1,256,64]{1,2,0:T(8,128)S(1)} %get-tuple-element.103), kind=kOutput, calls=%fused_computation.176 | convolution fusion | flops 8934113280 | bytes 79504384 | tf_op jit(solution)/shard_map/dot_general | solution.py:63
  652.9 46.8 %convolution_add_fusion = f32[2048,8512]{0,1:T(8,128)} fusion(f32[2048,8512]{0,1:T(8,128)} %fusion.95, f32[256]{0:T(256)S(1)} %copy-done.80, f32[2048]{0:T(1024)S(1)} %bitcast.442, bf16[2,1,256,2048]{3,2,1,0:T(8,128)(2,1)S(1)} %copy-done.8, f32[1,256,4096]{1,2,0:T(8,128)} %get-tuple-element.124, f32[1,256,4352]{1,2,0:T(8,128)} %get-tuple-element.108, ...), kind=kOutput, calls=%fused_computation | convolution fusion | flops 8951545856 | bytes 149234688 | tf_op jit(solution)/shard_map/dot_general | solution.py:63
  702.9 464.1 %reduce-scatter.6.cloned.1.call-done = f32[512,8512]{0,1:T(8,128)} async-done(((f32[2048,8512]{0,1:T(8,128)}), f32[512,8512]{0,1:T(8,128)}) %reduce-scatter.6.cloned.1.call-update) | async-done | bytes 17432592 | tf_op jit(solution)/shard_map/reduce_scatter | solution.py:164
  1170.0 20.5 %fusion.148 = f32[256,2048]{1,0:T(8,128)} fusion(bf16[2048,8512]{0,1:T(8,128)(2,1)} %all-gather.5.cloned.1.call-done, f32[1,256,4096]{1,2,0:T(8,128)} %get-tuple-element.124, f32[1,256,4352]{1,2,0:T(8,128)} %get-tuple-element.108, f32[1,256,64]{1,2,0:T(8,128)S(1)} %get-tuple-element.101), kind=kOutput, calls=%fused_computation.291 | convolution fusion | flops 8932016128 | bytes 45678592 | tf_op jit(solution)/shard_map/dot_general | solution.py:69
  1190.6 20.3 %fusion.75 = (f32[2048]{0:T(1024)S(1)}, f32[256]{0:T(256)S(1)}, f32[256]{0:T(256)S(1)}, f32[2048]{0:T(1024)S(1)}, f32[256,2048]{1,0:T(8,128)}) fusion(f32[256]{0:T(256)S(1)} %copy-done.82, bf16[2,1,256,2048]{3,2,1,0:T(8,128)(2,1)S(1)} %copy-done.8, f32[2048]{0:T(1024)S(1)} %bitcast.443, f32[256,2048]{1,0:T(8,128)} %fusion.148, f32[256]{0:T(256)S(1)} %copy-done.80, ...), kind=kOutput, calls=%fused_computation.152 | convolution fusion | flops 8939352064 | bytes 49901568 | tf_op jit(solution)/shard_map/dot_general | solution.py:69
  1211.1 11.6 all-reduce.48
  1223.1 11.9 fusion.70
  1235.0 10.8 fusion.71
  1253.7 40.2 %all-reduce.46 = (f32[512]{0:T(512)}, f32[4,1088]{1,0:T(4,128)}, f32[1088]{0:T(1024)}, f32[16]{0:T(128)}, f32[16]{0:T(128)}, /*index=5*/f32[16]{0:T(128)}, f32[1024]{0:T(1024)}) all-reduce(f32[512]{0:T(512)S(1)} %dynamic-slice.5, f32[4,1088]{1,0:T(4,128)S(1)} %copy.89, ...), channel_id=1, replica_groups=mesh['replica'=8,'fsdp'=4] {'replica'}, use_global_device_ids=true, to_apply=%region_27.29 | all-reduce | flops 7024 | bytes 56192 | tf_op jit(solution)/shard_map/psum | solution.py:173
  1293.9 679.8 %all-reduce.52.cloned.1.call-done = (f32[512,8512]{0,1:T(8,128)}, f32[1024,2048]{1,0:T(8,128)}) async-done(((f32[512,8512]{0,1:T(8,128)}, f32[1024,2048]{1,0:T(8,128)}), (f32[512,8512]{0,1:T(8,128)}, f32[1024,2048]{1,0:T(8,128)})) %all-reduce.52.cloned.1.call-update) | async-done | bytes 25821200 | tf_op jit(solution)/shard_map/psum | solution.py:173
  1973.7 13.0 copy.122
  (403 shorter events, 119.9 us)
Async XLA Ops:
  7.2 216.5 %all-gather.5.cloned.1.call-start = ((), (), s32[]{:S(2)}) async-start(), calls=%async_computation.3 | async-start | bytes 43581440 | tf_op jit(solution)/shard_map/all_gather | solution.py:96
  8.0 391.0 %all-gather.7.cloned.1.call-start = ((), (), s32[]{:S(2)}) async-start(), calls=%async_computation.4 | async-start | bytes 20971520 | tf_op jit(solution)/shard_map/all_gather | solution.py:103
  8.8 694.1 %reduce-scatter.8.cloned.1.call-start = ((), (), s32[]{:S(2)}) async-start(), calls=%async_computation.6 | async-start | bytes 41943040 | tf_op jit(solution)/shard_map/reduce_scatter | solution.py:171
  15.0 234.4 %copy-start.35 = (f32[4,1,512]{2,1,0:T(1,128)}, f32[4,1,512]{2,1,0:T(1,128)S(1)}, u32[]{:S(2)}) copy-start(f32[4,1,512]{2,1,0:T(1,128)S(1)} %convert_element_type.142) | copy-start | bytes 24580
  35.7 205.8 %copy-start.96 = (bf16[64]{0:T(256)(128)(2,1)}, bf16[64]{0:T(256)(128)(2,1)S(1)}, u32[]{:S(2)}) copy-start(bf16[64]{0:T(256)(128)(2,1)S(1)} %get-tuple-element.66) | copy-start | bytes 388
  35.7 261.8 %copy-start.84 = (f32[64]{0:T(128)}, f32[64]{0:T(128)S(1)}, u32[]{:S(2)}) copy-start(f32[64]{0:T(128)S(1)} %convert_element_type.115) | copy-start | bytes 772
  35.7 300.3 %copy-start.101 = (f32[64]{0:T(128)}, f32[64]{0:T(128)S(1)}, u32[]{:S(2)}) copy-start(f32[64]{0:T(128)S(1)} %convert_element_type.116) | copy-start | bytes 772
  41.1 391.4 %copy-start.20 = (f32[4096]{0:T(1024)}, f32[4096]{0:T(1024)S(1)}, u32[]{:S(2)}) copy-start(f32[4096]{0:T(1024)S(1)} %convert_element_type.117) | copy-start | bytes 49156
  41.2 232.4 %copy-start.70 = (f32[1,256]{1,0:T(1,128)}, f32[1,256]{1,0:T(1,128)S(1)}, u32[]{:S(2)}) copy-start(f32[1,256]{1,0:T(1,128)S(1)} %pad_convert_fusion.2) | copy-start | bytes 3076
  41.4 232.3 %copy-start.68 = (f32[1,256]{1,0:T(1,128)}, f32[1,256]{1,0:T(1,128)S(1)}, u32[]{:S(2)}) copy-start(f32[1,256]{1,0:T(1,128)S(1)} %pad_convert_fusion.3) | copy-start | bytes 3076
  41.6 232.1 %copy-start.66 = (f32[1,256]{1,0:T(1,128)}, f32[1,256]{1,0:T(1,128)S(1)}, u32[]{:S(2)}) copy-start(f32[1,256]{1,0:T(1,128)S(1)} %pad_convert_fusion) | copy-start | bytes 3076
  41.7 231.9 %copy-start.62 = (f32[1,256]{1,0:T(1,128)}, f32[1,256]{1,0:T(1,128)S(1)}, u32[]{:S(2)}) copy-start(f32[1,256]{1,0:T(1,128)S(1)} %pad_convert_fusion.1) | copy-start | bytes 3076
  41.9 231.8 %copy-start.72 = (f32[1,256]{1,0:T(1,128)}, f32[1,256]{1,0:T(1,128)S(1)}, u32[]{:S(2)}) copy-start(f32[1,256]{1,0:T(1,128)S(1)} %fusion.134) | copy-start | bytes 3076
  42.0 231.6 %copy-start.64 = (f32[1,256]{1,0:T(1,128)}, f32[1,256]{1,0:T(1,128)S(1)}, u32[]{:S(2)}) copy-start(f32[1,256]{1,0:T(1,128)S(1)} %fusion.135) | copy-start | bytes 3076
  42.2 231.5 %copy-start.22 = (f32[4352]{0:T(1024)}, f32[4352]{0:T(1024)S(1)}, u32[]{:S(2)}) copy-start(f32[4352]{0:T(1024)S(1)} %get-tuple-element.43) | copy-start | bytes 52228
  42.2 231.5 %copy-start.29 = (f32[4352]{0:T(1024)}, f32[4352]{0:T(1024)S(1)}, u32[]{:S(2)}) copy-start(f32[4352]{0:T(1024)S(1)} %get-tuple-element.44) | copy-start | bytes 52228
  42.2 231.5 %copy-start.31 = (f32[4352]{0:T(1024)}, f32[4352]{0:T(1024)S(1)}, u32[]{:S(2)}) copy-start(f32[4352]{0:T(1024)S(1)} %get-tuple-element.45) | copy-start | bytes 52228
  42.3 231.5 %copy-start.33 = (f32[4352]{0:T(1024)}, f32[4352]{0:T(1024)S(1)}, u32[]{:S(2)}) copy-start(f32[4352]{0:T(1024)S(1)} %get-tuple-element.46) | copy-start | bytes 52228
  42.3 255.2 %copy-start.86 = (f32[64]{0:T(128)}, f32[64]{0:T(128)S(1)}, u32[]{:S(2)}) copy-start(f32[64]{0:T(128)S(1)} %fusion.140) | copy-start | bytes 772
  42.8 198.7 %copy-start.74 = (f32[256]{0:T(256)}, f32[256]{0:T(256)S(1)}, u32[]{:S(2)}) copy-start(f32[256]{0:T(256)S(1)} %get-tuple-element.41) | copy-start | bytes 3076
  42.8 198.7 %copy-start.76 = (f32[256]{0:T(256)}, f32[256]{0:T(256)S(1)}, u32[]{:S(2)}) copy-start(f32[256]{0:T(256)S(1)} %get-tuple-element.42) | copy-start | bytes 3076
  42.8 206.6 %copy-start.79 = (f32[256]{0:T(256)}, f32[256]{0:T(256)S(1)}, u32[]{:S(2)}) copy-start(f32[256]{0:T(256)S(1)} %fusion.138) | copy-start | bytes 3076
  42.8 198.7 %copy-start.81 = (f32[256]{0:T(256)}, f32[256]{0:T(256)S(1)}, u32[]{:S(2)}) copy-start(f32[256]{0:T(256)S(1)} %fusion.136) | copy-start | bytes 3076
  43.0 441.0 %copy-start.40 = (pred[256,256]{1,0:T(8,128)(4,1)}, pred[256,256]{1,0:T(8,128)(4,1)S(1)}, u32[]{:S(2)}) copy-start(pred[256,256]{1,0:T(8,128)(4,1)S(1)} %fusion.122) | copy-start | bytes 196612
  43.1 410.9 %copy-start.42 = (pred[256,256]{1,0:T(8,128)(4,1)}, pred[256,256]{1,0:T(8,128)(4,1)S(1)}, u32[]{:S(2)}) copy-start(pred[256,256]{1,0:T(8,128)(4,1)S(1)} %fusion.123) | copy-start | bytes 196612
  241.5 56.0 %copy-start = (f32[1,256,8512]{1,2,0:T(8,128)}, f32[1,256,8512]{1,2,0:T(8,128)S(1)}, u32[]{:S(2)}) copy-start(f32[1,256,8512]{1,2,0:T(8,128)S(1)} %convolution_bitcast_fusion.1) | copy-start | bytes 26148868
  298.9 185.0 %copy-start.44 = (f32[1,256,64]{1,2,0:T(8,128)}, f32[1,256,64]{1,2,0:T(8,128)S(1)}, u32[]{:S(2)}) copy-start(f32[1,256,64]{1,2,0:T(8,128)S(1)} %copy.114) | copy-start | bytes 196612
  334.3 98.2 %copy-start.56 = (f32[256]{0:T(256)}, f32[256]{0:T(256)S(1)}, u32[]{:S(2)}) copy-start(f32[256]{0:T(256)S(1)} %fusion.139) | copy-start | bytes 3076
  360.7 71.8 %copy-start.58 = (f32[256]{0:T(256)}, f32[256]{0:T(256)S(1)}, u32[]{:S(2)}) copy-start(f32[256]{0:T(256)S(1)} %fusion.137) | copy-start | bytes 3076
  398.9 768.1 %reduce-scatter.6.cloned.1.call-start = ((), (), s32[]{:S(2)}) async-start(), calls=%async_computation.5 | async-start | bytes 87162880 | tf_op jit(solution)/shard_map/reduce_scatter | solution.py:164
  699.8 552.6 %reduce-scatter.10.cloned.1.call-start = ((), (), s32[]{:S(2)}) async-start(), calls=%async_computation.7 | async-start | bytes 2785280
  702.8 1270.9 %all-reduce.52.cloned.1.call-start = ((), (), s32[]{:S(2)}) async-start(), calls=%async_computation.8 | async-start | bytes 51642368 | tf_op jit(solution)/shard_map/psum | solution.py:173
  (95 other events, 1707.1 us)
Sparse Core Ops, SparseCore 0:
  9.6 214.0 all-gather.4
  225.3 105.9 all-gather.6
  399.1 235.2 reduce-scatter.7
  699.9 467.0 reduce-scatter.5
  1170.2 32.2 reduce-scatter.9
  1206.7 766.8 all-reduce.51
where the time goes:
time: 2000 us
  waiting for transfers between devices  1330 us (66%)
  matrix products  382 us (19%)
  other arithmetic  136 us (7%)
  blocking collectives  80.8 us (4%)
  local copies, waits for them, and re-layouts  53.5 us (3%)
  between operations  20.3 us (1%)
    psum x1, waiting for transfers between devices, on_device(): lax.psum((shards[0], shards[1], shards[2], shards[3], shards[4], shards[5...  680 us
    reduce_scatter x1, waiting for transfers between devices, on_device(): lax.psum_scatter(accum[1], 'fsdp', scatter_dimension=0, tiled=True)  464 us
    all_gather x1, waiting for transfers between devices, on_device(): lax.all_gather(w_in, 'fsdp', axis=0, tiled=True)  181 us
    dot_general x6, matrix products, mixer(): jnp.einsum('tsh,shp->thp', weights_ts, values_in, precision=HIGHEST)  131 us
    dot_general x4, matrix products, contract_rows(): lax.dot_general(left, right, (((0,), (0,)), ((), ())), preferred_element_...  113 us
    dot_general x4, matrix products, contract_cols(): lax.dot_general(left, right, (((1,), (1,)), ((), ())), preferred_element_...  72.8 us
    psum x1, blocking collectives, on_device(): lax.psum((shards[0], shards[1], shards[2], shards[3], shards[4], shards[5...  40.2 us
  transfers between devices with their start and end apart: 6, of which 3 were waited for; matrix products, arithmetic and copies ran while one was open for 28% of the time, Pallas kernels for 0%

commit v1 on v0

v1 whole, which is shorter than its diff:
```python
import functools

import jax
import jax.numpy as jnp
from jax import lax
from jax.experimental import pallas as pl
from jax.experimental.pallas import tpu as pltpu
from jax.sharding import PartitionSpec as P

EPS = 1e-05
HIGHEST = lax.Precision.HIGHEST
LANES = 128
F32 = jnp.float32
BF16 = jnp.bfloat16
LOG2E = 1.4426950408889634


def contract_rows(left, right, precision=None):
    return lax.dot_general(
        left, right, (((0,), (0,)), ((), ())), precision=precision, preferred_element_type=F32
    )


def contract_cols(left, right, precision=None):
    return lax.dot_general(
        left, right, (((1,), (1,)), ((), ())), precision=precision, preferred_element_type=F32
    )


def sigmoid(v):
    return 1.0 / (1.0 + jnp.exp(-v))


def convolve(conv_input, taps, bias, mask_refs):
    total = bias + taps[0] * conv_input
    shifted = []
    for offset in range(1, len(taps)):
        prior = pltpu.roll(conv_input, offset, 0) * mask_refs[offset - 1]
        shifted.append(prior)
        total = total + taps[offset] * prior
    return total, shifted


def prepare(dims, own_ref, proj_ref, seg_col_ref, seg_row_ref, mask_ref, head_ref, cw_ref,
            mask_wide, visible_bias, step_wide, cum_wide, cum_rows, state_act, affinity):
    tokens, inner, state2, heads, local_heads, taps = dims
    for offset in range(taps - 1):
        mask_wide[offset] = jnp.broadcast_to(mask_ref[:, offset : offset + 1], (tokens, LANES))
    rows = lax.broadcasted_iota(jnp.int32, (tokens, tokens), 0)
    cols = lax.broadcasted_iota(jnp.int32, (tokens, tokens), 1)
    visible = (rows >= cols) & (seg_col_ref[...] == seg_row_ref[...])
    visible_bias[...] = jnp.where(visible, 0.0, -1e30)
    common = 2 * inner
    raw = proj_ref[:, common + state2 : common + state2 + heads]
    raw = jnp.concatenate([raw, jnp.zeros((tokens, LANES - heads), F32)], 1)
    raw = pltpu.roll(raw, LANES - own_ref[0] * local_heads, 1)
    raw = raw + head_ref[0:1, :]
    step = jnp.maximum(raw, 0.0) + jnp.log1p(jnp.exp(-jnp.abs(raw)))
    log_decay = head_ref[1:2, :] * step
    lower = jnp.where(rows >= cols, 1.0, 0.0).astype(F32)
    cumulative = jnp.dot(lower, log_decay, precision=HIGHEST, preferred_element_type=F32)
    scaled_cum = cumulative * LOG2E
    flipped = scaled_cum.T
    lane = lax.broadcasted_iota(jnp.int32, (tokens, LANES), 1)
    for head in range(local_heads):
        cum_wide[head] = jnp.broadcast_to(scaled_cum[:, head : head + 1], (tokens, LANES))
        cum_rows[head] = flipped[head : head + 1, :]
    for pair in range(local_heads // 2):
        step_wide[pair] = jnp.where(
            lane < LANES // 2, step[:, 2 * pair : 2 * pair + 1], step[:, 2 * pair + 1 : 2 * pair + 2]
        )
    for part in range(state2 // LANES):
        at = inner + part * LANES
        conv, _ = convolve(
            proj_ref[:, common + part * LANES : common + (part + 1) * LANES],
            [cw_ref[j : j + 1, at : at + LANES] for j in range(taps)],
            cw_ref[taps : taps + 1, at : at + LANES],
            mask_wide,
        )
        state_act[part] = conv * sigmoid(conv)
    affinity[...] = contract_cols(state_act[1], state_act[0], HIGHEST)
    return raw, step, log_decay, rows, cols


def forward_kernel(dims, own_ref, proj_ref, seg_col_ref, seg_row_ref, mask_ref, head_ref, cw_ref, chan_ref,
                   gated_ref, square_ref,
                   mask_wide, visible_bias, step_wide, cum_wide, cum_rows, state_act, affinity):
    tokens, inner, state2, heads, local_heads, taps = dims
    prepare(dims, own_ref, proj_ref, seg_col_ref, seg_row_ref, mask_ref, head_ref, cw_ref,
            mask_wide, visible_bias, step_wide, cum_wide, cum_rows, state_act, affinity)
    lane = lax.broadcasted_iota(jnp.int32, (tokens, LANES), 1)
    first = lane < LANES // 2
    blocks = tokens // LANES

    def pair_step(pair, squares):
        here = pl.ds(pl.multiple_of(pair * LANES, LANES), LANES)
        conv, _ = convolve(
            proj_ref[:, here], [cw_ref[j : j + 1, here] for j in range(taps)],
            cw_ref[taps : taps + 1, here], mask_wide,
        )
        values = conv * sigmoid(conv)
        weighted = values * step_wide[pair]
        out = chan_ref[0:1, here] * values
        parts = [out[b * LANES : (b + 1) * LANES] for b in range(blocks)]
        for which in range(2):
            head = 2 * pair + which
            mine = jnp.where(first == (which == 0), weighted, 0.0).astype(BF16)
            for tb in range(blocks):
                t_rows = slice(tb * LANES, (tb + 1) * LANES)
                pieces = []
                for sb in range(tb + 1):
                    s_cols = slice(sb * LANES, (sb + 1) * LANES)
                    distance = (cum_wide[head, t_rows, :] - cum_rows[head, :, s_cols]) + visible_bias[t_rows, s_cols]
                    pieces.append((affinity[t_rows, s_cols] * jnp.exp2(distance)).astype(BF16))
                weights = jnp.concatenate(pieces, 1) if tb > 0 else pieces[0]
                parts[tb] = parts[tb] + jnp.dot(
                    weights, mine[: (tb + 1) * LANES], preferred_element_type=F32
                )
        out = jnp.concatenate(parts, 0)
        gate = proj_ref[:, pl.ds(pl.multiple_of(inner + pair * LANES, LANES), LANES)]
        gated = out * (gate * sigmoid(gate))
        gated_ref[:, here] = (gated * chan_ref[1:2, here]).astype(BF16)
        return squares + gated * gated

    squares = lax.fori_loop(0, local_heads // 2, pair_step, jnp.zeros((tokens, LANES), F32))
    square_ref[...] = jnp.sum(squares, 1, keepdims=True)


def backward_kernel(dims, own_ref, proj_ref, seg_col_ref, seg_row_ref, mask_ref, head_ref, cw_ref, chan_ref,
                    stats_ref, gn_ref,
                    gp_ref, grad_cw_ref, grad_chan_ref, grad_head_ref,
                    mask_wide, visible_bias, step_wide, cum_wide, cum_rows, state_act, affinity,
                    grad_affinity, row_sums, col_sums, wide_stats):
    tokens, inner, state2, heads, local_heads, taps = dims

    @pl.when(pl.program_id(0) == 0)
    def _():
        grad_cw_ref[...] = jnp.zeros_like(grad_cw_ref)
        grad_chan_ref[...] = jnp.zeros_like(grad_chan_ref)
        grad_head_ref[...] = jnp.zeros_like(grad_head_ref)

    raw, step, log_decay, rows, cols = prepare(
        dims, own_ref, proj_ref, seg_col_ref, seg_row_ref, mask_ref, head_ref, cw_ref,
        mask_wide, visible_bias, step_wide, cum_wide, cum_rows, state_act, affinity)
    grad_affinity[...] = jnp.zeros_like(grad_affinity)
    row_sums[...] = jnp.zeros_like(row_sums)
    col_sums[...] = jnp.zeros_like(col_sums)
    wide_stats[0] = jnp.broadcast_to(stats_ref[:, 0:1], (tokens, LANES))
    wide_stats[1] = jnp.broadcast_to(stats_ref[:, 1:2], (tokens, LANES))
    lane = lax.broadcasted_iota(jnp.int32, (tokens, LANES), 1)
    block_lane = lax.broadcasted_iota(jnp.int32, (LANES, LANES), 1)
    first = lane < LANES // 2
    blocks = tokens // LANES

    def conv_back(grad_conv, shifted, conv_input, here):
        grad_cw_ref[0:1, here] += jnp.sum(grad_conv * conv_input, 0, keepdims=True)
        grad_cw_ref[taps : taps + 1, here] += jnp.sum(grad_conv, 0, keepdims=True)
        back = cw_ref[0:1, here] * grad_conv
        for offset in range(1, taps):
            grad_cw_ref[offset : offset + 1, here] += jnp.sum(grad_conv * shifted[offset - 1], 0, keepdims=True)
            term = (cw_ref[offset : offset + 1, here] * grad_conv) * mask_wide[offset - 1]
            back = back + pltpu.roll(term, tokens - offset, 0)
        return back

    def pair_step(pair, carry):
        here = pl.ds(pl.multiple_of(pair * LANES, LANES), LANES)
        there = pl.ds(pl.multiple_of(inner + pair * LANES, LANES), LANES)
        conv_input = proj_ref[:, here]
        conv, shifted = convolve(
            conv_input, [cw_ref[j : j + 1, here] for j in range(taps)],
            cw_ref[taps : taps + 1, here], mask_wide,
        )
        conv_sig = sigmoid(conv)
        values = conv * conv_sig
        weighted = values * step_wide[pair]
        skip = chan_ref[0:1, here]
        halves = [jnp.where(first == (which == 0), weighted, 0.0).astype(BF16) for which in range(2)]
        out_parts = [(skip * values)[b * LANES : (b + 1) * LANES] for b in range(blocks)]
        for which in range(2):
            head = 2 * pair + which
            for tb in range(blocks):
                t_rows = slice(tb * LANES, (tb + 1) * LANES)
                pieces = []
                for sb in range(tb + 1):
                    s_cols = slice(sb * LANES, (sb + 1) * LANES)
                    distance = (cum_wide[head, t_rows, :] - cum_rows[head, :, s_cols]) + visible_bias[t_rows, s_cols]
                    pieces.append((affinity[t_rows, s_cols] * jnp.exp2(distance)).astype(BF16))
                weights = jnp.concatenate(pieces, 1) if tb > 0 else pieces[0]
                out_parts[tb] = out_parts[tb] + jnp.dot(
                    weights, halves[which][: (tb + 1) * LANES], preferred_element_type=F32
                )
        out = jnp.concatenate(out_parts, 0)
        gate = proj_ref[:, there]
        gate_sig = sigmoid(gate)
        gate_silu = gate * gate_sig
        gated = out * gate_silu
        gn = gn_ref[:, here]
        gain = chan_ref[1:2, here]
        root = wide_stats[0]
        grad_chan_ref[1:2, here] += jnp.sum(gn * gated * root, 0, keepdims=True)
        grad_gated = root * (gn * gain) - gated * wide_stats[1]
        grad_out = grad_gated * gate_silu
        gp_ref[:, there] = (grad_gated * out * (gate_sig * (1.0 + gate * (1.0 - gate_sig)))).astype(BF16)
        grad_chan_ref[0:1, here] += jnp.sum(grad_out * values, 0, keepdims=True)
        back_parts = [jnp.zeros((LANES, LANES), F32) for _ in range(blocks)]
        for which in range(2):
            head = 2 * pair + which
            mine = jnp.where(first == (which == 0), grad_out, 0.0).astype(BF16)
            for tb in range(blocks):
                t_rows = slice(tb * LANES, (tb + 1) * LANES)
                sums = None
                for sb in range(tb + 1):
                    s_cols = slice(sb * LANES, (sb + 1) * LANES)
                    distance = (cum_wide[head, t_rows, :] - cum_rows[head, :, s_cols]) + visible_bias[t_rows, s_cols]
                    decay = jnp.exp2(distance)
                    weights = affinity[t_rows, s_cols] * decay
                    cross = contract_cols(mine[t_rows], halves[which][s_cols])
                    grad_affinity[t_rows, s_cols] += cross * decay
                    energy = cross * weights
                    col_sums[head, :, s_cols] += jnp.sum(energy, 0, keepdims=True)
                    sums = energy if sums is None else sums + energy
                    back_parts[sb] = back_parts[sb] + contract_rows(weights.astype(BF16), mine[t_rows])
                row_sums[t_rows, :] += jnp.where(
                    block_lane == head, jnp.sum(sums, 1, keepdims=True), 0.0
                )
        grad_values = jnp.concatenate(back_parts, 0) * step_wide[pair] + skip * grad_out
        grad_conv = grad_values * (conv_sig * (1.0 + conv * (1.0 - conv_sig)))
        gp_ref[:, here] = conv_back(grad_conv, shifted, conv_input, here).astype(BF16)
        return carry

    lax.fori_loop(0, local_heads // 2, pair_step, 0)

    common = 2 * inner
    grad_states = [
        contract_rows(grad_affinity[...], state_act[1], HIGHEST),
        jnp.dot(grad_affinity[...], state_act[0], precision=HIGHEST, preferred_element_type=F32),
    ]
    for part in range(state2 // LANES):
        at = slice(inner + part * LANES, inner + (part + 1) * LANES)
        spot = slice(common + part * LANES, common + (part + 1) * LANES)
        conv_input = proj_ref[:, spot]
        conv, shifted = convolve(
            conv_input, [cw_ref[j : j + 1, at] for j in range(taps)], cw_ref[taps : taps + 1, at], mask_wide
        )
        conv_sig = sigmoid(conv)
        grad_conv = grad_states[part] * (conv_sig * (1.0 + conv * (1.0 - conv_sig)))
        gp_ref[:, spot] = conv_back(grad_conv, shifted, conv_input, at).astype(BF16)

    col_rows = [col_sums[head] for head in range(local_heads)]
    col_rows.append(jnp.zeros((LANES - local_heads, tokens), F32))
    col_energy = jnp.concatenate(col_rows, 0).T
    upper = jnp.where(cols >= rows, 1.0, 0.0).astype(F32)
    grad_decay = jnp.dot(upper, row_sums[...] - col_energy, precision=HIGHEST, preferred_element_type=F32)
    step_sig = sigmoid(raw)
    ratio = jnp.where(raw < -20.0, 1.0, step_sig / jnp.maximum(step, 1e-30))
    grad_raw = col_energy * ratio + (head_ref[1:2, :] * grad_decay) * step_sig
    grad_head_ref[0:1, :] += jnp.sum(grad_raw, 0, keepdims=True)
    grad_head_ref[1:2, :] += jnp.sum(grad_decay * log_decay, 0, keepdims=True)
    placed = pltpu.roll(grad_raw, own_ref[0] * local_heads, 1)
    gp_ref[:, common + state2 : common + state2 + heads] = placed[:, :heads].astype(BF16)


def mixer_specs(dims, width):
    tokens, inner, state2, heads, local_heads, taps = dims
    fixed = lambda shape: pl.BlockSpec(shape, lambda s: (0,) * len(shape))
    in_specs = [
        pl.BlockSpec(memory_space=pltpu.SMEM),
        pl.BlockSpec((tokens, width), lambda s: (s, 0)),
        pl.BlockSpec((None, tokens, 1), lambda s: (s, 0, 0)),
        pl.BlockSpec((None, 1, tokens), lambda s: (s, 0, 0)),
        pl.BlockSpec((None, tokens, 8), lambda s: (s, 0, 0)),
        fixed((8, LANES)),
        fixed((8, inner + state2)),
        fixed((8, inner)),
    ]
    scratch = [
        pltpu.VMEM((taps - 1, tokens, LANES), F32),
        pltpu.VMEM((tokens, tokens), F32),
        pltpu.VMEM((local_heads // 2, tokens, LANES), F32),
        pltpu.VMEM((local_heads, tokens, LANES), F32),
        pltpu.VMEM((local_heads, 1, tokens), F32),
        pltpu.VMEM((state2 // LANES, tokens, LANES), F32),
        pltpu.VMEM((tokens, tokens), F32),
    ]
    return in_specs, scratch


def mix_forward(dims, operands):
    tokens, inner, state2, heads, local_heads, taps = dims
    total, width = operands[1].shape
    in_specs, scratch = mixer_specs(dims, width)
    return pl.pallas_call(
        functools.partial(forward_kernel, dims),
        grid=(total // tokens,),
        in_specs=in_specs,
        out_specs=[
            pl.BlockSpec((tokens, inner), lambda s: (s, 0)),
            pl.BlockSpec((tokens, 1), lambda s: (s, 0)),
        ],
        out_shape=[
            jax.ShapeDtypeStruct((total, inner), BF16),
            jax.ShapeDtypeStruct((total, 1), F32),
        ],
        scratch_shapes=scratch,
        compiler_params=pltpu.CompilerParams(vmem_limit_bytes=48 << 20),
        cost_estimate=pl.CostEstimate(
            flops=total * local_heads * tokens * 4 * 64,
            bytes_accessed=total * width * 4,
            transcendentals=total * local_heads * tokens,
        ),
        name="mix_forward",
    )(*operands)


def mix_backward(dims, operands, stats, grad_normed):
    tokens, inner, state2, heads, local_heads, taps = dims
    total, width = operands[1].shape
    in_specs, scratch = mixer_specs(dims, width)
    fixed = lambda shape: pl.BlockSpec(shape, lambda s: (0,) * len(shape))
    return pl.pallas_call(
        functools.partial(backward_kernel, dims),
        grid=(total // tokens,),
        in_specs=in_specs + [
            pl.BlockSpec((tokens, 2), lambda s: (s, 0)),
            pl.BlockSpec((tokens, inner), lambda s: (s, 0)),
        ],
        out_specs=[
            pl.BlockSpec((tokens, width), lambda s: (s, 0)),
            fixed((8, inner + state2)),
            fixed((8, inner)),
            fixed((8, LANES)),
        ],
        out_shape=[
            jax.ShapeDtypeStruct((total, width), BF16),
            jax.ShapeDtypeStruct((8, inner + state2), F32),
            jax.ShapeDtypeStruct((8, inner), F32),
            jax.ShapeDtypeStruct((8, LANES), F32),
        ],
        scratch_shapes=scratch + [
            pltpu.VMEM((tokens, tokens), F32),
            pltpu.VMEM((tokens, LANES), F32),
            pltpu.VMEM((local_heads, 1, tokens), F32),
            pltpu.VMEM((2, tokens, LANES), F32),
        ],
        compiler_params=pltpu.CompilerParams(vmem_limit_bytes=48 << 20),
        cost_estimate=pl.CostEstimate(
            flops=total * local_heads * tokens * 12 * 64,
            bytes_accessed=total * width * 6,
            transcendentals=2 * total * local_heads * tokens,
        ),
        name="mix_backward",
    )(*operands, stats, grad_normed)


def swap(array, axis, size, bit):
    return lax.ppermute(array, axis, [(i, i ^ bit) for i in range(size)])


def axis_bits(size):
    bits = []
    bit = 1
    while bit < size:
        bits.append(bit)
        bit *= 2
    return bits


def gather_relative(array, axis, size):
    held = array[None]
    for bit in reversed(axis_bits(size)):
        held = jnp.concatenate([held, swap(held, axis, size, bit)], 0)
    return held


def scatter_relative(array, axis, size):
    total = array
    for bit in axis_bits(size):
        half = total.shape[0] // 2
        received = swap(total[half:].astype(BF16), axis, size, bit)
        total = total[:half].astype(F32) + received.astype(F32)
    return total[0]


def sum_tokens(array, axis, size):
    kinds, tokens = array.shape
    for bit in axis_bits(size):
        stride = tokens // (2 * bit)
        received = swap(array, axis, size, bit).reshape(kinds, bit, 2, stride)
        array = array + received[:, :, ::-1].reshape(kinds, tokens)
    return array


def halve_sum(array, order, replica, size):
    total = array
    for bit in order:
        blocks, rows, columns = total.shape
        mine = (replica // bit) % 2
        halves = total.reshape(blocks, 2, rows // 2, columns)
        kept = lax.dynamic_index_in_dim(halves, mine, 1, keepdims=False)
        sent = lax.dynamic_index_in_dim(halves, 1 - mine, 1, keepdims=False)
        received = swap(sent.astype(BF16), "replica", size, bit)
        total = kept + received.astype(F32)
    return total


def double_gather(array, order, replica, size):
    held = array
    for bit in reversed(order):
        received = swap(held, "replica", size, bit)
        upper = (replica // bit) % 2 == 1
        held = jnp.where(
            upper,
            jnp.concatenate([received, held], 1),
            jnp.concatenate([held, received], 1),
        )
    return held


def flip(index, bit):
    return index + bit * (1 - 2 * ((index // bit) % 2))


def reduce_chunks(size, copies, depth, inner, common, out_rows, width):
    bits = axis_bits(copies)
    first, second = bits, bits[1:] + bits[:1]
    chunks = []
    for index in range(out_rows // OUT_CHUNK):
        chunks.append(("out", index, second if index % 2 else first))
    for index in range(2 * inner // COL_CHUNK):
        chunks.append(("in", index, second if index % 2 else first))
    chunks.append(("shared", 0, first))
    return chunks


COL_CHUNK = 256
OUT_CHUNK = 256
STAGES = ("keep", "got0", "sent1", "got1", "sent2", "got2", "final")


def reduce_kernel(plan, in_ref, out_ref, sum_in_ref, sum_shared_ref, sum_out_ref, *scratch):
    size, copies, chunks, shapes = plan
    groups = {}
    position = 0
    for name in shapes:
        groups[name] = dict(zip(STAGES, scratch[position : position + len(STAGES)]))
        position += len(STAGES)
    shared_in, shared_sum = scratch[position], scratch[position + 1]
    send_sems, recv_sems, local_sems = scratch[position + 2 :]
    me = lax.axis_index("fsdp")
    replica = lax.axis_index("replica")
    levels = len(axis_bits(copies))
    MESH = pl.DeviceIdType.MESH

    def replica_peer(bit):
        return (flip(replica, bit), me)

    def copy_peer(offset):
        other = me
        for bit in axis_bits(size):
            if offset & bit:
                other = flip(other, bit)
        return other

    barrier = pltpu.get_barrier_semaphore()
    peers = [replica_peer(bit) for bit in axis_bits(copies)]
    peers += [(replica, copy_peer(offset)) for offset in range(1, size)]
    for peer in peers:
        pl.semaphore_signal(barrier, inc=1, device_id=peer, device_id_type=MESH)
    pl.semaphore_wait(barrier, len(peers))

    def run(number, group, index, order):
        blocks, rows, columns = shapes[group]
        if group == "in":
            source, target = in_ref, sum_in_ref
            cut = lambda ref, at, count: ref.at[:, pl.ds(at, count), pl.ds(index * columns, columns)]
        elif group == "shared":
            source, target = in_ref, sum_shared_ref
            cut = lambda ref, at, count: ref.at[:, pl.ds(at, count), pl.ds(in_ref.shape[2] - columns, columns)]
        else:
            source, target = out_ref, sum_out_ref
            cut = lambda ref, at, count: ref.at[pl.ds(index, 1), pl.ds(at, count)]
        if group == "shared":
            place = lambda at, count: target.at[pl.ds(at, count)]
        else:
            place = lambda at, count: cut(target, at, count)
        held = {name: groups[group][name].at[index] for name in STAGES}
        sizes = [rows >> (level + 1) for level in range(levels)]
        upper = [(replica // bit) % 2 for bit in order]
        starts = [0]
        for level in range(levels):
            starts.append(pl.multiple_of(starts[-1] + upper[level] * sizes[level], sizes[-1]))
        sem = 0
        pending = []

        def send(from_ref, to_ref, device, slot):
            copy = pltpu.make_async_remote_copy(
                src_ref=from_ref, dst_ref=to_ref, send_sem=send_sems.at[number, slot],
                recv_sem=recv_sems.at[number, slot], device_id=device, device_id_type=MESH,
            )
            copy.start()
            pending.append(copy)
            return copy

        other = pl.multiple_of((1 - upper[0]) * sizes[0], sizes[0])
        keep_copy = pltpu.make_async_copy(cut(source, starts[1], sizes[0]), held["keep"], local_sems.at[number, 0])
        keep_copy.start()
        copy = send(cut(source, other, sizes[0]), held["got0"], replica_peer(order[0]), 0)
        yield
        keep_copy.wait()

        def summed(level, at, count):
            total = None
            for name, base in [("keep", 1)] + [("got%d" % l, l + 1) for l in range(level)]:
                local = pl.multiple_of(at - starts[base], count)
                part = held[name][:, pl.ds(local, count), :].astype(F32)
                total = part if total is None else total + part
            return total

        for level in range(1, levels):
            copy.wait_recv()
            there = starts[level] + (1 - upper[level]) * sizes[level]
            held["sent%d" % level][...] = summed(level, there, sizes[level]).astype(BF16)
            copy = send(held["sent%d" % level], held["got%d" % level], replica_peer(order[level]), level)
            yield
        copy.wait_recv()
        held["final"][...] = summed(levels, starts[levels], sizes[-1]).astype(BF16)
        final = held["final"]
        here, count = starts[levels], sizes[-1]
        slot = levels
        if group == "out":
            own = pltpu.make_async_copy(final, place(here, count), local_sems.at[number, 1])
            own.start()
            own.wait()
        else:
            landing = shared_in if group == "shared" else None
            arrivals = []
            for offset in range(1, size):
                peer = copy_peer(offset)
                if group == "shared":
                    to_ref = shared_in.at[offset - 1]
                else:
                    to_ref = target.at[me, pl.ds(here, count), pl.ds(index * columns, columns)]
                arrivals.append(send(final.at[peer], to_ref, (replica, peer), slot))
                slot += 1
            if group == "shared":
                yield
                total = final[me].astype(F32)
                for offset in range(1, size):
                    arrivals[offset - 1].wait_recv()
                    total = total + shared_in[offset - 1].astype(F32)
                shared_sum[...] = total.astype(BF16)
                own = pltpu.make_async_copy(shared_sum, place(here, count), local_sems.at[number, 1])
                own.start()
                own.wait()
            else:
                own = pltpu.make_async_copy(
                    final.at[me], target.at[me, pl.ds(here, count), pl.ds(index * columns, columns)],
                    local_sems.at[number, 1],
                )
                own.start()
                yield
                own.wait()
                for arrival in arrivals:
                    arrival.wait_recv()
        for level in range(levels - 1, -1, -1):
            region = place(starts[level + 1], sizes[level])
            copy = send(region, region, replica_peer(order[level]), slot)
            slot += 1
            yield
            copy.wait_recv()
        for copy in pending:
            copy.wait_send()

    waiting = [run(number, *chunk) for number, chunk in enumerate(chunks)]
    active = []
    while waiting or active:
        active += waiting[:PER_TICK]
        waiting = waiting[PER_TICK:]
        still = []
        for steps in active:
            try:
                next(steps)
                still.append(steps)
            except StopIteration:
                pass
        active = still


PER_TICK = 2


def reduce_gradients(size, copies, depth, inner, common, grad_in, grad_out):
    width = grad_out.shape[2]
    chunks = reduce_chunks(size, copies, depth, inner, common, grad_out.shape[0] * OUT_CHUNK, width)
    shapes = {"out": (1, OUT_CHUNK, width), "in": (size, depth, COL_CHUNK), "shared": (size, depth, common)}
    counts = {name: sum(1 for chunk in chunks if chunk[0] == name) for name in shapes}
    scratch = []
    for name, (blocks, rows, columns) in shapes.items():
        fraction = {"keep": 2, "got0": 2, "sent1": 4, "got1": 4, "sent2": 8, "got2": 8, "final": 8}
        for stage in STAGES:
            scratch.append(pltpu.VMEM((counts[name], blocks, rows // fraction[stage], columns), BF16))
    scratch.append(pltpu.VMEM((size - 1, depth // copies, common), BF16))
    scratch.append(pltpu.VMEM((depth // copies, common), BF16))
    slots = 2 * len(axis_bits(copies)) + size - 1
    scratch.append(pltpu.SemaphoreType.DMA((len(chunks), slots)))
    scratch.append(pltpu.SemaphoreType.DMA((len(chunks), slots)))
    scratch.append(pltpu.SemaphoreType.DMA((len(chunks), 2)))
    anywhere = pl.BlockSpec(memory_space=pl.ANY)
    return pl.pallas_call(
        functools.partial(reduce_kernel, (size, copies, chunks, shapes)),
        in_specs=[anywhere] * 2,
        out_specs=[anywhere] * 3,
        out_shape=[
            jax.ShapeDtypeStruct((size, depth, 2 * inner), BF16),
            jax.ShapeDtypeStruct((depth, common), BF16),
            jax.ShapeDtypeStruct(grad_out.shape, BF16),
        ],
        scratch_shapes=scratch,
        compiler_params=pltpu.CompilerParams(
            collective_id=0, has_side_effects=True, vmem_limit_bytes=56 << 20
        ),
        cost_estimate=pl.CostEstimate(flops=0, bytes_accessed=700 << 20, transcendentals=0),
        name="reduce_gradients",
    )(grad_in, grad_out)


def small_pieces(size, copies, depth, inner, columns, me, replica, scaled_low, gp, normed_low, cot_all):
    replica_bits = axis_bits(copies)
    orders = [replica_bits, replica_bits[1:] + replica_bits[:1]]
    pieces = []
    part_rows = inner // 2
    for part in range(2):
        grad = contract_rows(normed_low[:, part * part_rows : (part + 1) * part_rows], cot_all)
        order = orders[part % 2]
        mine = halve_sum(grad[None], order, replica, copies)
        pieces.append(double_gather(mine.astype(BF16), order, replica, copies)[0])
    grad_w_out = jnp.concatenate(pieces, 0).astype(F32)


    def columns_sum(start, stop, order, shared):
        grad = contract_rows(scaled_low, gp[:, start:stop])
        mine = halve_sum(grad.reshape(size, depth, stop - start), order, replica, copies)
        own = lax.dynamic_index_in_dim(mine, me, 0, keepdims=False)
        got = [own]
        for offset in range(1, size):
            there = lax.dynamic_index_in_dim(mine, me ^ offset, 0, keepdims=False)
            got.append(swap(there.astype(BF16), "fsdp", size, offset))
        if shared:
            held = sum(block.astype(F32) for block in got)[None].astype(BF16)
        else:
            held = jnp.stack([block.astype(BF16) for block in got])
        return double_gather(held, order, replica, copies)

    halves = inner // 2
    value_parts = [columns_sum(c * halves, (c + 1) * halves, orders[c % 2], False) for c in range(2)]
    gate_parts = [
        columns_sum(inner + c * halves, inner + (c + 1) * halves, orders[c % 2], False) for c in range(2)
    ]
    shared_part = columns_sum(2 * inner, columns, orders[0], True)[0]

    def in_place(parts):
        placed = []
        for device in range(size):
            for part in parts:
                placed.append(lax.dynamic_index_in_dim(part, me ^ device, 0, keepdims=False))
        return placed

    grad_w_in = jnp.concatenate(in_place(gate_parts) + in_place(value_parts) + [shared_part], 1).astype(F32)
    return grad_w_in, grad_w_out


def on_device(copies, size, hidden_in, segment_ids, cotangent, norm_gain, w_in, conv_weight, conv_bias,
              dt_bias, a_log, skip_gain, gate_gain, w_out):
    micro_count, seq_count, tokens, width = hidden_in.shape
    own_rows = micro_count * seq_count * tokens
    total = size * own_rows
    inner = gate_gain.shape[0]
    local_heads = dt_bias.shape[0]
    heads = local_heads * size
    channel = inner // local_heads
    full_inner = inner * size
    taps, own_conv = conv_weight.shape
    conv_width = own_conv * size
    state2 = conv_width - full_inner
    depth = w_in.shape[0]
    common = state2 + heads
    columns = 2 * inner + common
    dims = (tokens, inner, state2, heads, local_heads, taps)
    me = lax.axis_index("fsdp")
    replica = lax.axis_index("replica")

    own_x = hidden_in.reshape(own_rows, width)
    own_cot = cotangent.reshape(own_rows, width)
    x_all = gather_relative(own_x, "fsdp", size).reshape(total, width)
    small = jnp.concatenate([norm_gain, conv_weight.reshape(-1), conv_bias])
    small = lax.all_gather(small, "fsdp", axis=0, tiled=False).astype(F32)
    full_norm = small[:, :depth].reshape(1, width)
    full_cw = small[:, depth : depth + taps * own_conv].reshape(size, taps, own_conv)
    full_cw = full_cw.transpose(1, 0, 2).reshape(taps, conv_width)
    full_cb = small[:, depth + taps * own_conv :].reshape(1, conv_width)
    seg_all = gather_relative(segment_ids.reshape(micro_count * seq_count, tokens), "fsdp", size)
    seg_all = seg_all.reshape(total // tokens, tokens)

    def columns_of(device):
        return jnp.concatenate(
            [
                lax.dynamic_slice(w_in, (0, full_inner + device * inner), (depth, inner)),
                lax.dynamic_slice(w_in, (0, device * inner), (depth, inner)),
                w_in[:, 2 * full_inner :],
            ],
            1,
        )

    w_cols = jnp.zeros((size * depth, columns), BF16)
    w_cols = lax.dynamic_update_slice(w_cols, columns_of(me), (me * depth, 0))
    for offset in range(1, size):
        received = swap(columns_of(me ^ offset), "fsdp", size, offset)
        w_cols = lax.dynamic_update_slice(w_cols, received, ((me ^ offset) * depth, 0))
    cot_all = gather_relative(own_cot, "fsdp", size).reshape(total, width)

    def normalise(inputs):
        wide = inputs.astype(F32)
        return lax.rsqrt(jnp.mean(wide * wide, -1, keepdims=True) + EPS)

    scaled_low = (x_all.astype(F32) * normalise(x_all) * full_norm).astype(BF16)
    projected = jnp.dot(scaled_low, w_cols, preferred_element_type=F32)

    conv_all = jnp.concatenate([full_cw, full_cb, jnp.zeros((7 - taps, conv_width), F32)], 0)
    conv_own = jnp.concatenate(
        [lax.dynamic_slice(conv_all, (0, me * inner), (8, inner)), conv_all[:, full_inner:]], 1
    )
    pad_heads = lambda row: jnp.pad(row.astype(F32), (0, LANES - local_heads))
    head_rows = jnp.stack([pad_heads(dt_bias), pad_heads(-jnp.exp(a_log.astype(F32)))])
    head_rows = jnp.pad(head_rows, ((0, 6), (0, 0)))
    chan_rows = jnp.stack([jnp.repeat(skip_gain.astype(F32), channel), gate_gain.astype(F32)])
    chan_rows = jnp.pad(chan_rows, ((0, 6), (0, 0)))
    same = []
    for offset in range(1, taps):
        equal = (seg_all[:, offset:] == seg_all[:, :-offset]).astype(F32)
        same.append(jnp.pad(equal, ((0, 0), (offset, 0))))
    same = jnp.pad(jnp.stack(same, 2), ((0, 0), (0, 0), (0, 9 - taps)))
    operands = (
        me.astype(jnp.int32).reshape(1), projected, seg_all[:, :, None], seg_all[:, None, :], same,
        head_rows, conv_own, chan_rows,
    )
    gated, squares = mix_forward(dims, operands)
    grad_normed = contract_cols(cot_all, w_out)
    cross = jnp.sum(gated.astype(F32) * grad_normed, 1)
    stats = sum_tokens(jnp.stack([squares[:, 0], cross]), "fsdp", size)
    root = lax.rsqrt(stats[0] / full_inner + EPS)
    pull = root * root * root * stats[1] / full_inner

    out_part = jnp.dot(gated, w_out, preferred_element_type=F32).astype(BF16)
    out_sum = scatter_relative(out_part.reshape(size, own_rows, width), "fsdp", size)
    block_out = (own_x.astype(F32) + root[:own_rows, None] * out_sum).astype(BF16)
    block_out = block_out.reshape(hidden_in.shape)

    normed_low = (gated.astype(F32) * root[:, None]).astype(BF16)
    gp, grad_conv, grad_chan, grad_head = mix_backward(
        dims, operands, jnp.stack([root, pull], 1), grad_normed
    )

    full_levels = copies == 8 and depth % (16 * copies) == 0 and inner % COL_CHUNK == 0
    if full_levels:
        grad_out = contract_rows(normed_low, cot_all).astype(BF16)
        grad_cols = contract_rows(scaled_low, gp).astype(BF16)
        sum_in, sum_shared, sum_out = reduce_gradients(
            size, copies, depth, inner, common,
            grad_cols.reshape(size, depth, columns), grad_out.reshape(inner // OUT_CHUNK, OUT_CHUNK, width),
        )
        grad_w_out = sum_out.reshape(inner, width).astype(F32)
        by_kind = [sum_in[device, :, inner:] for device in range(size)]
        by_kind += [sum_in[device, :, :inner] for device in range(size)]
        grad_w_in = jnp.concatenate(by_kind + [sum_shared], 1).astype(F32)
    else:
        grad_w_in, grad_w_out = small_pieces(
            size, copies, depth, inner, columns, me, replica, scaled_low, gp, normed_low, cot_all
        )

    scaled_part = contract_cols(gp, w_cols).astype(BF16)
    grad_scaled = scatter_relative(scaled_part.reshape(size, own_rows, width), "fsdp", size)
    own_wide = own_x.astype(F32)
    own_root = normalise(own_x)
    gained = grad_scaled * full_norm
    inner_mean = jnp.mean(gained * own_wide, -1, keepdims=True)
    grad_in = own_cot.astype(F32) + own_root * gained - own_wide * (own_root * own_root * own_root * inner_mean)
    grad_in = grad_in.reshape(hidden_in.shape)
    grad_norm = jnp.sum(grad_scaled * own_wide * own_root, 0)

    conv_full = jnp.zeros((8, conv_width), F32)
    conv_full = lax.dynamic_update_slice(conv_full, grad_conv[:, inner:], (0, full_inner))
    conv_full = lax.dynamic_update_slice(conv_full, grad_conv[:, :inner], (0, me * inner))
    conv_full = conv_full[: taps + 1].reshape(-1)
    skip_grad = grad_chan[0].reshape(local_heads, channel).sum(1)
    own_small = jnp.concatenate(
        [grad_head[0, :local_heads], grad_head[1, :local_heads], skip_grad, grad_chan[1]]
    )
    conv_full, grad_norm = lax.psum((conv_full, grad_norm), ("replica", "fsdp"))
    own_small = lax.psum(own_small, "replica")
    conv_full = lax.dynamic_slice(conv_full.reshape(taps + 1, conv_width), (0, me * own_conv), (taps + 1, own_conv))
    grad_norm = lax.dynamic_slice(grad_norm, (me * depth,), (depth,))
    return (
        block_out,
        grad_in,
        grad_norm,
        grad_w_in,
        conv_full[:taps],
        conv_full[taps],
        own_small[:local_heads],
        own_small[local_heads : 2 * local_heads],
        own_small[2 * local_heads : 3 * local_heads],
        own_small[3 * local_heads :],
        grad_w_out,
    )


def solution(mesh):
    rows = ("replica", "fsdp")
    placed = (
        P(None, rows, None, None),
        P(None, rows, None),
        P(None, rows, None, None),
        P("fsdp"),
        P("fsdp", None),
        P(None, "fsdp"),
        P("fsdp"),
        P("fsdp"),
        P("fsdp"),
        P("fsdp"),
        P("fsdp"),
        P("fsdp", None),
    )
    return jax.shard_map(
        functools.partial(on_device, mesh.shape["replica"], mesh.shape["fsdp"]),
        mesh=mesh,
        in_specs=placed,
        out_specs=(
            P(None, rows, None, None),
            P(None, rows, None, None),
            P("fsdp"),
            P("fsdp", None),
            P(None, "fsdp"),
            P("fsdp"),
            P("fsdp"),
            P("fsdp"),
            P("fsdp"),
            P("fsdp"),
            P("fsdp", None),
        ),
        check_vma=False,
    )
```

time: 2000 us -> 1040 us (0.52)
  waiting for transfers between devices: 1330 us -> 67.1 us
  Pallas kernels: 0 us -> 466 us
  matrix products: 382 us -> 119 us
  blocking collectives: 80.8 us -> 198 us
  other arithmetic: 136 us -> 65.3 us
  local copies, waits for them, and re-layouts: 53.5 us -> 95.1 us
    psum x1, waiting for transfers between devices: 680 us -> 0.01 us  [on_device(): conv_full, grad_norm = lax.psum((conv_full, grad_norm), ('replica', 'fsdp'))]
    pallas_call x0 -> x3, Pallas kernels: none -> 466 us  [the longest x1 346 us: reduce_gradients(): pl.pallas_call(functools.partial(reduce_kernel, (size, copies, chunks, sh...]
    reduce_scatter x2 -> x0, waiting for transfers between devices: 464 us -> none  [the longest x1 464 us: on_device(): lax.psum_scatter(accum[1], 'fsdp', scatter_dimension=0, tiled=True)]
    dot_general x24 -> x6, matrix products: 382 us -> 119 us  [the longest x2 40.2 us: contract_cols(): lax.dot_general(left, right, (((1,), (1,)), ((), ())), precision=precisio...]
    all_gather x2 -> x0, waiting for transfers between devices: 181 us -> none  [the longest x1 181 us: on_device(): lax.all_gather(w_in, 'fsdp', axis=0, tiled=True)]
    unnamed x2 -> x1, blocking collectives: 23.6 us -> 134 us
    reduce_sum x13 -> x4, other arithmetic: 82.2 us -> 11.2 us  [the longest x1 6.32 us: on_device(): grad_norm = jnp.sum(grad_scaled * own_wide * own_root, 0)]
    ppermute x0 -> x15, waiting for transfers between devices: none -> 67.1 us  [swap(): return lax.ppermute(array, axis, [(i, i ^ bit) for i in range(size)])]
  transfers between devices with their start and end apart: 6 -> 16, of which waited for: 3 -> 3; matrix products, arithmetic and copies ran while one was open for 28% -> 23% of each run, Pallas kernels for 0% -> 45%
where the time goes in v1:
time: 1040 us
  Pallas kernels  466 us (45%)
  blocking collectives  198 us (19%)
  matrix products  119 us (11%)
  local copies, waits for them, and re-layouts  95.1 us (9%)
  waiting for transfers between devices  67.1 us (6%)
  other arithmetic  65.3 us (6%)
  between operations  15.6 us (2%)
    pallas_call x1, Pallas kernels, reduce_gradients(): pl.pallas_call(functools.partial(reduce_kernel, (size, copies, chunks, sh...  346 us
    unnamed x1, blocking collectives  134 us
    pallas_call x1, Pallas kernels, mix_backward(): pl.pallas_call(functools.partial(backward_kernel, dims), grid=(total // t...  78.5 us
    ppermute x15, waiting for transfers between devices, swap(): return lax.ppermute(array, axis, [(i, i ^ bit) for i in range(size)])  67.1 us
    psum x1, blocking collectives, on_device(): conv_full, grad_norm = lax.psum((conv_full, grad_norm), ('replica', 'fsdp'))  42.8 us
    pallas_call x1, Pallas kernels, mix_forward(): pl.pallas_call(functools.partial(forward_kernel, dims), grid=(total // to...  41.1 us
    dot_general x2, matrix products, contract_cols(): lax.dot_general(left, right, (((1,), (1,)), ((), ())), precision=precisio...  40.2 us
    dot_general x2, matrix products, contract_rows(): lax.dot_general(left, right, (((0,), (0,)), ((), ())), precision=precisio...  38.7 us
  transfers between devices with their start and end apart: 16, of which 3 were waited for; matrix products, arithmetic and copies ran while one was open for 23% of the time, Pallas kernels for 45%

profile of v1, /device:TPU:0, one launch (start us, length us, event | category | flops | bytes accessed | tf_op | source)
XLA Modules:
  0.0 1035.9 jit_solution(11840607171286443664)
XLA Ops:
  12.3 3.9 constant_dynamic-slice_fusion.3
  16.2 4.9 broadcast_in_dim.6
  27.0 133.7 %all-reduce.9 = bf16[23808]{0:T(1024)(128)(2,1)S(1)} all-reduce(bf16[23808]{0:T(1024)(128)(2,1)S(1)} %dynamic-update-slice), channel_id=2, replica_groups=mesh['replica'=8,'fsdp'=4] {'fsdp'}, use_global_device_ids=true, to_apply=%add.9 | all-reduce | flops 23808 | bytes 95232
  161.9 4.0 pad_maximum_fusion.5
  167.4 5.7 collective-permute-done.6
  177.1 4.6 pad_maximum_fusion.6
  188.9 39.1 %collective-permute-done.4 = bf16[512,2368]{0,1:T(8,128)(2,1)} collective-permute-done((bf16[512,2368]{0,1:T(8,128)(2,1)}, bf16[512,2368]{0,1:T(8,128)(2,1)}, u32[]{:S(2)}, u32[]{:S(2)}) %collective-permute-start.4) | collective-permute-done | bytes 2424864 | tf_op jit(solution)/shard_map/ppermute | solution.py:356
  231.4 4.3 multiply_reduce_fusion
  235.7 4.0 maximum_convert_fusion
  243.1 29.0 %fusion.29.proj_ref = f32[2048,2368]{1,0:T(8,128)} fusion(bf16[2048,2048]{1,0:T(8,128)(2,1)S(1)} %fusion.1, bf16[2048,2368]{0,1:T(8,128)(2,1)} %constant_dynamic-update-slice_fusion.1), kind=kOutput, calls=%fused_computation.112 | convolution fusion | flops 19864223744 | bytes 37486592 | tf_op jit(solution)/shard_map/dot_general | solution.py:726
  272.1 41.1 %mix_forward.1 = (bf16[2048,1024]{1,0:T(8,128)(2,1)}, f32[2048,1]{1,0:T(8,128)S(1)}) custom-call(s32[1]{0:T(128)} %bitcast.own_ref, f32[2048,2368]{1,0:T(8,128)} %fusion.29.proj_ref, s32[8,256,1]{2,1,0:T(8,128)S(1)} %broadcast_in_dim_reshape.20.seg_col_ref, s32[8,1,256]{2,1,0:T(1,128)S(1)} %broadcast_in_dim_reshape.18.seg_row_ref, ...), custom_call_target="tpu_custom_call" | custom-call | flops 2147483648 | bytes 19398656 | tf_op jit(solution)/shard_map/mix_forward/pallas_call | solution.py:292
  313.5 5.6 pad_maximum_fusion
  319.5 11.9 %fusion.2 = (f32[2048]{0:T(1024)S(1)}, f32[2048,1024]{1,0:T(8,128)}) fusion(bf16[2048,1024]{1,0:T(8,128)(2,1)S(1)} %copy-done.25, bf16[2048,2048]{1,0:T(8,128)(2,1)S(1)} %bitcast.123, bf16[1024,2048]{1,0:T(8,128)(2,1)S(1)} %copy-done.24), kind=kOutput, calls=%fused_computation.7 | convolution fusion | flops 8596224000 | bytes 25174016 | tf_op jit(solution)/shard_map/dot_general | solution.py:25
  331.7 10.9 %convolution_convert_fusion.2 = bf16[2048,2048]{1,0:T(8,128)(2,1)} fusion(bf16[2048,1024]{1,0:T(8,128)(2,1)S(1)} %copy-done.25, bf16[1024,2048]{1,0:T(8,128)(2,1)S(1)} %copy-done.24), kind=kOutput, calls=%fused_computation.14 | convolution fusion | flops 8594128896 | bytes 16777216 | tf_op jit(solution)/shard_map/dot_general | solution.py:753
  344.6 6.1 fusion.26
  351.5 78.5 %mix_backward.1 = (bf16[2048,2368]{1,0:T(8,128)(2,1)}, f32[8,1280]{1,0:T(8,128)S(1)}, f32[8,1024]{1,0:T(8,128)S(1)}, f32[8,128]{1,0:T(8,128)S(1)}) custom-call(s32[1]{0:T(128)} %bitcast.own_ref, f32[2048,2368]{1,0:T(8,128)} %fusion.29.proj_ref, s32[8,256,1]{2,1,0:T(8,128)S(1)} %broadcast_in_dim_reshape.20.seg_col_ref, ...), custom_call_target="tpu_custom_call" | custom-call | flops 6442450944 | bytes 29097984 | tf_op jit(solution)/shard_map/mix_backward/pallas_call | solution.py:320
  430.0 28.3 %convolution_convert_fusion.1 = bf16[2048,2048]{1,0:T(8,128)(2,1)} fusion(bf16[2048,2368]{1,0:T(8,128)(2,1)} %get-tuple-element.22, bf16[2048,2368]{0,1:T(8,128)(2,1)} %constant_dynamic-update-slice_fusion.1), kind=kOutput, calls=%fused_computation.13 | convolution fusion | flops 19868418048 | bytes 27787264 | tf_op jit(solution)/shard_map/dot_general | solution.py:25
  458.3 27.3 %convolution_convert_fusion = bf16[2048,2368]{0,1:T(8,128)(2,1)} fusion(bf16[2048,2048]{1,0:T(8,128)(2,1)} %copy-done.9, bf16[2048,2368]{1,0:T(8,128)(2,1)} %get-tuple-element.22), kind=kOutput, calls=%fused_computation.4 | convolution fusion | flops 19869073408 | bytes 27787264 | tf_op jit(solution)/shard_map/dot_general | solution.py:19
  485.6 6.5 fusion.25
  492.5 11.4 %fusion.13 = bf16[1024,2048]{1,0:T(8,128)(2,1)} fusion(bf16[2048,2048]{1,0:T(8,128)(2,1)S(1)} %bitcast.126, bf16[2048,1024]{1,0:T(8,128)(2,1)S(1)} %copy-done.26, f32[2048]{0:T(1024)S(1)} %bitcast.143), kind=kOutput, calls=%fused_computation.40 | convolution fusion | flops 8598323200 | bytes 16785408 | tf_op jit(solution)/shard_map/dot_general | solution.py:19
  504.7 13.5 %copy.105 = bf16[2048,2368]{1,0:T(8,128)(2,1)} copy(bf16[2048,2368]{0,1:T(8,128)(2,1)} %convolution_convert_fusion) | data formatting | bytes 19398656 | tf_op jit(solution)/shard_map/convert_element_type | solution.py:766
  518.2 346.2 %reduce_gradients.1 = (bf16[4,512,2048]{2,1,0:T(8,128)(2,1)}, bf16[512,320]{1,0:T(8,128)(2,1)}, bf16[4,256,2048]{2,1,0:T(8,128)(2,1)}) custom-call(bf16[4,512,2368]{2,1,0:T(8,128)(2,1)} %bitcast.115, bf16[4,256,2048]{2,1,0:T(8,128)(2,1)} %bitcast.127), custom_call_target="tpu_custom_call" | custom-call | bytes 734003200 | tf_op jit(solution)/shard_map/reduce_gradients/pallas_call | solution.py:609
  879.1 4.0 convert_add_fusion.1
  888.4 4.0 convert_add_fusion
  898.4 21.8 %psum.23 = f32[1072]{0:T(1024)S(1)} all-reduce(f32[1072]{0:T(1024)S(1)} %concatenate.62), channel_id=1, replica_groups=mesh['replica'=8,'fsdp'=4] {'replica'}, use_global_device_ids=true, to_apply=%region_8.9 | all-reduce | flops 1072 | bytes 8576 | tf_op jit(solution)/shard_map/psum | solution.py:799
  920.8 6.7 bitcast_convert_fusion
  928.2 13.3 %copy.106 = f32[512,8512]{0,1:T(8,128)} copy(bf16[512,8512]{1,0:T(8,128)(2,1)} %constant_dynamic-update-slice_fusion) | data formatting | bytes 26148864
  944.4 5.8 slice_add_fusion.1
  950.2 22.2 %collective-permute-done.14 = bf16[1,512,2048]{2,1,0:T(8,128)(2,1)} collective-permute-done((bf16[1,512,2048]{2,1,0:T(8,128)(2,1)}, bf16[1,512,2048]{2,1,0:T(8,128)(2,1)}, u32[]{:S(2)}, u32[]{:S(2)}) %collective-permute-start.14) | collective-permute-done | bytes 2097184 | tf_op jit(solution)/shard_map/ppermute | solution.py:356
  972.4 6.3 fusion.11
  978.8 42.8 %psum.21 = f32[2048]{0:T(1024)S(1)} all-reduce(f32[2048]{0:T(1024)S(1)} %get-tuple-element.84), channel_id=1, replica_groups=mesh['replica'=8,'fsdp'=4] {'replica','fsdp'}, use_global_device_ids=true, to_apply=%region_5.6 | all-reduce | flops 2048 | bytes 16384 | tf_op jit(solution)/shard_map/psum | solution.py:798
  1022.2 6.6 fusion.8
  (191 shorter events, 66.3 us)
Async XLA Ops:
  7.2 934.2 %all-reduce.12.cloned.1.call-start = ((), (), s32[]{:S(2)}) async-start(), calls=%async_computation | async-start | bytes 278528 | tf_op jit(solution)/shard_map/psum | solution.py:798
  7.2 159.7 %collective-permute-start.5 = (s32[1,2,256]{2,0,1:T(1,128)}, s32[1,2,256]{2,0,1:T(1,128)S(1)}, u32[]{:S(2)}, u32[]{:S(2)}) collective-permute-start(s32[1,2,256]{2,0,1:T(1,128)} %bitcast.148), channel_id=1, source_target_pairs={{0,2},{1,3},{2,0},{3,1},{4,6},{5,7},{6,4},{7,5},{8,10},{9,11},{10,... | collective-permute-start | bytes 6152 | tf_op jit(solution)/shard_map/ppermute | solution.py:356
  10.3 166.8 %collective-permute-start.7 = (bf16[1,512,2048]{2,1,0:T(8,128)(2,1)}, bf16[1,512,2048]{2,1,0:T(8,128)(2,1)}, u32[]{:S(2)}, u32[]{:S(2)}) collective-permute-start(bf16[1,512,2048]{2,1,0:T(8,128)(2,1)} %bitcast.116), channel_id=1, source_target_pairs={{0,2},{1,3},{2,0},{3,1},{4,6},{5,7},{6,4},{7,5},{8,10},{9,11},{10,... | collective-permute-start | bytes 6291464 | tf_op jit(solution)/shard_map/ppermute | solution.py:356
  10.3 151.6 %collective-permute-start = (bf16[1,512,2048]{2,1,0:T(8,128)(2,1)}, bf16[1,512,2048]{2,1,0:T(8,128)(2,1)}, u32[]{:S(2)}, u32[]{:S(2)}) collective-permute-start(bf16[1,512,2048]{2,1,0:T(8,128)(2,1)} %bitcast.111), channel_id=1, source_target_pairs={{0,2},{1,3},{2,0},{3,1},{4,6},{5,7},{6,4},{7,5},{8,10},{9,11},{10,... | collective-permute-start | bytes 6291464 | tf_op jit(solution)/shard_map/ppermute | solution.py:356
  21.2 140.1 %copy-start = (bf16[2,1,256,2048]{3,2,1,0:T(8,128)(2,1)S(1)}, bf16[2,1,256,2048]{3,2,1,0:T(8,128)(2,1)}, u32[]{:S(2)}) copy-start(bf16[2,1,256,2048]{3,2,1,0:T(8,128)(2,1)} %param.12) | copy-start | bytes 6291460
  25.1 157.0 %collective-permute-start.2 = (bf16[512,2368]{0,1:T(8,128)(2,1)}, bf16[512,2368]{0,1:T(8,128)(2,1)}, u32[]{:S(2)}, u32[]{:S(2)}) collective-permute-start(bf16[512,2368]{0,1:T(8,128)(2,1)} %get-tuple-element.104), channel_id=1, source_target_pairs={{0,1},{1,0},{2,3},{3,2},{4,5},{5,4},{6,7},{7,6},{8,9},{9,8},{10,11... | collective-permute-start | bytes 7274504 | tf_op jit(solution)/shard_map/ppermute | solution.py:356
  25.1 160.3 %collective-permute-start.3 = (bf16[512,2368]{0,1:T(8,128)(2,1)}, bf16[512,2368]{0,1:T(8,128)(2,1)}, u32[]{:S(2)}, u32[]{:S(2)}) collective-permute-start(bf16[512,2368]{0,1:T(8,128)(2,1)} %get-tuple-element.105), channel_id=1, source_target_pairs={{0,2},{1,3},{2,0},{3,1},{4,6},{5,7},{6,4},{7,5},{8,10},{9,11},{10,... | collective-permute-start | bytes 7274504 | tf_op jit(solution)/shard_map/ppermute | solution.py:356
  161.8 14.3 %copy-start.14 = (f32[2,256]{1,0:T(2,128)}, f32[2,256]{1,0:T(2,128)S(1)}, u32[]{:S(2)}) copy-start(f32[2,256]{1,0:T(2,128)S(1)} %fusion.7) | copy-start | bytes 6148
  165.9 65.5 %collective-permute-start.1 = (bf16[2,512,2048]{2,1,0:T(8,128)(2,1)}, bf16[2,512,2048]{2,1,0:T(8,128)(2,1)}, u32[]{:S(2)}, u32[]{:S(2)}) collective-permute-start(bf16[2,512,2048]{2,1,0:T(8,128)(2,1)} %pad_maximum_fusion.5), channel_id=1, source_target_pairs={{0,1},{1,0},{2,3},{3,2},{4,5},{5,4},{6,7},{7,6},{8,9},{9,8},{10,11... | collective-permute-start | bytes 12582920 | tf_op jit(solution)/shard_map/ppermute | solution.py:356
  166.9 6.2 collective-permute-start.6
  173.1 55.0 %collective-permute-start.4 = (bf16[512,2368]{0,1:T(8,128)(2,1)}, bf16[512,2368]{0,1:T(8,128)(2,1)}, u32[]{:S(2)}, u32[]{:S(2)}) collective-permute-start(bf16[512,2368]{0,1:T(8,128)(2,1)} %get-tuple-element.103), channel_id=1, source_target_pairs={{0,3},{1,2},{2,1},{3,0},{4,7},{5,6},{6,5},{7,4},{8,11},{9,10},{10,... | collective-permute-start | bytes 7274504 | tf_op jit(solution)/shard_map/ppermute | solution.py:356
  175.1 64.6 %copy-start.12 = (f32[1,4,4,128]{3,1,2,0:T(4,128)}, f32[1,4,4,128]{3,1,2,0:T(4,128)S(1)}, u32[]{:S(2)}) copy-start(f32[1,4,4,128]{3,1,2,0:T(4,128)S(1)} %copy.110) | copy-start | bytes 24580
  181.7 131.8 %collective-permute-start.8 = (bf16[2,512,2048]{2,1,0:T(8,128)(2,1)}, bf16[2,512,2048]{2,1,0:T(8,128)(2,1)}, u32[]{:S(2)}, u32[]{:S(2)}) collective-permute-start(bf16[2,512,2048]{2,1,0:T(8,128)(2,1)} %pad_maximum_fusion.6), channel_id=1, source_target_pairs={{0,1},{1,0},{2,3},{3,2},{4,5},{5,4},{6,7},{7,6},{8,9},{9,8},{10,11... | collective-permute-start | bytes 12582920 | tf_op jit(solution)/shard_map/ppermute | solution.py:356
  185.4 46.0 %copy-start.1 = (bf16[2,1,256,2048]{3,2,1,0:T(8,128)(2,1)S(1)}, bf16[2,1,256,2048]{3,2,1,0:T(8,128)(2,1)}, u32[]{:S(2)}) copy-start(bf16[2,1,256,2048]{3,2,1,0:T(8,128)(2,1)} %param.12) | copy-start | bytes 6291460
  243.1 29.0 %copy-start.9 = (bf16[2048,2048]{1,0:T(8,128)(2,1)}, bf16[2048,2048]{1,0:T(8,128)(2,1)S(1)}, u32[]{:S(2)}) copy-start(bf16[2048,2048]{1,0:T(8,128)(2,1)S(1)} %fusion.1) | copy-start | bytes 25165828
  319.2 12.3 %copy-start.8 = (bf16[4,512,2048]{2,1,0:T(8,128)(2,1)}, bf16[4,512,2048]{2,1,0:T(8,128)(2,1)S(1)}, u32[]{:S(2)}) copy-start(bf16[4,512,2048]{2,1,0:T(8,128)(2,1)S(1)} %pad_maximum_fusion) | copy-start | bytes 25165828
  331.5 11.1 %collective-permute-start.9 = (f32[2,2048]{1,0:T(2,128)S(1)}, f32[2,2048]{1,0:T(2,128)S(1)}, u32[]{:S(2)}, u32[]{:S(2)}) collective-permute-start(f32[2,2048]{1,0:T(2,128)S(1)} %pad_maximum_fusion.8), channel_id=1, source_target_pairs={{0,1},{1,0},{2,3},{3,2},{4,5},{5,4},{6,7},{7,6},{8,9},{9,8},{10,11... | collective-permute-start | bytes 49160 | tf_op jit(solution)/shard_map/ppermute | solution.py:356
  342.9 7.9 collective-permute-start.10
  350.6 528.5 %collective-permute-start.11 = (bf16[2,512,2048]{2,1,0:T(8,128)(2,1)}, bf16[2,512,2048]{2,1,0:T(8,128)(2,1)}, u32[]{:S(2)}, u32[]{:S(2)}) collective-permute-start(bf16[2,512,2048]{2,1,0:T(8,128)(2,1)} %bitcast.16), channel_id=1, source_target_pairs={{0,1},{1,0},{2,3},{3,2},{4,5},{5,4},{6,7},{7,6},{8,9},{9,8},{10,11... | collective-permute-start | bytes 12582920 | tf_op jit(solution)/shard_map/ppermute | solution.py:356
  430.0 62.5 %slice-start.1 = ((s8[8388608]{0:T(1024)(128)(4,1)}), s8[4194304]{0:T(1024)(128)(4,1)S(1)}, s32[]{:S(2)}) async-start(s8[8388608]{0:T(1024)(128)(4,1)} %bitcast.124), calls=%async_computation.2 | async-start | bytes 8388608
  458.3 34.2 %slice-start.2 = ((s8[8388608]{0:T(1024)(128)(4,1)}), s8[4194304]{0:T(1024)(128)(4,1)S(1)}, s32[]{:S(2)}) async-start(s8[8388608]{0:T(1024)(128)(4,1)} %bitcast.124), calls=%async_computation.3 | async-start | bytes 8388608
  492.2 392.6 %collective-permute-start.13 = (bf16[2,512,2048]{2,1,0:T(8,128)(2,1)}, bf16[2,512,2048]{2,1,0:T(8,128)(2,1)}, u32[]{:S(2)}, u32[]{:S(2)}) collective-permute-start(bf16[2,512,2048]{2,1,0:T(8,128)(2,1)} %bitcast.21), channel_id=1, source_target_pairs={{0,1},{1,0},{2,3},{3,2},{4,5},{5,4},{6,7},{7,6},{8,9},{9,8},{10,11... | collective-permute-start | bytes 12582920 | tf_op jit(solution)/shard_map/ppermute | solution.py:356
  864.4 10.3 copy-start.7
  872.1 7.1 copy-start.5
  884.8 59.6 %collective-permute-start.12 = (bf16[1,512,2048]{2,1,0:T(8,128)(2,1)}, bf16[1,512,2048]{2,1,0:T(8,128)(2,1)}, u32[]{:S(2)}, u32[]{:S(2)}) collective-permute-start(bf16[1,512,2048]{2,1,0:T(8,128)(2,1)} %slice.253), channel_id=1, source_target_pairs={{0,2},{1,3},{2,0},{3,1},{4,6},{5,7},{6,4},{7,5},{8,10},{9,11},{10,... | collective-permute-start | bytes 6291464 | tf_op jit(solution)/shard_map/ppermute | solution.py:356
  888.4 8.9 copy-start.11
  897.3 75.1 %collective-permute-start.14 = (bf16[1,512,2048]{2,1,0:T(8,128)(2,1)}, bf16[1,512,2048]{2,1,0:T(8,128)(2,1)}, u32[]{:S(2)}, u32[]{:S(2)}) collective-permute-start(bf16[1,512,2048]{2,1,0:T(8,128)(2,1)} %slice.252), channel_id=1, source_target_pairs={{0,2},{1,3},{2,0},{3,1},{4,6},{5,7},{6,4},{7,5},{8,10},{9,11},{10,... | collective-permute-start | bytes 6291464 | tf_op jit(solution)/shard_map/ppermute | solution.py:356
  944.4 28.1 %copy-start.2 = (bf16[2,1,256,2048]{3,2,1,0:T(8,128)(2,1)S(1)}, bf16[2,1,256,2048]{3,2,1,0:T(8,128)(2,1)}, u32[]{:S(2)}) copy-start(bf16[2,1,256,2048]{3,2,1,0:T(8,128)(2,1)} %param.12) | copy-start | bytes 6291460
  944.4 28.1 %copy-start.13 = (f32[1,4,4,128]{3,1,2,0:T(4,128)S(1)}, f32[1,4,4,128]{3,1,2,0:T(4,128)}, u32[]{:S(2)}) copy-start(f32[1,4,4,128]{3,1,2,0:T(4,128)} %copy-done.12) | copy-start | bytes 24580
  944.4 28.1 %copy-start.18 = (f32[1,2,2,128]{3,1,2,0:T(2,128)S(1)}, f32[1,2,2,128]{3,1,2,0:T(2,128)}, u32[]{:S(2)}) copy-start(f32[1,2,2,128]{3,1,2,0:T(2,128)} %copy.112) | copy-start | bytes 6148
  972.4 49.8 %copy-start.15 = (f32[2,256]{1,0:T(2,128)S(1)}, f32[2,256]{1,0:T(2,128)}, u32[]{:S(2)}) copy-start(f32[2,256]{1,0:T(2,128)} %copy-done.14) | copy-start | bytes 6148
  972.4 49.8 %copy-start.17 = (f32[2,256]{1,0:T(2,128)S(1)}, f32[2,256]{1,0:T(2,128)}, u32[]{:S(2)}) copy-start(f32[2,256]{1,0:T(2,128)} %get-tuple-element.114) | copy-start | bytes 6148
  (17 other events, 81.1 us)
Sparse Core Ops, SparseCore 0:
  504.8 132.9 all-reduce.11

commit v2 on v1

--- a/solution.py
+++ b/solution.py
@@ -420,208 +420,495 @@
     return index + bit * (1 - 2 * ((index // bit) % 2))
 
 
-def reduce_chunks(size, copies, depth, inner, common, out_rows, width):
-    bits = axis_bits(copies)
-    first, second = bits, bits[1:] + bits[:1]
-    chunks = []
-    for index in range(out_rows // OUT_CHUNK):
-        chunks.append(("out", index, second if index % 2 else first))
-    for index in range(2 * inner // COL_CHUNK):
-        chunks.append(("in", index, second if index % 2 else first))
-    chunks.append(("shared", 0, first))
-    return chunks
-
-
-COL_CHUNK = 256
-OUT_CHUNK = 256
-STAGES = ("keep", "got0", "sent1", "got1", "sent2", "got2", "final")
-
-
-def reduce_kernel(plan, in_ref, out_ref, sum_in_ref, sum_shared_ref, sum_out_ref, *scratch):
-    size, copies, chunks, shapes = plan
-    groups = {}
-    position = 0
-    for name in shapes:
-        groups[name] = dict(zip(STAGES, scratch[position : position + len(STAGES)]))
-        position += len(STAGES)
-    shared_in, shared_sum = scratch[position], scratch[position + 1]
-    send_sems, recv_sems, local_sems = scratch[position + 2 :]
-    me = lax.axis_index("fsdp")
-    replica = lax.axis_index("replica")
-    levels = len(axis_bits(copies))
-    MESH = pl.DeviceIdType.MESH
-
-    def replica_peer(bit):
-        return (flip(replica, bit), me)
-
-    def copy_peer(offset):
-        other = me
-        for bit in axis_bits(size):
-            if offset & bit:
-                other = flip(other, bit)
-        return other
-
+MESH = pl.DeviceIdType.MESH
+
+
+def greet(peers):
     barrier = pltpu.get_barrier_semaphore()
-    peers = [replica_peer(bit) for bit in axis_bits(copies)]
-    peers += [(replica, copy_peer(offset)) for offset in range(1, size)]
     for peer in peers:
         pl.semaphore_signal(barrier, inc=1, device_id=peer, device_id_type=MESH)
     pl.semaphore_wait(barrier, len(peers))
 
-    def run(number, group, index, order):
-        blocks, rows, columns = shapes[group]
-        if group == "in":
-            source, target = in_ref, sum_in_ref
-            cut = lambda ref, at, count: ref.at[:, pl.ds(at, count), pl.ds(index * columns, columns)]
-        elif group == "shared":
-            source, target = in_ref, sum_shared_ref
-            cut = lambda ref, at, count: ref.at[:, pl.ds(at, count), pl.ds(in_ref.shape[2] - columns, columns)]
+
+def copy_peers(me):
+    return [flip(me, 1), flip(me, 2), flip(flip(me, 1), 2)]
+
+
+def gather_kernel(full_inner, inner, x_ref, seg_ref, small_ref, w_ref,
+                  x_all_ref, seg_all_ref, small_all_ref, cols_ref,
+                  x_held, cols_held, send_sems, recv_sems, local_sems, store_sems):
+    me = lax.axis_index("fsdp")
+    replica = lax.axis_index("replica")
+    depth, common = w_ref.shape[1], w_ref.shape[0] - 2 * full_inner
+    peers = [(replica, peer) for peer in copy_peers(me)]
+    beside, above = (flip(replica, 1), me), (flip(replica, 2), me)
+    greet(peers + [beside, above])
+    number = [0]
+    started = []
+
+    def send(from_ref, to_ref, device):
+        slot = number[0]
+        number[0] += 1
+        copy = pltpu.make_async_remote_copy(
+            src_ref=from_ref, dst_ref=to_ref, send_sem=send_sems.at[slot], recv_sem=recv_sems.at[slot],
+            device_id=device, device_id_type=MESH,
+        )
+        copy.start()
+        started.append(copy)
+        return copy
+
+    parts = [(0, inner), (inner, inner), (2 * inner, common)]
+
+    def targets(owner, first, count):
+        lanes = pl.ds(pl.multiple_of(owner * depth, depth), depth)
+        return [
+            cols_ref.at[pl.ds(pl.multiple_of(base + first * (length // 4), 16), count * (length // 4)), lanes]
+            for base, length in parts
+        ]
+
+    def sources(device, first, count):
+        bases = [full_inner + device * inner, device * inner, 2 * full_inner]
+        return [
+            w_ref.at[pl.ds(pl.multiple_of(base + first * (length // 4), 16), count * (length // 4))]
+            for base, (_, length) in zip(bases, parts)
+        ]
+
+    def send_parts(from_refs, to_refs, device):
+        return [send(source, target, device) for source, target in zip(from_refs, to_refs)]
+
+    spot = replica % 4
+    across = [send_parts(sources(peers[which][1], spot, 1), targets(me, spot, 1), peers[which]) for which in (1, 2)]
+    x_y = send(x_ref, x_all_ref.at[1], peers[1])
+    smalls = [send(small_ref, small_all_ref.at[me], peer) for peer in peers]
+    smalls += [send(seg_ref, seg_all_ref.at[slot], peer) for peer, slot in zip(peers, (2, 1, 3))]
+    near = send_parts(sources(peers[0][1], 0, 4), targets(me, 0, 4), peers[0])
+    x_near = send(x_ref, x_all_ref.at[2], peers[0])
+    held = [cols_held.at[pl.ds(base, length)] for base, length in parts] + [x_held]
+    own = list(zip(sources(me, 0, 4) + [x_ref], held, targets(me, 0, 4) + [x_all_ref.at[0]]))
+    loads = [pltpu.make_async_copy(source, held, local_sems.at[i]) for i, (source, held, _) in enumerate(own)]
+    stores = [pltpu.make_async_copy(held, target, store_sems.at[i]) for i, (_, held, target) in enumerate(own)]
+    stores += [
+        pltpu.make_async_copy(small_ref, small_all_ref.at[me], local_sems.at[4]),
+        pltpu.make_async_copy(seg_ref, seg_all_ref.at[0], local_sems.at[5]),
+    ]
+    for copy in loads + stores[4:]:
+        copy.start()
+    for load, store in zip(loads, stores):
+        load.wait()
+        store.start()
+
+    def relay(which, first, count, device):
+        refs = targets(peers[which][1], first, count)
+        return send_parts(refs, refs, device)
+
+    for copy in across[0]:
+        copy.wait_recv()
+    first_beside = relay(1, spot, 1, beside)
+    for copy in across[1]:
+        copy.wait_recv()
+    first_above = relay(2, spot, 1, above)
+    for copy in first_beside:
+        copy.wait_recv()
+    last = relay(1, (spot // 2) * 2, 2, above)
+    for copy in first_above:
+        copy.wait_recv()
+    last += relay(2, spot, 1, beside)
+    last += relay(2, flip(spot, 2), 1, beside)
+    x_y.wait_recv()
+    last.append(send(x_all_ref.at[1], x_all_ref.at[3], peers[0]))
+    for copy in last + smalls + near + [x_near]:
+        copy.wait_recv()
+    for copy in stores:
+        copy.wait()
+    for copy in started:
+        copy.wait_send()
+
+
+GATHER_COPIES = 34
+
+
+def gather_inputs(size, inner, x, segments, small, w_flipped):
+    full, depth = w_flipped.shape
+    full_inner = inner * size
+    columns = 2 * inner + full - 2 * full_inner
+    anywhere = pl.BlockSpec(memory_space=pl.ANY)
+    return pl.pallas_call(
+        functools.partial(gather_kernel, full_inner, inner),
+        in_specs=[anywhere] * 4,
+        out_specs=[anywhere] * 4,
+        out_shape=[
+            jax.ShapeDtypeStruct((size,) + x.shape, BF16),
+            jax.ShapeDtypeStruct((size,) + segments.shape, jnp.int32),
+            jax.ShapeDtypeStruct((size,) + small.shape, F32),
+            jax.ShapeDtypeStruct((columns, size * depth), BF16),
+        ],
+        scratch_shapes=[
+            pltpu.VMEM(x.shape, BF16),
+            pltpu.VMEM((columns, depth), BF16),
+            pltpu.SemaphoreType.DMA((GATHER_COPIES,)),
+            pltpu.SemaphoreType.DMA((GATHER_COPIES,)),
+            pltpu.SemaphoreType.DMA((6,)),
+            pltpu.SemaphoreType.DMA((4,)),
+        ],
+        compiler_params=pltpu.CompilerParams(
+            collective_id=1, has_side_effects=True, vmem_limit_bytes=16 << 20
+        ),
+        cost_estimate=pl.CostEstimate(flops=0, bytes_accessed=200 << 20, transcendentals=0),
+        name="gather_inputs",
+    )(x, segments, small, w_flipped)
+
+
+PARTS = {
+    "side": {"keep": 2, "got": 2, "lift": 2, "sent": 4, "swapped": 4, "final": 4},
+    "lift": {"keep": 1, "got": 1, "sent": 2, "swapped": 2, "sent_side": 4, "got_side": 4, "final": 4},
+}
+SLOTS = 9
+OUT_ROWS = (64,) * 16
+IN_ROWS = (64,) * 32
+PER_TICK = 3
+TOKEN_PIECES = 16
+
+
+def reduce_chunks(inner, common):
+    pieces = []
+    start = 0
+    for rows in OUT_ROWS:
+        pieces.append(("out", start, rows))
+        start += rows
+    start = 0
+    for rows in IN_ROWS:
+        pieces.append(("in", start, rows))
+        start += rows
+    pieces.insert(len(OUT_ROWS), ("shared", 0, common))
+    counts = {}
+    placed = []
+    for number, (kind, start, rows) in enumerate(pieces):
+        order = "lift" if number % 3 == 2 else "side"
+        key = (kind == "shared", rows, order)
+        where = counts.get(key, 0)
+        counts[key] = where + 1
+        placed.append((kind, start, rows, order, where))
+    return placed, counts
+
+
+def reduce_kernel(plan, in_ref, out_ref, tok_out_ref, tok_grad_ref, small_ref,
+                  sum_in_ref, sum_shared_ref, sum_out_ref, got_out_ref, got_grad_ref, small_sum_ref, *scratch):
+    chunks, counts, inner, depth = plan
+    groups = {}
+    position = 0
+    for key in counts:
+        names = list(PARTS[key[2]])
+        groups[key] = dict(zip(names, scratch[position : position + len(names)]))
+        position += len(names)
+    (shared_in, shared_sum, small_got, send_sems, recv_sems, local_sems, tok_send, tok_recv,
+     small_send, small_recv, shared_send, shared_recv) = scratch[position:]
+    me = lax.axis_index("fsdp")
+    replica = lax.axis_index("replica")
+    up = replica // 2
+    inside = (up == 1) | (up == 2)
+    outside = (up == 0) | (up == 3)
+    half = up // 2
+    aside = replica % 2
+    beside = (flip(replica, 1), me)
+    partner = (flip(replica, 2), me)
+    middle = (flip(flip(replica, 2), 4), me)
+    peers = [(replica, peer) for peer in copy_peers(me)]
+    greet(peers + [beside, partner, middle])
+
+    def remote(from_ref, to_ref, device, sends, recvs):
+        return pltpu.make_async_remote_copy(
+            src_ref=from_ref, dst_ref=to_ref, send_sem=sends, recv_sem=recvs, device_id=device, device_id_type=MESH
+        )
+
+    def lanes_of(device):
+        return pl.ds(pl.multiple_of(device * depth, depth), depth)
+
+    def activations():
+        rows = got_out_ref.shape[0] // TOKEN_PIECES
+        copies = []
+        for piece in range(TOKEN_PIECES):
+            at = pl.ds(piece * rows, rows)
+            for which, (source, target) in enumerate([(tok_out_ref, got_out_ref), (tok_grad_ref, got_grad_ref)]):
+                copy = remote(
+                    source.at[1, at], target.at[at], peers[1], tok_send.at[which, piece], tok_recv.at[which, piece]
+                )
+                copy.start()
+                copies.append(copy)
+            yield
+        for copy in copies:
+            copy.wait()
+
+    def smalls():
+        small_sum_ref[...] = small_ref[...]
+        for level, peer in enumerate([peers[0], peers[1], beside, partner, middle]):
+            copy = remote(small_sum_ref, small_got.at[level], peer, small_send.at[level], small_recv.at[level])
+            copy.start()
+            yield
+            copy.wait()
+            small_sum_ref[...] += small_got[level]
+
+    def run(number, kind, start, rows, order, where):
+        held = {name: ref.at[where] for name, ref in groups[kind == "shared", rows, order].items()}
+        if kind == "in":
+            group = 0 if start >= inner else 4
+            local_start = start % inner
+            source = lambda at, count: in_ref.at[pl.ds(pl.multiple_of(start + at, 16), count)]
+            place = lambda at, count: sum_in_ref.at[pl.ds(group, 4), pl.ds(pl.multiple_of(local_start + at, 16), count)]
+        elif kind == "out":
+            source = lambda at, count: out_ref.at[pl.ds(pl.multiple_of(start + at, 16), count)]
+            place = lambda at, count: sum_out_ref.at[pl.ds(pl.multiple_of(start + at, 16), count)]
         else:
-            source, target = out_ref, sum_out_ref
-            cut = lambda ref, at, count: ref.at[pl.ds(index, 1), pl.ds(at, count)]
-        if group == "shared":
-            place = lambda at, count: target.at[pl.ds(at, count)]
-        else:
-            place = lambda at, count: cut(target, at, count)
-        held = {name: groups[group][name].at[index] for name in STAGES}
-        sizes = [rows >> (level + 1) for level in range(levels)]
-        upper = [(replica // bit) % 2 for bit in order]
-        starts = [0]
-        for level in range(levels):
-            starts.append(pl.multiple_of(starts[-1] + upper[level] * sizes[level], sizes[-1]))
-        sem = 0
-        pending = []
-
-        def send(from_ref, to_ref, device, slot):
-            copy = pltpu.make_async_remote_copy(
-                src_ref=from_ref, dst_ref=to_ref, send_sem=send_sems.at[number, slot],
-                recv_sem=recv_sems.at[number, slot], device_id=device, device_id_type=MESH,
+            source = lambda at, count: shared_sum.at[pl.ds(at, count)]
+            place = lambda at, count: sum_shared_ref.at[pl.ds(at, count)]
+            copies = []
+            for offset in range(3):
+                copy = remote(
+                    in_ref.at[pl.ds(2 * inner, rows), lanes_of(peers[offset][1])],
+                    shared_in.at[offset], peers[offset], shared_send.at[offset], shared_recv.at[offset],
+                )
+                copy.start()
+                copies.append(copy)
+            own = pltpu.make_async_copy(
+                in_ref.at[pl.ds(2 * inner, rows), lanes_of(me)], shared_in.at[3], local_sems.at[number, 1]
             )
-            copy.start()
-            pending.append(copy)
-            return copy
-
-        other = pl.multiple_of((1 - upper[0]) * sizes[0], sizes[0])
-        keep_copy = pltpu.make_async_copy(cut(source, starts[1], sizes[0]), held["keep"], local_sems.at[number, 0])
-        keep_copy.start()
-        copy = send(cut(source, other, sizes[0]), held["got0"], replica_peer(order[0]), 0)
-        yield
-        keep_copy.wait()
-
-        def summed(level, at, count):
+            own.start()
+            yield
+            own.wait()
+            total = shared_in[3].astype(F32)
+            for offset in range(3):
+                copies[offset].wait_recv()
+                total = total + shared_in[offset].astype(F32)
+            shared_sum[...] = total.astype(BF16)
+
+        def link(from_ref, to_ref, device, slot):
+            return remote(from_ref, to_ref, device, send_sems.at[number, slot], recv_sems.at[number, slot])
+
+        def added(names_at, at, count):
             total = None
-            for name, base in [("keep", 1)] + [("got%d" % l, l + 1) for l in range(level)]:
-                local = pl.multiple_of(at - starts[base], count)
-                part = held[name][:, pl.ds(local, count), :].astype(F32)
+            for name, base in names_at:
+                local = pl.multiple_of(at - base, count)
+                part = held[name][pl.ds(local, count), :].astype(F32)
                 total = part if total is None else total + part
             return total
 
-        for level in range(1, levels):
-            copy.wait_recv()
-            there = starts[level] + (1 - upper[level]) * sizes[level]
-            held["sent%d" % level][...] = summed(level, there, sizes[level]).astype(BF16)
-            copy = send(held["sent%d" % level], held["got%d" % level], replica_peer(order[level]), level)
+        two, four = rows // 2, rows // 4
+        if order == "side":
+            mine, other = pl.multiple_of(aside * two, two), pl.multiple_of((1 - aside) * two, two)
+            low, high = pl.multiple_of(mine + half * four, four), pl.multiple_of(mine + (1 - half) * four, four)
+            keep = pltpu.make_async_copy(source(mine, two), held["keep"], local_sems.at[number, 0])
+            keep.start()
+            side = link(source(other, two), held["got"], beside, 0)
+            side.start()
             yield
-        copy.wait_recv()
-        held["final"][...] = summed(levels, starts[levels], sizes[-1]).astype(BF16)
+            keep.wait()
+            side.wait_recv()
+            lift = link(held["lift"], held["lift"], partner, 1)
+
+            @pl.when(outside)
+            def _():
+                held["lift"][...] = added([("keep", mine), ("got", mine)], mine, two).astype(BF16)
+                lift.start()
+
+            yield
+            bases = [("keep", mine), ("got", mine), ("lift", mine)]
+            across = link(held["sent"], held["swapped"], middle, 2)
+
+            @pl.when(inside)
+            def _():
+                lift.wait_recv()
+                held["sent"][...] = added(bases, high, four).astype(BF16)
+                across.start()
+
+            yield
+            bases = bases + [("swapped", low)]
+        else:
+            mine, other = pl.multiple_of(half * two, two), pl.multiple_of((1 - half) * two, two)
+            low, high = pl.multiple_of(mine + aside * four, four), pl.multiple_of(mine + (1 - aside) * four, four)
+            keep = pltpu.make_async_copy(source(0, rows), held["keep"], local_sems.at[number, 0])
+            lift = link(source(0, rows), held["got"], partner, 1)
+
+            @pl.when(outside)
+            def _():
+                lift.start()
+
+            @pl.when(inside)
+            def _():
+                keep.start()
+
+            yield
+            bases = [("keep", 0), ("got", 0)]
+            across = link(held["sent"], held["swapped"], middle, 2)
+
+            @pl.when(inside)
+            def _():
+                keep.wait()
+                lift.wait_recv()
+                held["sent"][...] = added(bases, other, two).astype(BF16)
+                across.start()
+
+            yield
+            bases = bases + [("swapped", mine)]
+            side = link(held["sent_side"], held["got_side"], beside, 0)
+
+            @pl.when(inside)
+            def _():
+                across.wait_recv()
+                held["sent_side"][...] = added(bases, high, four).astype(BF16)
+                side.start()
+
+            yield
+            bases = bases + [("got_side", low)]
+
         final = held["final"]
-        here, count = starts[levels], sizes[-1]
-        slot = levels
-        if group == "out":
-            own = pltpu.make_async_copy(final, place(here, count), local_sems.at[number, 1])
+        trade = []
+        if kind == "in":
+            target = sum_in_ref.at[group + me, pl.ds(pl.multiple_of(local_start + low, 16), four)]
+            trade = [
+                link(final.at[:, lanes_of(peers[offset][1])], target, peers[offset], 3 + offset) for offset in range(3)
+            ]
+            own = pltpu.make_async_copy(final.at[:, lanes_of(me)], target, local_sems.at[number, 1])
+        else:
+            own = pltpu.make_async_copy(final, place(low, four), local_sems.at[number, 1])
+
+        if order == "side":
+            back = [
+                link(place(low, four), place(low, four), middle, 6),
+                link(place(mine, two), place(mine, two), partner, 7),
+                link(place(mine, two), place(mine, two), beside, 8),
+            ]
+        else:
+            back = [
+                link(place(low, four), place(low, four), beside, 6),
+                link(place(mine, two), place(mine, two), middle, 7),
+                link(place(0, rows), place(0, rows), partner, 8),
+            ]
+
+        @pl.when(inside)
+        def _():
+            (across if order == "side" else side).wait_recv()
+            final[...] = added(bases, low, four).astype(BF16)
+            for copy in trade:
+                copy.start()
             own.start()
             own.wait()
+            for copy in trade:
+                copy.wait_recv()
+            back[0].start()
+
+        yield
+
+        @pl.when(inside)
+        def _():
+            back[0].wait_recv()
+            back[1].start()
+            if order == "side":
+                back[2].start()
+
+        yield
+        if order == "side":
+
+            @pl.when(outside)
+            def _():
+                back[1].wait_recv()
+                back[2].start()
+
+            yield
+            back[2].wait_recv()
+            side.wait_send()
+            back[2].wait_send()
+
+            @pl.when(outside)
+            def _():
+                lift.wait_send()
+
+            @pl.when(inside)
+            def _():
+                across.wait_send()
+                for copy in trade + back[:2]:
+                    copy.wait_send()
+
         else:
-            landing = shared_in if group == "shared" else None
-            arrivals = []
-            for offset in range(1, size):
-                peer = copy_peer(offset)
-                if group == "shared":
-                    to_ref = shared_in.at[offset - 1]
-                else:
-                    to_ref = target.at[me, pl.ds(here, count), pl.ds(index * columns, columns)]
-                arrivals.append(send(final.at[peer], to_ref, (replica, peer), slot))
-                slot += 1
-            if group == "shared":
-                yield
-                total = final[me].astype(F32)
-                for offset in range(1, size):
-                    arrivals[offset - 1].wait_recv()
-                    total = total + shared_in[offset - 1].astype(F32)
-                shared_sum[...] = total.astype(BF16)
-                own = pltpu.make_async_copy(shared_sum, place(here, count), local_sems.at[number, 1])
-                own.start()
-                own.wait()
-            else:
-                own = pltpu.make_async_copy(
-                    final.at[me], target.at[me, pl.ds(here, count), pl.ds(index * columns, columns)],
-                    local_sems.at[number, 1],
-                )
-                own.start()
-                yield
-                own.wait()
-                for arrival in arrivals:
-                    arrival.wait_recv()
-        for level in range(levels - 1, -1, -1):
-            region = place(starts[level + 1], sizes[level])
-            copy = send(region, region, replica_peer(order[level]), slot)
-            slot += 1
+
+            @pl.when(inside)
+            def _():
+                back[1].wait_recv()
+                back[2].start()
+
             yield
-            copy.wait_recv()
-        for copy in pending:
-            copy.wait_send()
+
+            @pl.when(outside)
+            def _():
+                back[2].wait_recv()
+                lift.wait_send()
+
+            @pl.when(inside)
+            def _():
+                across.wait_send()
+                side.wait_send()
+                for copy in trade + back:
+                    copy.wait_send()
+
+        if kind == "shared":
+            for copy in copies:
+                copy.wait_send()
 
     waiting = [run(number, *chunk) for number, chunk in enumerate(chunks)]
-    active = []
-    while waiting or active:
-        active += waiting[:PER_TICK]
-        waiting = waiting[PER_TICK:]
+    active, extra = [], [activations(), smalls()]
+
+    def advance(running):
         still = []
-        for steps in active:
+        for steps in running:
             try:
                 next(steps)
                 still.append(steps)
             except StopIteration:
                 pass
-        active = still
-
-
-PER_TICK = 2
-
-
-def reduce_gradients(size, copies, depth, inner, common, grad_in, grad_out):
-    width = grad_out.shape[2]
-    chunks = reduce_chunks(size, copies, depth, inner, common, grad_out.shape[0] * OUT_CHUNK, width)
-    shapes = {"out": (1, OUT_CHUNK, width), "in": (size, depth, COL_CHUNK), "shared": (size, depth, common)}
-    counts = {name: sum(1 for chunk in chunks if chunk[0] == name) for name in shapes}
+        return still
+
+    while waiting or active:
+        active = advance(active + waiting[:PER_TICK])
+        waiting = waiting[PER_TICK:]
+        extra = advance(extra)
+    while extra:
+        extra = advance(extra)
+
+
+def reduce_gradients(size, depth, inner, common, grad_in, grad_out, tok_out, tok_grad, small):
+    width = grad_out.shape[1]
+    chunks, counts = reduce_chunks(inner, common)
     scratch = []
-    for name, (blocks, rows, columns) in shapes.items():
-        fraction = {"keep": 2, "got0": 2, "sent1": 4, "got1": 4, "sent2": 8, "got2": 8, "final": 8}
-        for stage in STAGES:
-            scratch.append(pltpu.VMEM((counts[name], blocks, rows // fraction[stage], columns), BF16))
-    scratch.append(pltpu.VMEM((size - 1, depth // copies, common), BF16))
-    scratch.append(pltpu.VMEM((depth // copies, common), BF16))
-    slots = 2 * len(axis_bits(copies)) + size - 1
-    scratch.append(pltpu.SemaphoreType.DMA((len(chunks), slots)))
-    scratch.append(pltpu.SemaphoreType.DMA((len(chunks), slots)))
-    scratch.append(pltpu.SemaphoreType.DMA((len(chunks), 2)))
+    for (shared, rows, order), count in counts.items():
+        for fraction in PARTS[order].values():
+            scratch.append(pltpu.VMEM((count, rows // fraction, depth if shared else width), BF16))
+    sems = pltpu.SemaphoreType.DMA
+    scratch += [
+        pltpu.VMEM((4, common, depth), BF16),
+        pltpu.VMEM((common, depth), BF16),
+        pltpu.VMEM((5,) + small.shape, F32),
+        sems((len(chunks), SLOTS)), sems((len(chunks), SLOTS)), sems((len(chunks), 2)),
+        sems((2, TOKEN_PIECES)), sems((2, TOKEN_PIECES)), sems((5,)), sems((5,)), sems((3,)), sems((3,)),
+    ]
     anywhere = pl.BlockSpec(memory_space=pl.ANY)
+    local = pl.BlockSpec(memory_space=pltpu.VMEM)
     return pl.pallas_call(
-        functools.partial(reduce_kernel, (size, copies, chunks, shapes)),
-        in_specs=[anywhere] * 2,
-        out_specs=[anywhere] * 3,
+        functools.partial(reduce_kernel, (chunks, counts, inner, depth)),
+        in_specs=[anywhere] * 4 + [local],
+        out_specs=[anywhere] * 5 + [local],
         out_shape=[
-            jax.ShapeDtypeStruct((size, depth, 2 * inner), BF16),
-            jax.ShapeDtypeStruct((depth, common), BF16),
+            jax.ShapeDtypeStruct((2 * size, inner, depth), BF16),
+            jax.ShapeDtypeStruct((common, depth), BF16),
             jax.ShapeDtypeStruct(grad_out.shape, BF16),
+            jax.ShapeDtypeStruct(tok_out.shape[1:], BF16),
+            jax.ShapeDtypeStruct(tok_grad.shape[1:], BF16),
+            jax.ShapeDtypeStruct(small.shape, F32),
         ],
         scratch_shapes=scratch,
         compiler_params=pltpu.CompilerParams(
-            collective_id=0, has_side_effects=True, vmem_limit_bytes=56 << 20
+            collective_id=0, has_side_effects=True, vmem_limit_bytes=58 << 20
         ),
         cost_estimate=pl.CostEstimate(flops=0, bytes_accessed=700 << 20, transcendentals=0),
         name="reduce_gradients",
-    )(grad_in, grad_out)
+    )(grad_in, grad_out, tok_out, tok_grad, small)
 
 
 def small_pieces(size, copies, depth, inner, columns, me, replica, scaled_low, gp, normed_low, cot_all):
@@ -667,6 +954,27 @@
 
     grad_w_in = jnp.concatenate(in_place(gate_parts) + in_place(value_parts) + [shared_part], 1).astype(F32)
     return grad_w_in, grad_w_out
+
+
+def recut(size, full_inner, inner, me, w_in):
+    depth, full = w_in.shape
+
+    def columns_of(device):
+        return jnp.concatenate(
+            [
+                lax.dynamic_slice(w_in, (0, full_inner + device * inner), (depth, inner)),
+                lax.dynamic_slice(w_in, (0, device * inner), (depth, inner)),
+                w_in[:, 2 * full_inner :],
+            ],
+            1,
+        )
+
+    w_cols = jnp.zeros((size * depth, 2 * inner + full - 2 * full_inner), BF16)
+    w_cols = lax.dynamic_update_slice(w_cols, columns_of(me), (me * depth, 0))
+    for offset in range(1, size):
+        received = swap(columns_of(me ^ offset), "fsdp", size, offset)
+        w_cols = lax.dynamic_update_slice(w_cols, received, ((me ^ offset) * depth, 0))
+    return w_cols
 
 
 def on_device(copies, size, hidden_in, segment_ids, cotangent, norm_gain, w_in, conv_weight, conv_bias,
@@ -691,39 +999,36 @@
 
     own_x = hidden_in.reshape(own_rows, width)
     own_cot = cotangent.reshape(own_rows, width)
-    x_all = gather_relative(own_x, "fsdp", size).reshape(total, width)
     small = jnp.concatenate([norm_gain, conv_weight.reshape(-1), conv_bias])
-    small = lax.all_gather(small, "fsdp", axis=0, tiled=False).astype(F32)
+    segments = segment_ids.reshape(micro_count * seq_count, tokens)
+    fused = copies == 8 and size == 4 and sum(OUT_ROWS) == inner and sum(IN_ROWS) == 2 * inner
+    if fused:
+        padded = jnp.pad(small.astype(F32), (0, -small.shape[0] % (8 * LANES))).reshape(-1, LANES)
+        x_all, seg_all, small, w_cols = gather_inputs(
+            size, inner, own_x, segments.reshape(-1, LANES), padded, w_in.T
+        )
+        x_all = x_all.reshape(total, width)
+        small = small.reshape(size, -1)
+        own_cot_later, _ = lax.optimization_barrier((own_cot, seg_all))
+        cot_across = swap(own_cot_later, "fsdp", size, 2)
+    else:
+        small = lax.all_gather(small, "fsdp", axis=0, tiled=False).astype(F32)
+        x_all = gather_relative(own_x, "fsdp", size).reshape(total, width)
+        seg_all = gather_relative(segments, "fsdp", size)
+        w_cols = recut(size, full_inner, inner, me, w_in).T
+        cot_all = gather_relative(own_cot, "fsdp", size).reshape(total, width)
+    seg_all = seg_all.reshape(total // tokens, tokens)
     full_norm = small[:, :depth].reshape(1, width)
     full_cw = small[:, depth : depth + taps * own_conv].reshape(size, taps, own_conv)
     full_cw = full_cw.transpose(1, 0, 2).reshape(taps, conv_width)
-    full_cb = small[:, depth + taps * own_conv :].reshape(1, conv_width)
-    seg_all = gather_relative(segment_ids.reshape(micro_count * seq_count, tokens), "fsdp", size)
-    seg_all = seg_all.reshape(total // tokens, tokens)
-
-    def columns_of(device):
-        return jnp.concatenate(
-            [
-                lax.dynamic_slice(w_in, (0, full_inner + device * inner), (depth, inner)),
-                lax.dynamic_slice(w_in, (0, device * inner), (depth, inner)),
-                w_in[:, 2 * full_inner :],
-            ],
-            1,
-        )
-
-    w_cols = jnp.zeros((size * depth, columns), BF16)
-    w_cols = lax.dynamic_update_slice(w_cols, columns_of(me), (me * depth, 0))
-    for offset in range(1, size):
-        received = swap(columns_of(me ^ offset), "fsdp", size, offset)
-        w_cols = lax.dynamic_update_slice(w_cols, received, ((me ^ offset) * depth, 0))
-    cot_all = gather_relative(own_cot, "fsdp", size).reshape(total, width)
+    full_cb = small[:, depth + taps * own_conv : depth + (taps + 1) * own_conv].reshape(1, conv_width)
 
     def normalise(inputs):
         wide = inputs.astype(F32)
         return lax.rsqrt(jnp.mean(wide * wide, -1, keepdims=True) + EPS)
 
     scaled_low = (x_all.astype(F32) * normalise(x_all) * full_norm).astype(BF16)
-    projected = jnp.dot(scaled_low, w_cols, preferred_element_type=F32)
+    projected = contract_cols(scaled_low, w_cols)
 
     conv_all = jnp.concatenate([full_cw, full_cb, jnp.zeros((7 - taps, conv_width), F32)], 0)
     conv_own = jnp.concatenate(
@@ -744,48 +1049,22 @@
         head_rows, conv_own, chan_rows,
     )
     gated, squares = mix_forward(dims, operands)
+    if fused:
+        cot_across, squares = lax.optimization_barrier((cot_across, squares))
+        pair = jnp.stack([own_cot, cot_across])
+        cot_all = jnp.concatenate([pair, swap(pair, "fsdp", size, 1)], 0).reshape(total, width)
     grad_normed = contract_cols(cot_all, w_out)
     cross = jnp.sum(gated.astype(F32) * grad_normed, 1)
     stats = sum_tokens(jnp.stack([squares[:, 0], cross]), "fsdp", size)
     root = lax.rsqrt(stats[0] / full_inner + EPS)
     pull = root * root * root * stats[1] / full_inner
 
-    out_part = jnp.dot(gated, w_out, preferred_element_type=F32).astype(BF16)
-    out_sum = scatter_relative(out_part.reshape(size, own_rows, width), "fsdp", size)
-    block_out = (own_x.astype(F32) + root[:own_rows, None] * out_sum).astype(BF16)
-    block_out = block_out.reshape(hidden_in.shape)
-
     normed_low = (gated.astype(F32) * root[:, None]).astype(BF16)
     gp, grad_conv, grad_chan, grad_head = mix_backward(
         dims, operands, jnp.stack([root, pull], 1), grad_normed
     )
-
-    full_levels = copies == 8 and depth % (16 * copies) == 0 and inner % COL_CHUNK == 0
-    if full_levels:
-        grad_out = contract_rows(normed_low, cot_all).astype(BF16)
-        grad_cols = contract_rows(scaled_low, gp).astype(BF16)
-        sum_in, sum_shared, sum_out = reduce_gradients(
-            size, copies, depth, inner, common,
-            grad_cols.reshape(size, depth, columns), grad_out.reshape(inner // OUT_CHUNK, OUT_CHUNK, width),
-        )
-        grad_w_out = sum_out.reshape(inner, width).astype(F32)
-        by_kind = [sum_in[device, :, inner:] for device in range(size)]
-        by_kind += [sum_in[device, :, :inner] for device in range(size)]
-        grad_w_in = jnp.concatenate(by_kind + [sum_shared], 1).astype(F32)
-    else:
-        grad_w_in, grad_w_out = small_pieces(
-            size, copies, depth, inner, columns, me, replica, scaled_low, gp, normed_low, cot_all
-        )
-
-    scaled_part = contract_cols(gp, w_cols).astype(BF16)
-    grad_scaled = scatter_relative(scaled_part.reshape(size, own_rows, width), "fsdp", size)
     own_wide = own_x.astype(F32)
     own_root = normalise(own_x)
-    gained = grad_scaled * full_norm
-    inner_mean = jnp.mean(gained * own_wide, -1, keepdims=True)
-    grad_in = own_cot.astype(F32) + own_root * gained - own_wide * (own_root * own_root * own_root * inner_mean)
-    grad_in = grad_in.reshape(hidden_in.shape)
-    grad_norm = jnp.sum(grad_scaled * own_wide * own_root, 0)
 
     conv_full = jnp.zeros((8, conv_width), F32)
     conv_full = lax.dynamic_update_slice(conv_full, grad_conv[:, inner:], (0, full_inner))
@@ -795,8 +1074,56 @@
     own_small = jnp.concatenate(
         [grad_head[0, :local_heads], grad_head[1, :local_heads], skip_grad, grad_chan[1]]
     )
-    conv_full, grad_norm = lax.psum((conv_full, grad_norm), ("replica", "fsdp"))
-    own_small = lax.psum(own_small, "replica")
+
+    if fused:
+        near = total // 2
+
+        def halves(product):
+            sent = swap(product(near, total).astype(BF16), "fsdp", size, 1)
+            kept = product(0, near) + sent.astype(F32)
+            return kept.astype(BF16).reshape(2, own_rows, width)
+
+        tok_out = halves(lambda start, stop: jnp.dot(gated[start:stop], w_out, preferred_element_type=F32))
+        far_grad = jnp.dot(gp[near:], w_cols, preferred_element_type=F32).astype(BF16)
+        near_grad = jnp.dot(gp[:near], w_cols, preferred_element_type=F32).astype(BF16)
+        tok_grad = (near_grad.astype(F32) + swap(far_grad, "fsdp", size, 1).astype(F32)).astype(BF16)
+        tok_grad = tok_grad.reshape(2, own_rows, width)
+        scaled_part = jnp.concatenate([near_grad, far_grad], 0)
+        grad_norm = jnp.sum(scaled_part.astype(F32) * x_all.astype(F32) * normalise(x_all), 0)
+        grad_out = contract_rows(normed_low, cot_all).astype(BF16)
+        grad_cols = contract_rows(gp, scaled_low).astype(BF16)
+        spread = lax.dynamic_update_slice(jnp.zeros((size, own_small.shape[0]), F32), own_small[None], (me, 0))
+        vector = jnp.concatenate([conv_full, grad_norm, spread.reshape(-1)])
+        vector = jnp.pad(vector, (0, -vector.shape[0] % (8 * LANES))).reshape(-1, LANES)
+        sum_in, sum_shared, sum_out, got_out, got_grad, vector = reduce_gradients(
+            size, depth, inner, common, grad_cols, grad_out, tok_out, tok_grad, vector
+        )
+        grad_w_out = sum_out.astype(F32)
+        grad_w_in = jnp.concatenate([sum_in.reshape(2 * full_inner, depth), sum_shared], 0).astype(F32).T
+        out_sum = tok_out[0].astype(F32) + got_out.astype(F32)
+        grad_scaled = tok_grad[0].astype(F32) + got_grad.astype(F32)
+        vector = vector.reshape(-1)
+        conv_full = vector[: conv_full.shape[0]]
+        grad_norm = vector[conv_full.shape[0] : conv_full.shape[0] + width]
+        start = conv_full.shape[0] + width
+        own_small = lax.dynamic_slice(vector, (start + me * own_small.shape[0],), own_small.shape)
+    else:
+        out_part = jnp.dot(gated, w_out, preferred_element_type=F32).astype(BF16)
+        out_sum = scatter_relative(out_part.reshape(size, own_rows, width), "fsdp", size)
+        grad_w_in, grad_w_out = small_pieces(
+            size, copies, depth, inner, columns, me, replica, scaled_low, gp, normed_low, cot_all
+        )
+        scaled_part = jnp.dot(gp, w_cols, preferred_element_type=F32).astype(BF16)
+        grad_scaled = scatter_relative(scaled_part.reshape(size, own_rows, width), "fsdp", size)
+        grad_norm = jnp.sum(grad_scaled * own_wide * own_root, 0)
+        conv_full, grad_norm = lax.psum((conv_full, grad_norm), ("replica", "fsdp"))
+        own_small = lax.psum(own_small, "replica")
+
+    block_out = (own_wide + root[:own_rows, None] * out_sum).astype(BF16).reshape(hidden_in.shape)
+    gained = grad_scaled * full_norm
+    inner_mean = jnp.mean(gained * own_wide, -1, keepdims=True)
+    grad_in = own_cot.astype(F32) + own_root * gained - own_wide * (own_root * own_root * own_root * inner_mean)
+    grad_in = grad_in.reshape(hidden_in.shape)
     conv_full = lax.dynamic_slice(conv_full.reshape(taps + 1, conv_width), (0, me * own_conv), (taps + 1, own_conv))
     grad_norm = lax.dynamic_slice(grad_norm, (me * depth,), (depth,))
     return (

time: 1040 us -> 729 us (0.70)
  blocking collectives: 198 us -> 0 us
  waiting for transfers between devices: 67.1 us -> 0.84 us
  local copies, waits for them, and re-layouts: 95.1 us -> 28.9 us
  Pallas kernels: 466 us -> 486 us
  between operations: 15.6 us -> 1.64 us
  matrix products: 119 us -> 130 us
    unnamed x1 -> x0, blocking collectives: 134 us -> none
    ppermute x15 -> x6, waiting for transfers between devices: 67.1 us -> 0.84 us  [swap(): return lax.ppermute(array, axis, [(i, i ^ bit) for i in range(size)])]
    psum x2 -> x0, blocking collectives: 64.6 us -> none  [the longest x1 42.8 us: on_device(): conv_full, grad_norm = lax.psum((conv_full, grad_norm), ('replica', 'fsdp'))]
    unnamed x81 -> x64, local copies, waits for them, and re-layouts: 37.5 us -> 16.9 us
    pallas_call x1 -> x2, Pallas kernels: 346 us -> 364 us  [the longest x1 284 us: reduce_gradients(): pl.pallas_call(functools.partial(reduce_kernel, (chunks, counts, inner, d...]
    transpose x0 -> x1, other arithmetic: none -> 14.8 us  [on_device(): jnp.concatenate([sum_in.reshape(2 * full_inner, depth), sum_shared], 0)]
    slice x7 -> x3, local copies, waits for them, and re-layouts: 15.9 us -> 1.61 us  [the longest x1 0.9 us: on_device(): conv_full = vector[:conv_full.shape[0]]]
    add x3 -> x0, other arithmetic: 13.8 us -> none  [scatter_relative(): total = total[:half].astype(F32) + received.astype(F32)]
  transfers between devices with their start and end apart: 16 -> 6, of which waited for: 3 -> 1; matrix products, arithmetic and copies ran while one was open for 23% -> 15% of each run, Pallas kernels for 45% -> 6%
where the time goes in v2:
time: 729 us; the launch traced here: 721 us
  Pallas kernels  486 us (67%)
  matrix products  130 us (18%)
  other arithmetic  70 us (10%)
  local copies, waits for them, and re-layouts  28.9 us (4%)
    pallas_call x1, Pallas kernels, reduce_gradients(): pl.pallas_call(functools.partial(reduce_kernel, (chunks, counts, inner, d...  284 us
    pallas_call x1, Pallas kernels, gather_inputs(): pl.pallas_call(functools.partial(gather_kernel, full_inner, inner), in_sp...  80.9 us
    pallas_call x1, Pallas kernels, mix_backward(): pl.pallas_call(functools.partial(backward_kernel, dims), grid=(total // t...  79.8 us
    dot_general x2, matrix products, contract_rows(): lax.dot_general(left, right, (((0,), (0,)), ((), ())), precision=precisio...  41.5 us
    pallas_call x1, Pallas kernels, mix_forward(): pl.pallas_call(functools.partial(forward_kernel, dims), grid=(total // to...  41.5 us
    dot_general x2, matrix products, contract_cols(): lax.dot_general(left, right, (((1,), (1,)), ((), ())), precision=precisio...  40.2 us
    dot_general x1, matrix products, on_device(): jnp.dot(gp[:near], w_cols, preferred_element_type=F32).astype(BF16)  17 us
    unnamed x64, local copies, waits for them, and re-layouts  16.9 us
  transfers between devices with their start and end apart: 6, of which 1 were waited for; matrix products, arithmetic and copies ran while one was open for 15% of the time, Pallas kernels for 6%

profile of v2, /device:TPU:0, one launch (start us, length us, event | category | flops | bytes accessed | tf_op | source)
XLA Modules:
  0.0 720.5 jit_solution(14251826077368884294)
XLA Ops:
  2.2 1.6 copy-done.1
  3.7 3.5 copy-done.3
  7.9 80.9 %gather_inputs.1 = (bf16[4,512,2048]{2,1,0:T(8,128)(2,1)S(1)}, s32[4,4,128]{2,1,0:T(4,128)S(1)}, f32[4,48,128]{2,1,0:T(8,128)S(1)}, bf16[2368,2048]{1,0:T(8,128)(2,1)S(1)}) custom-call(bf16[512,2048]{1,0:T(8,128)(2,1)S(1)} %bitcast.106, s32[4,128]{1,0:T(4,128)S(1)} %bitcast.111, f32[48,128]{1,0:T(8,128)S(1)} %fusion.37.small_ref, bf16[8512,512]{1,0:T(8,128)(2,1)S(1)} %bitcast.107), custom_call_target="tpu_custom_call" | custom-call | bytes 209715200 | tf_op jit(solution)/shard_map/gather_inputs/pallas_call | solution.py:535
  88.8 3.4 copy-done
  92.2 3.6 copy-done.9
  98.1 5.2 multiply_reduce_fusion
  104.5 8.7 %fusion.3 = bf16[2048,2048]{1,0:T(8,128)(2,1)} fusion(bf16[4,512,2048]{2,1,0:T(8,128)(2,1)} %copy-done, f32[2048]{0:T(1024)S(1)} %bitcast.126, f32[2048]{0:T(1024)S(1)} %bitcast.140), kind=kLoop, calls=%fused_computation.6 | loop fusion | flops 16777216 | bytes 16793600 | tf_op jit(solution)/shard_map/convert_element_type | solution.py:1030
  113.2 28.7 %fusion.48.proj_ref = f32[2048,2368]{1,0:T(8,128)} fusion(bf16[2048,2048]{1,0:T(8,128)(2,1)} %fusion.3, bf16[2368,2048]{1,0:T(8,128)(2,1)} %copy-done.9), kind=kOutput, calls=%fused_computation.96 | convolution fusion | flops 19864223744 | bytes 37486592 | tf_op jit(solution)/shard_map/dot_general | solution.py:25
  143.0 41.5 %mix_forward.1 = (bf16[2048,1024]{1,0:T(8,128)(2,1)}, f32[2048,1]{1,0:T(8,128)S(1)}) custom-call(s32[1]{0:T(128)} %bitcast.5.own_ref, f32[2048,2368]{1,0:T(8,128)} %fusion.48.proj_ref, s32[8,256,1]{2,1,0:T(8,128)S(1)} %broadcast_in_dim_reshape.8.seg_col_ref, s32[8,1,256]{2,1,0:T(1,128)S(1)} %bitcast.109, f32[8,256,8]{2,1,0:T(8,128)S(1)} %pad_convert_fusion.mask_ref, ...), custom_call_target="tpu_custom_call" | custom-call | flops 2147483648 | bytes 19398656 | tf_op jit(solution)/shard_map/mix_forward/pallas_call | solution.py:292
  184.5 5.2 pad_maximum_fusion.2
  189.8 1.3 copy-done.23
  191.1 6.0 convolution_convert_fusion.1
  197.7 1.6 reduce.4
  199.3 5.6 pad_maximum_fusion
  205.3 11.5 %fusion.4 = (f32[2048]{0:T(1024)S(1)}, f32[2048,1024]{1,0:T(8,128)}) fusion(bf16[2048,1024]{1,0:T(8,128)(2,1)S(1)} %copy-done.24, bf16[2048,2048]{1,0:T(8,128)(2,1)S(1)} %bitcast.115, bf16[1024,2048]{1,0:T(8,128)(2,1)S(1)} %copy-done.22), kind=kOutput, calls=%fused_computation.11 | convolution fusion | flops 8596224000 | bytes 25174016 | tf_op jit(solution)/shard_map/dot_general | solution.py:25
  219.9 10.5 %add_convert_fusion.1 = bf16[1024,2048]{1,0:T(8,128)(2,1)} fusion(bf16[1024,2048]{1,0:T(8,128)(2,1)} %collective-permute-done.4, bf16[1024,2048]{1,0:T(8,128)(2,1)} %param.23, bf16[2048,1024]{1,0:T(8,128)(2,1)} %get-tuple-element.37), kind=kOutput, calls=%fused_computation.16 | convolution fusion | flops 4301258752 | bytes 14680064 | tf_op jit(solution)/shard_map/dot_general | solution.py:1086
  230.8 14.4 %fusion.22.out_ref = bf16[1024,2048]{1,0:T(8,128)(2,1)} fusion(bf16[2048,2048]{1,0:T(8,128)(2,1)} %bitcast.116, bf16[2048,1024]{1,0:T(8,128)(2,1)} %get-tuple-element.37, f32[2048]{0:T(1024)S(1)} %bitcast.138), kind=kOutput, calls=%fused_computation.35 | convolution fusion | flops 8598323200 | bytes 16785408 | tf_op jit(solution)/shard_map/dot_general | solution.py:19
  245.2 1.3 copy.88.stats_ref
  246.5 1.2 copy-done.5
  247.7 1.2 copy-done.7
  249.0 79.8 %mix_backward.1 = (bf16[2048,2368]{1,0:T(8,128)(2,1)}, f32[8,1280]{1,0:T(8,128)S(1)}, f32[8,1024]{1,0:T(8,128)S(1)}, f32[8,128]{1,0:T(8,128)S(1)}) custom-call(s32[1]{0:T(128)} %bitcast.5.own_ref, f32[2048,2368]{1,0:T(8,128)} %fusion.48.proj_ref, s32[8,256,1]{2,1,0:T(8,128)S(1)} %copy-done.5, s32[8,1,256]{2,1,0:T(1,128)S(1)} %bitcast.110, ...), custom_call_target="tpu_custom_call" | custom-call | flops 6442450944 | bytes 29097984 | tf_op jit(solution)/shard_map/mix_backward/pallas_call | solution.py:320
  329.3 15.2 %fusion.19 = bf16[1024,2048]{1,0:T(8,128)(2,1)S(1)} fusion(bf16[2368,2048]{1,0:T(8,128)(2,1)} %copy-done.9, bf16[2048,2368]{1,0:T(8,128)(2,1)} %get-tuple-element.39), kind=kOutput, calls=%fused_computation.33 | convolution fusion | flops 9934209024 | bytes 18874368 | tf_op jit(solution)/shard_map/dot_general | solution.py:1087
  344.7 27.1 %convolution_convert_fusion.in_ref = bf16[2368,2048]{1,0:T(8,128)(2,1)} fusion(bf16[2048,2368]{1,0:T(8,128)(2,1)} %get-tuple-element.39, bf16[2048,2048]{1,0:T(8,128)(2,1)} %fusion.3), kind=kOutput, calls=%fused_computation.8 | convolution fusion | flops 19869073408 | bytes 27787264 | tf_op jit(solution)/shard_map/dot_general | solution.py:19
  371.8 17.0 %add_convert_fusion = (bf16[1024,2048]{1,0:T(8,128)(2,1)}, bf16[1024,2048]{1,0:T(8,128)(2,1)S(1)}) fusion(bf16[1024,2048]{1,0:T(8,128)(2,1)} %collective-permute-done.5, bf16[2368,2048]{1,0:T(8,128)(2,1)} %copy-done.9, bf16[2048,2368]{1,0:T(8,128)(2,1)} %get-tuple-element.39), kind=kOutput, calls=%fused_computation.15 | convolution fusion | flops 9942597632 | bytes 27262976 | tf_op jit(solution)/shard_map/dot_general | solution.py:1088
  388.8 9.6 %fusion.1 = f32[2048]{0:T(1024)S(1)} fusion(bf16[4,512,2048]{2,1,0:T(8,128)(2,1)S(1)} %bitcast.105, f32[4,512]{1,0:T(4,128)S(1)} %copy-done.18, bf16[1024,2048]{1,0:T(8,128)(2,1)S(1)} %fusion.19, bf16[1024,2048]{1,0:T(8,128)(2,1)S(1)} %get-tuple-element.120), kind=kLoop, calls=%fused_computation.3 | loop fusion | flops 37746688 | bytes 16793600 | tf_op jit(solution)/shard_map/reduce_sum | solution.py:1092
  399.1 283.6 %reduce_gradients.1 = (bf16[8,1024,512]{2,1,0:T(8,128)(2,1)}, bf16[320,512]{1,0:T(8,128)(2,1)}, bf16[1024,2048]{1,0:T(8,128)(2,1)}, bf16[512,2048]{1,0:T(8,128)(...) custom-call(bf16[2368,2048]{1,0:T(8,128)(2,1)} %convolution_convert_fusion.in_ref, ...), custom_call_target="tpu_custom_call" | custom-call | bytes 734003200 | tf_op jit(solution)/shard_map/reduce_gradients/pallas_call | solution.py:893
  684.3 3.2 fusion.11
  688.9 6.7 convert_element_type.148
  695.6 1.4 dynamic-slice.5
  697.0 1.4 fusion.46
  699.1 14.8 %convert_bitcast_fusion = f32[512,8512]{0,1:T(8,128)} fusion(bf16[320,512]{1,0:T(8,128)(2,1)S(1)} %copy-done.15, bf16[8192,512]{1,0:T(8,128)(2,1)} %bitcast.114), kind=kLoop, calls=%fused_computation | loop fusion | flops 17432576 | bytes 26148864 | tf_op jit(solution)/shard_map/transpose | solution.py:1102
  713.8 6.3 fusion.12
  (137 shorter events, 16.0 us)
Async XLA Ops:
  2.1 1.6 copy-start.1
  3.7 3.5 copy-start.3
  7.9 90.0 %copy-start.19 = (bf16[1024]{0:T(1024)(128)(2,1)S(1)}, bf16[1024]{0:T(1024)(128)(2,1)}, u32[]{:S(2)}) copy-start(bf16[1024]{0:T(1024)(128)(2,1)} %param.22) | copy-start | bytes 6148
  7.9 90.0 %copy-start.20 = (bf16[16]{0:T(256)(128)(2,1)S(1)}, bf16[16]{0:T(256)(128)(2,1)}, u32[]{:S(2)}) copy-start(bf16[16]{0:T(256)(128)(2,1)} %param.21) | copy-start | bytes 100
  88.8 3.4 copy-start
  92.2 3.7 copy-start.9
  95.9 88.6 %collective-permute-start = (bf16[512,2048]{1,0:T(8,128)(2,1)}, bf16[512,2048]{1,0:T(8,128)(2,1)}, u32[]{:S(2)}, u32[]{:S(2)}) collective-permute-start(bf16[512,2048]{1,0:T(8,128)(2,1)} %bitcast.1), channel_id=1, source_target_pairs={{0,2},{1,3},{2,0},{3,1},{4,6},{5,7},{6,4},{7,5},{8,10},{9,11},{10,... | collective-permute-start | bytes 6291464 | tf_op jit(solution)/shard_map/ppermute | solution.py:356
  97.9 45.1 %copy-start.4 = (s32[8,256,1]{2,1,0:T(8,128)}, s32[8,256,1]{2,1,0:T(8,128)S(1)}, u32[]{:S(2)}) copy-start(s32[8,256,1]{2,1,0:T(8,128)S(1)} %broadcast_in_dim_reshape.8.seg_col_ref) | copy-start | bytes 24580
  98.1 6.4 copy-start.16
  113.2 29.5 %copy-start.25 = (bf16[16]{0:T(256)(128)(2,1)S(1)}, bf16[16]{0:T(256)(128)(2,1)}, u32[]{:S(2)}) copy-start(bf16[16]{0:T(256)(128)(2,1)} %param.19) | copy-start | bytes 100
  113.2 29.6 %copy-start.26 = (bf16[16]{0:T(256)(128)(2,1)S(1)}, bf16[16]{0:T(256)(128)(2,1)}, u32[]{:S(2)}) copy-start(bf16[16]{0:T(256)(128)(2,1)} %param.20) | copy-start | bytes 100
  184.4 5.2 copy-start.6
  184.4 5.3 copy-start.21
  184.5 6.6 copy-start.23
  189.6 9.7 %collective-permute-start.1 = (bf16[2,512,2048]{2,1,0:T(8,128)(2,1)}, bf16[2,512,2048]{2,1,0:T(8,128)(2,1)}, u32[]{:S(2)}, u32[]{:S(2)}) collective-permute-start(bf16[2,512,2048]{2,1,0:T(8,128)(2,1)} %pad_maximum_fusion.2), channel_id=1, source_target_pairs={{0,1},{1,0},{2,3},{3,2},{4,5},{5,4},{6,7},{7,6},{8,9},{9,8},{10,11... | collective-permute-start | bytes 12582920 | tf_op jit(solution)/shard_map/ppermute | solution.py:356
  191.1 6.2 copy-start.2
  197.1 22.8 %collective-permute-start.4 = (bf16[1024,2048]{1,0:T(8,128)(2,1)}, bf16[1024,2048]{1,0:T(8,128)(2,1)}, u32[]{:S(2)}, u32[]{:S(2)}) collective-permute-start(bf16[1024,2048]{1,0:T(8,128)(2,1)} %convolution_convert_fusion.1), channel_id=1, source_target_pairs={{0,1},{1,0},{2,3},{3,2},{4,5},{5,4},{6,7},{7,6},{8,9},{9,8},{10,11... | collective-permute-start | bytes 12582920 | tf_op jit(solution)/shard_map/ppermute | solution.py:356
  199.3 5.7 copy-start.22
  199.3 6.0 copy-start.24
  205.0 11.8 %copy-start.13 = (bf16[4,512,2048]{2,1,0:T(8,128)(2,1)}, bf16[4,512,2048]{2,1,0:T(8,128)(2,1)S(1)}, u32[]{:S(2)}) copy-start(bf16[4,512,2048]{2,1,0:T(8,128)(2,1)S(1)} %pad_maximum_fusion) | copy-start | bytes 25165828
  216.8 1.3 collective-permute-start.2
  218.8 11.6 %collective-permute-start.3 = (f32[2,2048]{1,0:T(2,128)S(1)}, f32[2,2048]{1,0:T(2,128)S(1)}, u32[]{:S(2)}, u32[]{:S(2)}) collective-permute-start(f32[2,2048]{1,0:T(2,128)S(1)} %fusion.44), channel_id=1, source_target_pairs={{0,2},{1,3},{2,0},{3,1},{4,6},{5,7},{6,4},{7,5},{8,10},{9,11},{10,... | collective-permute-start | bytes 49160 | tf_op jit(solution)/shard_map/ppermute | solution.py:356
  329.3 59.5 %slice-start = ((s8[8388608]{0:T(1024)(128)(4,1)}), s8[4194304]{0:T(1024)(128)(4,1)S(1)}, s32[]{:S(2)}) async-start(s8[8388608]{0:T(1024)(128)(4,1)} %bitcast.104), calls=%async_computation | async-start | bytes 8388608
  344.5 44.3 %slice-start.1 = ((s8[8388608]{0:T(1024)(128)(4,1)}), s8[4194304]{0:T(1024)(128)(4,1)S(1)}, s32[]{:S(2)}) async-start(s8[8388608]{0:T(1024)(128)(4,1)} %bitcast.104), calls=%async_computation.1 | async-start | bytes 8388608
  344.5 27.3 %collective-permute-start.5 = (bf16[1024,2048]{1,0:T(8,128)(2,1)S(1)}, bf16[1024,2048]{1,0:T(8,128)(2,1)}, u32[]{:S(2)}, u32[]{:S(2)}) collective-permute-start(bf16[1024,2048]{1,0:T(8,128)(2,1)S(1)} %fusion.19), channel_id=1, source_target_pairs={{0,1},{1,0},{2,3},{3,2},{4,5},{5,4},{6,7},{7,6},{8,9},{9,8},{10,11... | collective-permute-start | bytes 12582920 | tf_op jit(solution)/shard_map/ppermute | solution.py:356
  371.8 17.0 %copy-start.18 = (f32[4,512]{1,0:T(4,128)S(1)}, f32[4,512]{1,0:T(4,128)}, u32[]{:S(2)}) copy-start(f32[4,512]{1,0:T(4,128)} %get-tuple-element.113) | copy-start | bytes 24580
  399.1 285.2 %copy-start.17 = (f32[1,4,4,128]{3,1,2,0:T(4,128)S(1)}, f32[1,4,4,128]{3,1,2,0:T(4,128)}, u32[]{:S(2)}) copy-start(f32[1,4,4,128]{3,1,2,0:T(4,128)} %copy-done.16) | copy-start | bytes 24580
  688.9 10.1 %copy-start.15 = (bf16[320,512]{1,0:T(8,128)(2,1)S(1)}, bf16[320,512]{1,0:T(8,128)(2,1)}, u32[]{:S(2)}) copy-start(bf16[320,512]{1,0:T(8,128)(2,1)} %get-tuple-element.47) | copy-start | bytes 983044
  699.0 14.8 %copy-start.10 = (bf16[1024,2048]{1,0:T(8,128)(2,1)S(1)}, bf16[1024,2048]{1,0:T(8,128)(2,1)}, u32[]{:S(2)}) copy-start(bf16[1024,2048]{1,0:T(8,128)(2,1)} %get-tuple-element.119) | copy-start | bytes 12582916
  699.0 14.8 %copy-start.11 = (bf16[1024,2048]{1,0:T(8,128)(2,1)S(1)}, bf16[1024,2048]{1,0:T(8,128)(2,1)}, u32[]{:S(2)}) copy-start(bf16[1024,2048]{1,0:T(8,128)(2,1)} %add_convert_fusion.1) | copy-start | bytes 12582916
  699.0 14.8 %copy-start.12 = (bf16[512,2048]{1,0:T(8,128)(2,1)S(1)}, bf16[512,2048]{1,0:T(8,128)(2,1)}, u32[]{:S(2)}) copy-start(bf16[512,2048]{1,0:T(8,128)(2,1)} %get-tuple-element.44) | copy-start | bytes 6291460
  699.0 14.8 %copy-start.14 = (bf16[512,2048]{1,0:T(8,128)(2,1)S(1)}, bf16[512,2048]{1,0:T(8,128)(2,1)}, u32[]{:S(2)}) copy-start(bf16[512,2048]{1,0:T(8,128)(2,1)} %get-tuple-element.43) | copy-start | bytes 6291460
  (3 other events, 3.1 us)

commit v3 on v2

--- a/solution.py
+++ b/solution.py
@@ -28,7 +28,7 @@
 
 
 def sigmoid(v):
-    return 1.0 / (1.0 + jnp.exp(-v))
+    return 0.5 * jnp.tanh(0.5 * v) + 0.5
 
 
 def convolve(conv_input, taps, bias, mask_refs):
@@ -82,6 +82,17 @@
     return raw, step, log_decay, rows, cols
 
 
+def over_pairs(count, step, carry):
+    group = 4 if count % 4 == 0 else 2
+
+    def turn(index, carried):
+        for inner in range(group):
+            carried = step(index * group + inner, carried)
+        return carried
+
+    return lax.fori_loop(0, count // group, turn, carry)
+
+
 def forward_kernel(dims, own_ref, proj_ref, seg_col_ref, seg_row_ref, mask_ref, head_ref, cw_ref, chan_ref,
                    gated_ref, square_ref,
                    mask_wide, visible_bias, step_wide, cum_wide, cum_rows, state_act, affinity):
@@ -122,7 +133,7 @@
         gated_ref[:, here] = (gated * chan_ref[1:2, here]).astype(BF16)
         return squares + gated * gated
 
-    squares = lax.fori_loop(0, local_heads // 2, pair_step, jnp.zeros((tokens, LANES), F32))
+    squares = over_pairs(local_heads // 2, pair_step, jnp.zeros((tokens, LANES), F32))
     square_ref[...] = jnp.sum(squares, 1, keepdims=True)
 
 
@@ -228,7 +239,7 @@
         gp_ref[:, here] = conv_back(grad_conv, shifted, conv_input, here).astype(BF16)
         return carry
 
-    lax.fori_loop(0, local_heads // 2, pair_step, 0)
+    over_pairs(local_heads // 2, pair_step, 0)
 
     common = 2 * inner
     grad_states = [
@@ -559,27 +570,26 @@
 
 
 PARTS = {
-    "side": {"keep": 2, "got": 2, "lift": 2, "sent": 4, "swapped": 4, "final": 4},
-    "lift": {"keep": 1, "got": 1, "sent": 2, "swapped": 2, "sent_side": 4, "got_side": 4, "final": 4},
+    "side": {"got": 2, "lift": 2, "sent": 4, "swapped": 4, "final": 4},
+    "lift": {"got": 1, "sent": 2, "swapped": 2, "sent_side": 4, "got_side": 4, "final": 4},
 }
 SLOTS = 9
-OUT_ROWS = (64,) * 16
 IN_ROWS = (64,) * 32
-PER_TICK = 3
-TOKEN_PIECES = 16
+SHARED_AT = 4
+COLUMN_BLOCK = 256
+ROW_BLOCK = 256
+LANE_TILE = 256
+PER_TURN = 3
+TOKEN_PIECES = 8
 
 
 def reduce_chunks(inner, common):
     pieces = []
-    start = 0
-    for rows in OUT_ROWS:
-        pieces.append(("out", start, rows))
-        start += rows
     start = 0
     for rows in IN_ROWS:
         pieces.append(("in", start, rows))
         start += rows
-    pieces.insert(len(OUT_ROWS), ("shared", 0, common))
+    pieces.insert(SHARED_AT, ("shared", 0, common))
     counts = {}
     placed = []
     for number, (kind, start, rows) in enumerate(pieces):
@@ -591,17 +601,74 @@
     return placed, counts
 
 
-def reduce_kernel(plan, in_ref, out_ref, tok_out_ref, tok_grad_ref, small_ref,
-                  sum_in_ref, sum_shared_ref, sum_out_ref, got_out_ref, got_grad_ref, small_sum_ref, *scratch):
-    chunks, counts, inner, depth = plan
+def reduce_kernel(plan, gp_ref, scaled_ref, cols_ref, tok_out_ref, small_ref,
+                  sum_in_ref, sum_shared_ref, got_out_ref, own_grad_ref, got_grad_ref, small_sum_ref,
+                  far_land_ref, across_ref, *scratch):
+    chunks, counts, inner, depth, common, norm_row = plan
     groups = {}
     position = 0
     for key in counts:
         names = list(PARTS[key[2]])
         groups[key] = dict(zip(names, scratch[position : position + len(names)]))
         position += len(names)
-    (shared_in, shared_sum, small_got, send_sems, recv_sems, local_sems, tok_send, tok_recv,
-     small_send, small_recv, shared_send, shared_recv) = scratch[position:]
+    (shared_in, shared_sum, small_got, scaled, cols, grads, gp_cols, gp_flipped, gp_rows, tiles, far_tile, norm_sum,
+     send_sems, recv_sems, local_sems, tok_send, tok_recv,
+     small_send, small_recv, shared_send, shared_recv, far_send, far_recv, load_sems, store_sems) = scratch[position:]
+    whole_loads = [
+        pltpu.make_async_copy(scaled_ref, scaled, load_sems.at[0]),
+        pltpu.make_async_copy(cols_ref, cols, load_sems.at[1]),
+    ]
+    for copy in whole_loads:
+        copy.start()
+    loaded = [False, False]
+
+    def need(which):
+        if not loaded[which]:
+            whole_loads[which].wait()
+            loaded[which] = True
+
+    column_blocks = [(start, COLUMN_BLOCK) for start in range(0, 2 * inner, COLUMN_BLOCK)]
+    column_blocks.insert(1, (2 * inner, common))
+    width = scaled.shape[1]
+    rows_of_block = tiles.shape[1]
+    lane_tiles = width // LANE_TILE
+    column_loads = []
+    columns_done = []
+
+    def load_columns(number):
+        if number < len(column_blocks):
+            start, count = column_blocks[number]
+            copy = pltpu.make_async_copy(
+                gp_ref.at[:, pl.ds(start, count)], gp_cols.at[:, pl.ds(0, count)], load_sems.at[2]
+            )
+            copy.start()
+            column_loads.append(copy)
+
+    def next_columns():
+        number = len(columns_done)
+        if number == len(column_blocks):
+            return
+        start, count = column_blocks[number]
+        need(0)
+        column_loads[number].wait()
+        gp_flipped[pl.ds(0, count), :] = gp_cols[:, pl.ds(0, count)].T
+        load_columns(number + 1)
+
+        def lanes_step(tile, carry):
+            lanes = pl.ds(pl.multiple_of(tile * LANE_TILE, LANE_TILE), LANE_TILE)
+            grads[pl.ds(start, count), lanes] = jnp.dot(
+                gp_flipped[pl.ds(0, count), :], scaled[:, lanes], preferred_element_type=F32
+            ).astype(BF16)
+            return carry
+
+        lax.fori_loop(0, lane_tiles, lanes_step, 0)
+        columns_done.append(start)
+
+    def ensure_columns(start):
+        while start not in columns_done:
+            next_columns()
+
+    load_columns(0)
     me = lax.axis_index("fsdp")
     replica = lax.axis_index("replica")
     up = replica // 2
@@ -628,18 +695,87 @@
         copies = []
         for piece in range(TOKEN_PIECES):
             at = pl.ds(piece * rows, rows)
-            for which, (source, target) in enumerate([(tok_out_ref, got_out_ref), (tok_grad_ref, got_grad_ref)]):
-                copy = remote(
-                    source.at[1, at], target.at[at], peers[1], tok_send.at[which, piece], tok_recv.at[which, piece]
-                )
-                copy.start()
-                copies.append(copy)
+            copy = remote(tok_out_ref.at[1, at], got_out_ref.at[at], peers[1], tok_send.at[0, piece], tok_recv.at[0, piece])
+            copy.start()
+            copies.append(copy)
+            yield
+        for piece in range(TOKEN_PIECES):
+            at = pl.ds(piece * rows, rows)
+            copy = remote(across_ref.at[at], got_grad_ref.at[at], peers[1], tok_send.at[1, piece], tok_recv.at[1, piece])
+            copy.start()
+            copies.append(copy)
             yield
         for copy in copies:
             copy.wait()
 
+    def row_products():
+        half_blocks = gp_ref.shape[0] // (2 * rows_of_block)
+        quarter_blocks = half_blocks // 2
+        later = list(range(quarter_blocks, half_blocks))
+        sooner = list(range(quarter_blocks))
+        order = [(True, i) for i in later] + [(False, i) for i in later]
+        order += [(True, i) for i in sooner] + [(False, i) for i in sooner]
+        norm_sum[...] = jnp.zeros_like(norm_sum)
+        row_loads = []
+
+        def load_rows(number):
+            if number < len(order):
+                far, block = order[number]
+                at = (half_blocks + block if far else block) * rows_of_block
+                copy = pltpu.make_async_copy(gp_ref.at[pl.ds(at, rows_of_block)], gp_rows, load_sems.at[3])
+                copy.start()
+                row_loads.append((copy, at))
+
+        load_rows(0)
+        need(0)
+        need(1)
+        arrivals = {}
+        busy = [None, None]
+        for number, (far, block) in enumerate(order):
+            slot = number % 2
+            if busy[slot] is not None:
+                busy[slot]()
+            if not far:
+                arrivals[block].wait_recv()
+                load = pltpu.make_async_copy(far_land_ref.at[block], far_tile, load_sems.at[4])
+                load.start()
+                load.wait()
+            copy, at = row_loads[number]
+            copy.wait()
+
+            def lanes_step(tile, carry):
+                lanes = pl.ds(pl.multiple_of(tile * LANE_TILE, LANE_TILE), LANE_TILE)
+                part = jnp.dot(gp_rows[...], cols[:, lanes], preferred_element_type=F32)
+                norm_sum[:, lanes] += jnp.sum(
+                    part * scaled[pl.ds(at, rows_of_block), lanes].astype(F32), 0, keepdims=True
+                )
+                if not far:
+                    part = part + far_tile[:, lanes].astype(F32)
+                tiles[slot, :, lanes] = part.astype(BF16)
+                return carry
+
+            lax.fori_loop(0, lane_tiles, lanes_step, 0)
+            load_rows(number + 1)
+            if far:
+                sent = remote(tiles.at[slot], far_land_ref.at[block], peers[0], far_send.at[block], far_recv.at[block])
+                sent.start()
+                arrivals[block] = sent
+                busy[slot] = sent.wait_send
+            else:
+                target = own_grad_ref if block < quarter_blocks else across_ref
+                place = pl.ds((block % quarter_blocks) * rows_of_block, rows_of_block)
+                store = pltpu.make_async_copy(tiles.at[slot], target.at[place], store_sems.at[block])
+                store.start()
+                busy[slot] = store.wait
+            yield
+        for wait in busy:
+            wait()
+        for tile in range(width // LANES):
+            small_sum_ref[norm_row + tile : norm_row + tile + 1, :] = norm_sum[:, tile * LANES : (tile + 1) * LANES]
+
     def smalls():
         small_sum_ref[...] = small_ref[...]
+        yield from row_products()
         for level, peer in enumerate([peers[0], peers[1], beside, partner, middle]):
             copy = remote(small_sum_ref, small_got.at[level], peer, small_send.at[level], small_recv.at[level])
             copy.start()
@@ -652,65 +788,58 @@
         if kind == "in":
             group = 0 if start >= inner else 4
             local_start = start % inner
-            source = lambda at, count: in_ref.at[pl.ds(pl.multiple_of(start + at, 16), count)]
+            ensure_columns(start // COLUMN_BLOCK * COLUMN_BLOCK)
+            base_ref, base_start = grads, start
             place = lambda at, count: sum_in_ref.at[pl.ds(group, 4), pl.ds(pl.multiple_of(local_start + at, 16), count)]
-        elif kind == "out":
-            source = lambda at, count: out_ref.at[pl.ds(pl.multiple_of(start + at, 16), count)]
-            place = lambda at, count: sum_out_ref.at[pl.ds(pl.multiple_of(start + at, 16), count)]
         else:
-            source = lambda at, count: shared_sum.at[pl.ds(at, count)]
+            ensure_columns(2 * inner)
+            base_ref, base_start = shared_sum, 0
             place = lambda at, count: sum_shared_ref.at[pl.ds(at, count)]
             copies = []
             for offset in range(3):
                 copy = remote(
-                    in_ref.at[pl.ds(2 * inner, rows), lanes_of(peers[offset][1])],
+                    grads.at[pl.ds(2 * inner, rows), lanes_of(peers[offset][1])],
                     shared_in.at[offset], peers[offset], shared_send.at[offset], shared_recv.at[offset],
                 )
                 copy.start()
                 copies.append(copy)
-            own = pltpu.make_async_copy(
-                in_ref.at[pl.ds(2 * inner, rows), lanes_of(me)], shared_in.at[3], local_sems.at[number, 1]
-            )
-            own.start()
             yield
-            own.wait()
-            total = shared_in[3].astype(F32)
+            total = grads[pl.ds(2 * inner, rows), lanes_of(me)].astype(F32)
             for offset in range(3):
                 copies[offset].wait_recv()
                 total = total + shared_in[offset].astype(F32)
             shared_sum[...] = total.astype(BF16)
 
+        def source(at, count):
+            return base_ref.at[pl.ds(pl.multiple_of(base_start + at, 16), count)]
+
         def link(from_ref, to_ref, device, slot):
             return remote(from_ref, to_ref, device, send_sems.at[number, slot], recv_sems.at[number, slot])
 
         def added(names_at, at, count):
-            total = None
+            total = source(at, count)[...].astype(F32)
             for name, base in names_at:
                 local = pl.multiple_of(at - base, count)
-                part = held[name][pl.ds(local, count), :].astype(F32)
-                total = part if total is None else total + part
+                total = total + held[name][pl.ds(local, count), :].astype(F32)
             return total
 
         two, four = rows // 2, rows // 4
         if order == "side":
             mine, other = pl.multiple_of(aside * two, two), pl.multiple_of((1 - aside) * two, two)
             low, high = pl.multiple_of(mine + half * four, four), pl.multiple_of(mine + (1 - half) * four, four)
-            keep = pltpu.make_async_copy(source(mine, two), held["keep"], local_sems.at[number, 0])
-            keep.start()
             side = link(source(other, two), held["got"], beside, 0)
             side.start()
             yield
-            keep.wait()
             side.wait_recv()
             lift = link(held["lift"], held["lift"], partner, 1)
 
             @pl.when(outside)
             def _():
-                held["lift"][...] = added([("keep", mine), ("got", mine)], mine, two).astype(BF16)
+                held["lift"][...] = added([("got", mine)], mine, two).astype(BF16)
                 lift.start()
 
             yield
-            bases = [("keep", mine), ("got", mine), ("lift", mine)]
+            bases = [("got", mine), ("lift", mine)]
             across = link(held["sent"], held["swapped"], middle, 2)
 
             @pl.when(inside)
@@ -724,24 +853,18 @@
         else:
             mine, other = pl.multiple_of(half * two, two), pl.multiple_of((1 - half) * two, two)
             low, high = pl.multiple_of(mine + aside * four, four), pl.multiple_of(mine + (1 - aside) * four, four)
-            keep = pltpu.make_async_copy(source(0, rows), held["keep"], local_sems.at[number, 0])
             lift = link(source(0, rows), held["got"], partner, 1)
 
             @pl.when(outside)
             def _():
                 lift.start()
 
+            yield
+            bases = [("got", 0)]
+            across = link(held["sent"], held["swapped"], middle, 2)
+
             @pl.when(inside)
             def _():
-                keep.start()
-
-            yield
-            bases = [("keep", 0), ("got", 0)]
-            across = link(held["sent"], held["swapped"], middle, 2)
-
-            @pl.when(inside)
-            def _():
-                keep.wait()
                 lift.wait_recv()
                 held["sent"][...] = added(bases, other, two).astype(BF16)
                 across.start()
@@ -766,9 +889,9 @@
             trade = [
                 link(final.at[:, lanes_of(peers[offset][1])], target, peers[offset], 3 + offset) for offset in range(3)
             ]
-            own = pltpu.make_async_copy(final.at[:, lanes_of(me)], target, local_sems.at[number, 1])
+            own = pltpu.make_async_copy(final.at[:, lanes_of(me)], target, local_sems.at[number])
         else:
-            own = pltpu.make_async_copy(final, place(low, four), local_sems.at[number, 1])
+            own = pltpu.make_async_copy(final, place(low, four), local_sems.at[number])
 
         if order == "side":
             back = [
@@ -853,7 +976,7 @@
                 copy.wait_send()
 
     waiting = [run(number, *chunk) for number, chunk in enumerate(chunks)]
-    active, extra = [], [activations(), smalls()]
+    active, extra = [], [smalls(), activations()]
 
     def advance(running):
         still = []
@@ -866,49 +989,65 @@
         return still
 
     while waiting or active:
-        active = advance(active + waiting[:PER_TICK])
-        waiting = waiting[PER_TICK:]
+        active = advance(active + waiting[:PER_TURN])
+        waiting = waiting[PER_TURN:]
         extra = advance(extra)
+        next_columns()
     while extra:
         extra = advance(extra)
 
 
-def reduce_gradients(size, depth, inner, common, grad_in, grad_out, tok_out, tok_grad, small):
-    width = grad_out.shape[1]
+def reduce_gradients(size, depth, inner, common, norm_row, gp, scaled, cols, tok_out, small):
+    total, width = scaled.shape
+    own_rows = tok_out.shape[1]
     chunks, counts = reduce_chunks(inner, common)
     scratch = []
     for (shared, rows, order), count in counts.items():
         for fraction in PARTS[order].values():
             scratch.append(pltpu.VMEM((count, rows // fraction, depth if shared else width), BF16))
     sems = pltpu.SemaphoreType.DMA
+    half_blocks = total // 2 // ROW_BLOCK
     scratch += [
-        pltpu.VMEM((4, common, depth), BF16),
+        pltpu.VMEM((3, common, depth), BF16),
         pltpu.VMEM((common, depth), BF16),
         pltpu.VMEM((5,) + small.shape, F32),
-        sems((len(chunks), SLOTS)), sems((len(chunks), SLOTS)), sems((len(chunks), 2)),
+        pltpu.VMEM(scaled.shape, BF16),
+        pltpu.VMEM(cols.shape, BF16),
+        pltpu.VMEM(cols.shape, BF16),
+        pltpu.VMEM((total, max(common, COLUMN_BLOCK)), BF16),
+        pltpu.VMEM((max(common, COLUMN_BLOCK), total), BF16),
+        pltpu.VMEM((ROW_BLOCK, gp.shape[1]), BF16),
+        pltpu.VMEM((2, ROW_BLOCK, width), BF16),
+        pltpu.VMEM((ROW_BLOCK, width), BF16),
+        pltpu.VMEM((1, width), F32),
+        sems((len(chunks), SLOTS)), sems((len(chunks), SLOTS)), sems((len(chunks),)),
         sems((2, TOKEN_PIECES)), sems((2, TOKEN_PIECES)), sems((5,)), sems((5,)), sems((3,)), sems((3,)),
+        sems((half_blocks,)), sems((half_blocks,)), sems((5,)), sems((half_blocks,)),
     ]
     anywhere = pl.BlockSpec(memory_space=pl.ANY)
     local = pl.BlockSpec(memory_space=pltpu.VMEM)
+    own = jax.ShapeDtypeStruct((own_rows, width), BF16)
     return pl.pallas_call(
-        functools.partial(reduce_kernel, (chunks, counts, inner, depth)),
+        functools.partial(reduce_kernel, (chunks, counts, inner, depth, common, norm_row)),
         in_specs=[anywhere] * 4 + [local],
-        out_specs=[anywhere] * 5 + [local],
+        out_specs=[anywhere] * 5 + [local] + [anywhere] * 2,
         out_shape=[
             jax.ShapeDtypeStruct((2 * size, inner, depth), BF16),
             jax.ShapeDtypeStruct((common, depth), BF16),
-            jax.ShapeDtypeStruct(grad_out.shape, BF16),
-            jax.ShapeDtypeStruct(tok_out.shape[1:], BF16),
-            jax.ShapeDtypeStruct(tok_grad.shape[1:], BF16),
+            own, own, own,
             jax.ShapeDtypeStruct(small.shape, F32),
+            jax.ShapeDtypeStruct((half_blocks, ROW_BLOCK, width), BF16),
+            own,
         ],
         scratch_shapes=scratch,
         compiler_params=pltpu.CompilerParams(
-            collective_id=0, has_side_effects=True, vmem_limit_bytes=58 << 20
+            collective_id=0, has_side_effects=True, vmem_limit_bytes=60 << 20
         ),
-        cost_estimate=pl.CostEstimate(flops=0, bytes_accessed=700 << 20, transcendentals=0),
+        cost_estimate=pl.CostEstimate(
+            flops=4 * total * gp.shape[1] * width, bytes_accessed=600 << 20, transcendentals=0
+        ),
         name="reduce_gradients",
-    )(grad_in, grad_out, tok_out, tok_grad, small)
+    )(gp, scaled, cols, tok_out, small)
 
 
 def small_pieces(size, copies, depth, inner, columns, me, replica, scaled_low, gp, normed_low, cot_all):
@@ -1001,7 +1140,7 @@
     own_cot = cotangent.reshape(own_rows, width)
     small = jnp.concatenate([norm_gain, conv_weight.reshape(-1), conv_bias])
     segments = segment_ids.reshape(micro_count * seq_count, tokens)
-    fused = copies == 8 and size == 4 and sum(OUT_ROWS) == inner and sum(IN_ROWS) == 2 * inner
+    fused = copies == 8 and size == 4 and sum(IN_ROWS) == 2 * inner
     if fused:
         padded = jnp.pad(small.astype(F32), (0, -small.shape[0] % (8 * LANES))).reshape(-1, LANES)
         x_all, seg_all, small, w_cols = gather_inputs(
@@ -1060,9 +1199,17 @@
     pull = root * root * root * stats[1] / full_inner
 
     normed_low = (gated.astype(F32) * root[:, None]).astype(BF16)
+    if fused:
+        grad_out = contract_rows(normed_low, cot_all).astype(BF16)
+        head_rows, grad_out = lax.optimization_barrier((head_rows, grad_out))
+        operands = operands[:5] + (head_rows,) + operands[6:]
+        own_out = lax.psum_scatter(grad_out, "replica", scatter_dimension=0, tiled=True)
     gp, grad_conv, grad_chan, grad_head = mix_backward(
         dims, operands, jnp.stack([root, pull], 1), grad_normed
     )
+    if fused:
+        own_out, grad_head = lax.optimization_barrier((own_out, grad_head))
+        grad_w_out = lax.all_gather(own_out, "replica", axis=0, tiled=True).astype(F32)
     own_wide = own_x.astype(F32)
     own_root = normalise(own_x)
 
@@ -1084,28 +1231,22 @@
             return kept.astype(BF16).reshape(2, own_rows, width)
 
         tok_out = halves(lambda start, stop: jnp.dot(gated[start:stop], w_out, preferred_element_type=F32))
-        far_grad = jnp.dot(gp[near:], w_cols, preferred_element_type=F32).astype(BF16)
-        near_grad = jnp.dot(gp[:near], w_cols, preferred_element_type=F32).astype(BF16)
-        tok_grad = (near_grad.astype(F32) + swap(far_grad, "fsdp", size, 1).astype(F32)).astype(BF16)
-        tok_grad = tok_grad.reshape(2, own_rows, width)
-        scaled_part = jnp.concatenate([near_grad, far_grad], 0)
-        grad_norm = jnp.sum(scaled_part.astype(F32) * x_all.astype(F32) * normalise(x_all), 0)
-        grad_out = contract_rows(normed_low, cot_all).astype(BF16)
-        grad_cols = contract_rows(gp, scaled_low).astype(BF16)
         spread = lax.dynamic_update_slice(jnp.zeros((size, own_small.shape[0]), F32), own_small[None], (me, 0))
-        vector = jnp.concatenate([conv_full, grad_norm, spread.reshape(-1)])
+        norm_row = -(-conv_full.shape[0] // LANES)
+        conv_padded = jnp.pad(conv_full, (0, norm_row * LANES - conv_full.shape[0]))
+        vector = jnp.concatenate([conv_padded, jnp.zeros((width,), F32), spread.reshape(-1)])
         vector = jnp.pad(vector, (0, -vector.shape[0] % (8 * LANES))).reshape(-1, LANES)
-        sum_in, sum_shared, sum_out, got_out, got_grad, vector = reduce_gradients(
-            size, depth, inner, common, grad_cols, grad_out, tok_out, tok_grad, vector
+        sum_in, sum_shared, got_out, own_grad, got_grad, vector, _, _ = reduce_gradients(
+            size, depth, inner, common, norm_row, gp, scaled_low, w_cols, tok_out, vector
         )
-        grad_w_out = sum_out.astype(F32)
         grad_w_in = jnp.concatenate([sum_in.reshape(2 * full_inner, depth), sum_shared], 0).astype(F32).T
         out_sum = tok_out[0].astype(F32) + got_out.astype(F32)
-        grad_scaled = tok_grad[0].astype(F32) + got_grad.astype(F32)
+        grad_scaled = own_grad.astype(F32) + got_grad.astype(F32)
         vector = vector.reshape(-1)
         conv_full = vector[: conv_full.shape[0]]
-        grad_norm = vector[conv_full.shape[0] : conv_full.shape[0] + width]
-        start = conv_full.shape[0] + width
+        start = norm_row * LANES
+        grad_norm = vector[start : start + width] / full_norm[0]
+        start = start + width
         own_small = lax.dynamic_slice(vector, (start + me * own_small.shape[0],), own_small.shape)
     else:
         out_part = jnp.dot(gated, w_out, preferred_element_type=F32).astype(BF16)

time: 729 us -> 662 us (0.908)
  matrix products: 130 us -> 75.2 us
  Pallas kernels: 486 us -> 464 us
  other arithmetic: 70 us -> 52.6 us
  waiting for transfers between devices: 0.84 us -> 17.7 us
  between operations: 1.64 us -> 15 us
    dot_general x2 -> x0, matrix products: 32.2 us -> none  [the longest x1 17 us: on_device(): jnp.dot(gp[:near], w_cols, preferred_element_type=F32).astype(BF16)]
    dot_general x2 -> x1, matrix products: 41.5 us -> 14.8 us  [contract_rows(): lax.dot_general(left, right, (((0,), (0,)), ((), ())), precision=precisio...]
    ppermute x6 -> x5, waiting for transfers between devices: 0.84 us -> 17.7 us  [swap(): return lax.ppermute(array, axis, [(i, i ^ bit) for i in range(size)])]
    pallas_call x1, Pallas kernels: 284 us -> 269 us  [reduce_gradients(): pl.pallas_call(functools.partial(reduce_kernel, (chunks, counts, inner, d...]
    reduce_sum x1 -> x0, other arithmetic: 9.62 us -> none  [on_device(): jnp.sum(scaled_part.astype(F32) * x_all.astype(F32) * normalise(x_all), 0)]
    unnamed x64 -> x54, local copies, waits for them, and re-layouts: 16.9 us -> 15.4 us
  transfers between devices with their start and end apart: 6 -> 7, of which waited for: 1 -> 4; matrix products, arithmetic and copies ran while one was open for 15% -> 15% of each run, Pallas kernels for 6% -> 59%
where the time goes in v3:
time: 662 us; the launch traced here: 653 us
  Pallas kernels  464 us (70%)
  matrix products  75.2 us (11%)
  other arithmetic  52.6 us (8%)
  local copies, waits for them, and re-layouts  26.4 us (4%)
  waiting for transfers between devices  17.7 us (3%)
  between operations  15 us (2%)
    pallas_call x1, Pallas kernels, reduce_gradients(): pl.pallas_call(functools.partial(reduce_kernel, (chunks, counts, inner, d...  269 us
    pallas_call x1, Pallas kernels, gather_inputs(): pl.pallas_call(functools.partial(gather_kernel, full_inner, inner), in_sp...  80.9 us
    pallas_call x1, Pallas kernels, mix_backward(): pl.pallas_call(functools.partial(backward_kernel, dims), grid=(total // t...  76.8 us
    dot_general x2, matrix products, contract_cols(): lax.dot_general(left, right, (((1,), (1,)), ((), ())), precision=precisio...  40.2 us
    pallas_call x1, Pallas kernels, mix_forward(): pl.pallas_call(functools.partial(forward_kernel, dims), grid=(total // to...  36.7 us
    dot_general x2, matrix products, on_device(): jnp.dot(gated[start:stop], w_out, preferred_element_type=F32)  20.2 us
    ppermute x5, waiting for transfers between devices, swap(): return lax.ppermute(array, axis, [(i, i ^ bit) for i in range(size)])  17.7 us
    unnamed x54, local copies, waits for them, and re-layouts  15.4 us
  transfers between devices with their start and end apart: 7, of which 4 were waited for; matrix products, arithmetic and copies ran while one was open for 15% of the time, Pallas kernels for 59%

profile of v3, /device:TPU:0, one launch (start us, length us, event | category | flops | bytes accessed | tf_op | source)
XLA Modules:
  0.0 653.1 jit_solution(5602864197644111099)
XLA Ops:
  8.7 1.6 copy-done
  10.3 3.5 copy-done.3
  14.5 80.9 %gather_inputs.1 = (bf16[4,512,2048]{2,1,0:T(8,128)(2,1)S(1)}, s32[4,4,128]{2,1,0:T(4,128)S(1)}, f32[4,48,128]{2,1,0:T(8,128)S(1)}, bf16[2368,2048]{1,0:T(8,128)(2,1)S(1)}) custom-call(bf16[512,2048]{1,0:T(8,128)(2,1)S(1)} %bitcast.96, s32[4,128]{1,0:T(4,128)S(1)} %bitcast.101, f32[48,128]{1,0:T(8,128)S(1)} %fusion.25.small_ref, bf16[8512,512]{1,0:T(8,128)(2,1)S(1)} %bitcast.97), custom_call_target="tpu_custom_call" | custom-call | bytes 209715200 | tf_op jit(solution)/shard_map/gather_inputs/pallas_call | solution.py:546
  95.4 3.4 copy-done.2
  98.8 3.6 copy-done.8
  102.5 1.0 collective-permute-start
  105.1 5.1 multiply_reduce_fusion
  110.2 8.7 %fusion.1.scaled_ref = bf16[2048,2048]{1,0:T(8,128)(2,1)} fusion(f32[2048]{0:T(1024)S(1)} %bitcast.115, f32[2048]{0:T(1024)S(1)} %bitcast.132, bf16[4,512,2048]{2,1,0:T(8,128)(2,1)} %copy-done.2), kind=kLoop, calls=%fused_computation.3 | loop fusion | flops 16777216 | bytes 16793600 | tf_op jit(solution)/shard_map/convert_element_type | solution.py:1169
  118.9 28.7 %fusion.35.proj_ref = f32[2048,2368]{1,0:T(8,128)} fusion(bf16[2048,2048]{1,0:T(8,128)(2,1)} %fusion.1.scaled_ref, bf16[2368,2048]{1,0:T(8,128)(2,1)} %copy-done.8), kind=kOutput, calls=%fused_computation.84 | convolution fusion | flops 19864223744 | bytes 37486592 | tf_op jit(solution)/shard_map/dot_general | solution.py:25
  148.8 36.7 %mix_forward.1 = (bf16[2048,1024]{1,0:T(8,128)(2,1)}, f32[2048,1]{1,0:T(8,128)S(1)}) custom-call(s32[1]{0:T(128)} %bitcast.5.own_ref, f32[2048,2368]{1,0:T(8,128)} %fusion.35.proj_ref, s32[8,256,1]{2,1,0:T(8,128)S(1)} %broadcast_in_dim_reshape.8.seg_col_ref, s32[8,1,256]{2,1,0:T(1,128)S(1)} %bitcast.99, f32[8,256,8]{2,1,0:T(8,128)S(1)} %pad_convert_fusion.mask_ref, ...), custom_call_target="tpu_custom_call" | custom-call | flops 2147483648 | bytes 19398656 | tf_op jit(solution)/shard_map/mix_forward/pallas_call | solution.py:303
  185.6 4.6 pad_maximum_fusion.1
  190.7 7.0 %collective-permute-done.1 = bf16[2,512,2048]{2,1,0:T(8,128)(2,1)} collective-permute-done((bf16[2,512,2048]{2,1,0:T(8,128)(2,1)}, bf16[2,512,2048]{2,1,0:T(8,128)(2,1)}, u32[]{:S(2)}, u32[]{:S(2)}) %collective-permute-start.1) | collective-permute-done | bytes 4194336 | tf_op jit(solution)/shard_map/ppermute | solution.py:367
  197.7 4.2 pad_maximum_fusion
  201.9 11.5 %fusion.2 = (f32[2048]{0:T(1024)S(1)}, f32[2048,1024]{1,0:T(8,128)}) fusion(bf16[2048,1024]{1,0:T(8,128)(2,1)S(1)} %copy-done.19, bf16[2048,2048]{1,0:T(8,128)(2,1)S(1)} %bitcast.105, bf16[1024,2048]{1,0:T(8,128)(2,1)S(1)} %copy-done.18), kind=kOutput, calls=%fused_computation.7 | convolution fusion | flops 8596224000 | bytes 25174016 | tf_op jit(solution)/shard_map/dot_general | solution.py:25
  213.7 1.0 collective-permute-done.2
  215.1 1.1 collective-permute-start.3
  216.2 2.7 collective-permute-done.3
  219.2 14.8 %fusion.10 = bf16[1024,2048]{1,0:T(8,128)(2,1)} fusion(bf16[2048,2048]{1,0:T(8,128)(2,1)} %bitcast.106, bf16[2048,1024]{1,0:T(8,128)(2,1)} %get-tuple-element.41, f32[2048]{0:T(1024)S(1)} %bitcast.130), kind=kOutput, calls=%fused_computation.23 | convolution fusion | flops 8598323200 | bytes 16785408 | tf_op jit(solution)/shard_map/dot_general | solution.py:19
  234.0 9.5 %convolution_convert_fusion = bf16[1024,2048]{1,0:T(8,128)(2,1)} fusion(bf16[1024,2048]{1,0:T(8,128)(2,1)} %param.23, bf16[2048,1024]{1,0:T(8,128)(2,1)} %get-tuple-element.41), kind=kOutput, calls=%fused_computation.22 | convolution fusion | flops 4297064448 | bytes 10485760 | tf_op jit(solution)/shard_map/dot_general | solution.py:1233
  244.0 7.0 %collective-permute-done.4 = bf16[1024,2048]{1,0:T(8,128)(2,1)} collective-permute-done((bf16[1024,2048]{1,0:T(8,128)(2,1)}, bf16[1024,2048]{1,0:T(8,128)(2,1)}, u32[]{:S(2)}, u32[]{:S(2)}) %collective-permute-start.4) | collective-permute-done | bytes 4194336 | tf_op jit(solution)/shard_map/ppermute | solution.py:367
  251.0 10.7 %add_convert_fusion = bf16[1024,2048]{1,0:T(8,128)(2,1)} fusion(bf16[1024,2048]{1,0:T(8,128)(2,1)} %collective-permute-done.4, bf16[1024,2048]{1,0:T(8,128)(2,1)} %param.23, bf16[2048,1024]{1,0:T(8,128)(2,1)} %get-tuple-element.41), kind=kOutput, calls=%fused_computation.10 | convolution fusion | flops 4301258752 | bytes 14680064 | tf_op jit(solution)/shard_map/dot_general | solution.py:1233
  261.7 1.3 copy.88.stats_ref
  263.1 1.2 copy-done.5
  264.3 1.2 copy-done.6
  265.5 76.8 %mix_backward.1 = (bf16[2048,2368]{1,0:T(8,128)(2,1)}, f32[8,1280]{1,0:T(8,128)S(1)}, f32[8,1024]{1,0:T(8,128)S(1)}, f32[8,128]{1,0:T(8,128)S(1)}) custom-call(s32[1]{0:T(128)} %bitcast.5.own_ref, f32[2048,2368]{1,0:T(8,128)} %fusion.35.proj_ref, s32[8,256,1]{2,1,0:T(8,128)S(1)} %copy-done.5, s32[8,1,256]{2,1,0:T(1,128)S(1)} %bitcast.100, ...), custom_call_target="tpu_custom_call" | custom-call | flops 6442450944 | bytes 29097984 | tf_op jit(solution)/shard_map/mix_backward/pallas_call | solution.py:331
  343.6 269.1 %reduce_gradients.1 = (bf16[8,1024,512]{2,1,0:T(8,128)(2,1)}, bf16[320,512]{1,0:T(8,128)(2,1)}, bf16[512,2048]{1,0:T(8,128)(2,1)}, bf16[512,2048]{1,0:T(8,128)(2...) custom-call(bf16[2048,2368]{1,0:T(8,128)(2,1)} %get-tuple-element.44, ...), custom_call_target="tpu_custom_call" | custom-call | flops 39728447488 | bytes 629145600 | tf_op jit(solution)/shard_map/reduce_gradients/pallas_call | solution.py:1030
  613.7 1.5 dynamic-slice.5
  615.9 1.4 fusion.33
  618.7 3.2 fusion.5
  622.6 6.3 fusion.6
  629.0 10.2 %convert_bitcast_fusion = f32[512,8512]{0,1:T(8,128)} fusion(bf16[320,512]{1,0:T(8,128)(2,1)S(1)} %copy-done.13, bf16[8192,512]{1,0:T(8,128)(2,1)S(1)} %bitcast.104), kind=kLoop, calls=%fused_computation | loop fusion | flops 17432576 | bytes 26148864 | tf_op jit(solution)/shard_map/transpose | solution.py:1242
  639.2 6.7 %convert_element_type.112 = f32[1024,2048]{1,0:T(8,128)} convert(bf16[1024,2048]{1,0:T(8,128)(2,1)} %all-gather.2.cloned.1.call-done) | non-fusion elementwise | flops 2097152 | bytes 12582912 | tf_op jit(solution)/shard_map/convert_element_type | solution.py:1212
  (128 shorter events, 11.8 us)
Async XLA Ops:
  7.2 335.5 %reduce-scatter.2.cloned.1.call-start = ((), (), s32[]{:S(2)}) async-start(), calls=%async_computation.1 | async-start | bytes 4718592 | tf_op jit(solution)/shard_map/reduce_scatter | solution.py:1206
  8.7 1.6 copy-start
  10.3 3.5 copy-start.3
  13.8 0.7 copy-start.7
  95.4 3.4 copy-start.2
  98.8 3.6 copy-start.8
  102.5 83.1 %collective-permute-start = (bf16[512,2048]{1,0:T(8,128)(2,1)}, bf16[512,2048]{1,0:T(8,128)(2,1)}, u32[]{:S(2)}, u32[]{:S(2)}) collective-permute-start(bf16[512,2048]{1,0:T(8,128)(2,1)} %bitcast.1), channel_id=1, source_target_pairs={{0,2},{1,3},{2,0},{3,1},{4,6},{5,7},{6,4},{7,5},{8,10},{9,11},{10,... | collective-permute-start | bytes 6291464 | tf_op jit(solution)/shard_map/ppermute | solution.py:367
  104.4 44.4 %copy-start.4 = (s32[8,256,1]{2,1,0:T(8,128)}, s32[8,256,1]{2,1,0:T(8,128)S(1)}, u32[]{:S(2)}) copy-start(s32[8,256,1]{2,1,0:T(8,128)S(1)} %broadcast_in_dim_reshape.8.seg_col_ref) | copy-start | bytes 24580
  105.1 5.1 copy-start.14
  118.9 29.5 %copy-start.17 = (bf16[16]{0:T(256)(128)(2,1)S(1)}, bf16[16]{0:T(256)(128)(2,1)}, u32[]{:S(2)}) copy-start(bf16[16]{0:T(256)(128)(2,1)} %param.21) | copy-start | bytes 100
  118.9 29.7 %copy-start.16 = (bf16[1024]{0:T(1024)(128)(2,1)S(1)}, bf16[1024]{0:T(1024)(128)(2,1)}, u32[]{:S(2)}) copy-start(bf16[1024]{0:T(1024)(128)(2,1)} %param.22) | copy-start | bytes 6148
  118.9 29.7 %copy-start.20 = (bf16[16]{0:T(256)(128)(2,1)S(1)}, bf16[16]{0:T(256)(128)(2,1)}, u32[]{:S(2)}) copy-start(bf16[16]{0:T(256)(128)(2,1)} %param.20) | copy-start | bytes 100
  118.9 29.7 %copy-start.21 = (bf16[16]{0:T(256)(128)(2,1)S(1)}, bf16[16]{0:T(256)(128)(2,1)}, u32[]{:S(2)}) copy-start(bf16[16]{0:T(256)(128)(2,1)} %param.19) | copy-start | bytes 100
  190.2 7.5 %collective-permute-start.1 = (bf16[2,512,2048]{2,1,0:T(8,128)(2,1)}, bf16[2,512,2048]{2,1,0:T(8,128)(2,1)}, u32[]{:S(2)}, u32[]{:S(2)}) collective-permute-start(bf16[2,512,2048]{2,1,0:T(8,128)(2,1)} %pad_maximum_fusion.1), channel_id=1, source_target_pairs={{0,1},{1,0},{2,3},{3,2},{4,5},{5,4},{6,7},{7,6},{8,9},{9,8},{10,11... | collective-permute-start | bytes 12582920 | tf_op jit(solution)/shard_map/ppermute | solution.py:367
  190.7 11.2 %copy-start.18 = (bf16[1024,2048]{1,0:T(8,128)(2,1)S(1)}, bf16[1024,2048]{1,0:T(8,128)(2,1)}, u32[]{:S(2)}) copy-start(bf16[1024,2048]{1,0:T(8,128)(2,1)} %param.23) | copy-start | bytes 12582916
  190.7 11.2 %copy-start.19 = (bf16[2048,1024]{1,0:T(8,128)(2,1)S(1)}, bf16[2048,1024]{1,0:T(8,128)(2,1)}, u32[]{:S(2)}) copy-start(bf16[2048,1024]{1,0:T(8,128)(2,1)} %get-tuple-element.41) | copy-start | bytes 12582916
  201.9 11.5 %copy-start.11 = (bf16[4,512,2048]{2,1,0:T(8,128)(2,1)}, bf16[4,512,2048]{2,1,0:T(8,128)(2,1)S(1)}, u32[]{:S(2)}) copy-start(bf16[4,512,2048]{2,1,0:T(8,128)(2,1)S(1)} %pad_maximum_fusion) | copy-start | bytes 25165828
  213.5 1.2 collective-permute-start.2
  215.1 3.8 collective-permute-start.3
  234.0 9.5 %copy-start.1 = (bf16[2,1,256,2048]{3,2,1,0:T(8,128)(2,1)S(1)}, bf16[2,1,256,2048]{3,2,1,0:T(8,128)(2,1)}, u32[]{:S(2)}) copy-start(bf16[2,1,256,2048]{3,2,1,0:T(8,128)(2,1)} %param.12) | copy-start | bytes 6291460
  234.0 405.2 %all-gather.2.cloned.1.call-start = ((), (), s32[]{:S(2)}) async-start(), calls=%async_computation.2 | async-start | bytes 4718592 | tf_op jit(solution)/shard_map/all_gather | solution.py:1212
  243.5 7.5 %collective-permute-start.4 = (bf16[1024,2048]{1,0:T(8,128)(2,1)}, bf16[1024,2048]{1,0:T(8,128)(2,1)}, u32[]{:S(2)}, u32[]{:S(2)}) collective-permute-start(bf16[1024,2048]{1,0:T(8,128)(2,1)} %convolution_convert_fusion), channel_id=1, source_target_pairs={{0,1},{1,0},{2,3},{3,2},{4,5},{5,4},{6,7},{7,6},{8,9},{9,8},{10,11... | collective-permute-start | bytes 12582920 | tf_op jit(solution)/shard_map/ppermute | solution.py:367
  263.1 1.2 copy-start.5
  264.3 1.2 copy-start.6
  343.6 274.4 %copy-start.15 = (f32[1,4,4,128]{3,1,2,0:T(4,128)S(1)}, f32[1,4,4,128]{3,1,2,0:T(4,128)}, u32[]{:S(2)}) copy-start(f32[1,4,4,128]{3,1,2,0:T(4,128)} %copy-done.14) | copy-start | bytes 24580
  613.7 8.9 %copy-start.9 = (bf16[512,2048]{1,0:T(8,128)(2,1)S(1)}, bf16[512,2048]{1,0:T(8,128)(2,1)}, u32[]{:S(2)}) copy-start(bf16[512,2048]{1,0:T(8,128)(2,1)} %get-tuple-element.51) | copy-start | bytes 6291460
  613.7 8.9 %copy-start.10 = (bf16[512,2048]{1,0:T(8,128)(2,1)S(1)}, bf16[512,2048]{1,0:T(8,128)(2,1)}, u32[]{:S(2)}) copy-start(bf16[512,2048]{1,0:T(8,128)(2,1)} %get-tuple-element.52) | copy-start | bytes 6291460
  613.7 8.9 %copy-start.12 = (bf16[512,2048]{1,0:T(8,128)(2,1)S(1)}, bf16[512,2048]{1,0:T(8,128)(2,1)}, u32[]{:S(2)}) copy-start(bf16[512,2048]{1,0:T(8,128)(2,1)} %get-tuple-element.50) | copy-start | bytes 6291460
  622.6 6.4 slice-start
  622.6 6.3 slice-start.1
  622.6 6.3 copy-start.13
Sparse Core Ops, SparseCore 0:
  234.1 88.1 reduce-scatter.1
  343.1 116.0 all-gather.1

commit v4 on v3

--- a/solution.py
+++ b/solution.py
@@ -13,6 +13,7 @@
 F32 = jnp.float32
 BF16 = jnp.bfloat16
 LOG2E = 1.4426950408889634
+VMEM_LIMIT = 60 << 20
 
 
 def contract_rows(left, right, precision=None):
@@ -94,7 +95,7 @@
 
 
 def forward_kernel(dims, own_ref, proj_ref, seg_col_ref, seg_row_ref, mask_ref, head_ref, cw_ref, chan_ref,
-                   gated_ref, square_ref,
+                   gated_ref, square_ref, out_ref,
                    mask_wide, visible_bias, step_wide, cum_wide, cum_rows, state_act, affinity):
     tokens, inner, state2, heads, local_heads, taps = dims
     prepare(dims, own_ref, proj_ref, seg_col_ref, seg_row_ref, mask_ref, head_ref, cw_ref,
@@ -128,6 +129,7 @@
                     weights, mine[: (tb + 1) * LANES], preferred_element_type=F32
                 )
         out = jnp.concatenate(parts, 0)
+        out_ref[:, here] = out.astype(BF16)
         gate = proj_ref[:, pl.ds(pl.multiple_of(inner + pair * LANES, LANES), LANES)]
         gated = out * (gate * sigmoid(gate))
         gated_ref[:, here] = (gated * chan_ref[1:2, here]).astype(BF16)
@@ -138,7 +140,7 @@
 
 
 def backward_kernel(dims, own_ref, proj_ref, seg_col_ref, seg_row_ref, mask_ref, head_ref, cw_ref, chan_ref,
-                    stats_ref, gn_ref,
+                    stats_ref, gn_ref, out_ref,
                     gp_ref, grad_cw_ref, grad_chan_ref, grad_head_ref,
                     mask_wide, visible_bias, step_wide, cum_wide, cum_rows, state_act, affinity,
                     grad_affinity, row_sums, col_sums, wide_stats):
@@ -186,21 +188,7 @@
         weighted = values * step_wide[pair]
         skip = chan_ref[0:1, here]
         halves = [jnp.where(first == (which == 0), weighted, 0.0).astype(BF16) for which in range(2)]
-        out_parts = [(skip * values)[b * LANES : (b + 1) * LANES] for b in range(blocks)]
-        for which in range(2):
-            head = 2 * pair + which
-            for tb in range(blocks):
-                t_rows = slice(tb * LANES, (tb + 1) * LANES)
-                pieces = []
-                for sb in range(tb + 1):
-                    s_cols = slice(sb * LANES, (sb + 1) * LANES)
-                    distance = (cum_wide[head, t_rows, :] - cum_rows[head, :, s_cols]) + visible_bias[t_rows, s_cols]
-                    pieces.append((affinity[t_rows, s_cols] * jnp.exp2(distance)).astype(BF16))
-                weights = jnp.concatenate(pieces, 1) if tb > 0 else pieces[0]
-                out_parts[tb] = out_parts[tb] + jnp.dot(
-                    weights, halves[which][: (tb + 1) * LANES], preferred_element_type=F32
-                )
-        out = jnp.concatenate(out_parts, 0)
+        out = out_ref[:, here].astype(F32)
         gate = proj_ref[:, there]
         gate_sig = sigmoid(gate)
         gate_silu = gate * gate_sig
@@ -307,13 +295,15 @@
         out_specs=[
             pl.BlockSpec((tokens, inner), lambda s: (s, 0)),
             pl.BlockSpec((tokens, 1), lambda s: (s, 0)),
+            pl.BlockSpec((tokens, inner), lambda s: (s, 0)),
         ],
         out_shape=[
             jax.ShapeDtypeStruct((total, inner), BF16),
             jax.ShapeDtypeStruct((total, 1), F32),
+            jax.ShapeDtypeStruct((total, inner), BF16),
         ],
         scratch_shapes=scratch,
-        compiler_params=pltpu.CompilerParams(vmem_limit_bytes=48 << 20),
+        compiler_params=pltpu.CompilerParams(vmem_limit_bytes=VMEM_LIMIT),
         cost_estimate=pl.CostEstimate(
             flops=total * local_heads * tokens * 4 * 64,
             bytes_accessed=total * width * 4,
@@ -323,7 +313,7 @@
     )(*operands)
 
 
-def mix_backward(dims, operands, stats, grad_normed):
+def mix_backward(dims, operands, stats, grad_normed, scan_out):
     tokens, inner, state2, heads, local_heads, taps = dims
     total, width = operands[1].shape
     in_specs, scratch = mixer_specs(dims, width)
@@ -333,6 +323,7 @@
         grid=(total // tokens,),
         in_specs=in_specs + [
             pl.BlockSpec((tokens, 2), lambda s: (s, 0)),
+            pl.BlockSpec((tokens, inner), lambda s: (s, 0)),
             pl.BlockSpec((tokens, inner), lambda s: (s, 0)),
         ],
         out_specs=[
@@ -353,14 +344,35 @@
             pltpu.VMEM((local_heads, 1, tokens), F32),
             pltpu.VMEM((2, tokens, LANES), F32),
         ],
-        compiler_params=pltpu.CompilerParams(vmem_limit_bytes=48 << 20),
+        compiler_params=pltpu.CompilerParams(vmem_limit_bytes=VMEM_LIMIT),
         cost_estimate=pl.CostEstimate(
             flops=total * local_heads * tokens * 12 * 64,
             bytes_accessed=total * width * 6,
             transcendentals=2 * total * local_heads * tokens,
         ),
         name="mix_backward",
-    )(*operands, stats, grad_normed)
+    )(*operands, stats, grad_normed, scan_out)
+
+
+def norm_kernel(x_ref, gain_ref, scaled_ref):
+    wide = x_ref[...].astype(F32)
+    root = lax.rsqrt(jnp.mean(wide * wide, 1, keepdims=True) + EPS)
+    scaled_ref[...] = (wide * root * gain_ref[...]).astype(BF16)
+
+
+def norm_rows(inputs, gain):
+    rows, width = inputs.shape
+    block = pl.BlockSpec((256, width), lambda s: (s, 0))
+    return pl.pallas_call(
+        norm_kernel,
+        grid=(rows // 256,),
+        in_specs=[block, pl.BlockSpec((1, width), lambda s: (0, 0))],
+        out_specs=block,
+        out_shape=jax.ShapeDtypeStruct(inputs.shape, BF16),
+        compiler_params=pltpu.CompilerParams(vmem_limit_bytes=VMEM_LIMIT),
+        cost_estimate=pl.CostEstimate(flops=4 * rows * width, bytes_accessed=4 * rows * width, transcendentals=rows),
+        name="norm_rows",
+    )(inputs, gain)
 
 
 def swap(array, axis, size, bit):
@@ -446,8 +458,8 @@
 
 
 def gather_kernel(full_inner, inner, x_ref, seg_ref, small_ref, w_ref,
-                  x_all_ref, seg_all_ref, small_all_ref, cols_ref,
-                  x_held, cols_held, send_sems, recv_sems, local_sems, store_sems):
+                  scaled_ref, seg_all_ref, small_all_ref, cols_ref,
+                  x_all_ref, scaled, gain, cols_held, send_sems, recv_sems, local_sems, store_sems, norm_sems):
     me = lax.axis_index("fsdp")
     replica = lax.axis_index("replica")
     depth, common = w_ref.shape[1], w_ref.shape[0] - 2 * full_inner
@@ -488,25 +500,53 @@
         return [send(source, target, device) for source, target in zip(from_refs, to_refs)]
 
     spot = replica % 4
+    smalls = [send(small_ref, small_all_ref.at[me], peer) for peer in peers]
+    smalls += [send(seg_ref, seg_all_ref.at[slot], peer) for peer, slot in zip(peers, (2, 1, 3))]
     across = [send_parts(sources(peers[which][1], spot, 1), targets(me, spot, 1), peers[which]) for which in (1, 2)]
     x_y = send(x_ref, x_all_ref.at[1], peers[1])
-    smalls = [send(small_ref, small_all_ref.at[me], peer) for peer in peers]
-    smalls += [send(seg_ref, seg_all_ref.at[slot], peer) for peer, slot in zip(peers, (2, 1, 3))]
     near = send_parts(sources(peers[0][1], 0, 4), targets(me, 0, 4), peers[0])
     x_near = send(x_ref, x_all_ref.at[2], peers[0])
-    held = [cols_held.at[pl.ds(base, length)] for base, length in parts] + [x_held]
-    own = list(zip(sources(me, 0, 4) + [x_ref], held, targets(me, 0, 4) + [x_all_ref.at[0]]))
+    held = [cols_held.at[pl.ds(base, length)] for base, length in parts]
+    own = list(zip(sources(me, 0, 4), held, targets(me, 0, 4)))
     loads = [pltpu.make_async_copy(source, held, local_sems.at[i]) for i, (source, held, _) in enumerate(own)]
     stores = [pltpu.make_async_copy(held, target, store_sems.at[i]) for i, (_, held, target) in enumerate(own)]
-    stores += [
-        pltpu.make_async_copy(small_ref, small_all_ref.at[me], local_sems.at[4]),
-        pltpu.make_async_copy(seg_ref, seg_all_ref.at[0], local_sems.at[5]),
-    ]
-    for copy in loads + stores[4:]:
+    x_own = pltpu.make_async_copy(x_ref, x_all_ref.at[0], local_sems.at[3])
+    small_own = pltpu.make_async_copy(small_ref, small_all_ref.at[me], local_sems.at[4])
+    stores.append(pltpu.make_async_copy(seg_ref, seg_all_ref.at[0], local_sems.at[5]))
+    for copy in loads + [x_own, small_own, stores[-1]]:
         copy.start()
     for load, store in zip(loads, stores):
         load.wait()
         store.start()
+
+    rows_at_once = 128
+    block_rows, width = scaled.shape[1:]
+    tiles_of_owner = depth // LANES
+
+    def normalise(block):
+        def step(piece, carry):
+            rows = pl.ds(pl.multiple_of(piece * rows_at_once, rows_at_once), rows_at_once)
+            wide = x_all_ref[block, rows, :].astype(F32)
+            root = lax.rsqrt(jnp.mean(wide * wide, 1, keepdims=True) + EPS)
+            scaled[block, rows, :] = (wide * root * gain[...]).astype(BF16)
+            return carry
+
+        lax.fori_loop(0, block_rows // rows_at_once, step, 0)
+        store = pltpu.make_async_copy(
+            scaled.at[block], scaled_ref.at[pl.ds(block * block_rows, block_rows)], norm_sems.at[block]
+        )
+        store.start()
+        stores.append(store)
+
+    small_own.wait()
+    for copy in smalls:
+        copy.wait_recv()
+    for tile in range(width // LANES):
+        gain[:, tile * LANES : (tile + 1) * LANES] = small_all_ref[
+            tile // tiles_of_owner, tile % tiles_of_owner : tile % tiles_of_owner + 1, :
+        ]
+    x_own.wait()
+    normalise(0)
 
     def relay(which, first, count, device):
         refs = targets(peers[which][1], first, count)
@@ -525,9 +565,14 @@
         copy.wait_recv()
     last += relay(2, spot, 1, beside)
     last += relay(2, flip(spot, 2), 1, beside)
+    x_near.wait_recv()
+    normalise(2)
     x_y.wait_recv()
-    last.append(send(x_all_ref.at[1], x_all_ref.at[3], peers[0]))
-    for copy in last + smalls + near + [x_near]:
+    x_last = send(x_all_ref.at[1], x_all_ref.at[3], peers[0])
+    normalise(1)
+    x_last.wait_recv()
+    normalise(3)
+    for copy in last + near:
         copy.wait_recv()
     for copy in stores:
         copy.wait()
@@ -542,27 +587,30 @@
     full, depth = w_flipped.shape
     full_inner = inner * size
     columns = 2 * inner + full - 2 * full_inner
-    anywhere = pl.BlockSpec(memory_space=pl.ANY)
+    anywhere = pl.BlockSpec(memory_space=pltpu.HBM)
     return pl.pallas_call(
         functools.partial(gather_kernel, full_inner, inner),
         in_specs=[anywhere] * 4,
-        out_specs=[anywhere] * 4,
+        out_specs=[anywhere] * 2 + [pl.BlockSpec(memory_space=pltpu.VMEM), anywhere],
         out_shape=[
-            jax.ShapeDtypeStruct((size,) + x.shape, BF16),
+            jax.ShapeDtypeStruct((size * x.shape[0], x.shape[1]), BF16),
             jax.ShapeDtypeStruct((size,) + segments.shape, jnp.int32),
             jax.ShapeDtypeStruct((size,) + small.shape, F32),
             jax.ShapeDtypeStruct((columns, size * depth), BF16),
         ],
         scratch_shapes=[
-            pltpu.VMEM(x.shape, BF16),
+            pltpu.VMEM((size,) + x.shape, BF16),
+            pltpu.VMEM((size,) + x.shape, BF16),
+            pltpu.VMEM((1, x.shape[1]), F32),
             pltpu.VMEM((columns, depth), BF16),
             pltpu.SemaphoreType.DMA((GATHER_COPIES,)),
             pltpu.SemaphoreType.DMA((GATHER_COPIES,)),
             pltpu.SemaphoreType.DMA((6,)),
+            pltpu.SemaphoreType.DMA((3,)),
             pltpu.SemaphoreType.DMA((4,)),
         ],
         compiler_params=pltpu.CompilerParams(
-            collective_id=1, has_side_effects=True, vmem_limit_bytes=16 << 20
+            collective_id=1, has_side_effects=True, vmem_limit_bytes=VMEM_LIMIT
         ),
         cost_estimate=pl.CostEstimate(flops=0, bytes_accessed=200 << 20, transcendentals=0),
         name="gather_inputs",
@@ -578,7 +626,7 @@
 SHARED_AT = 4
 COLUMN_BLOCK = 256
 ROW_BLOCK = 256
-LANE_TILE = 256
+LANE_TILE = 1024
 PER_TURN = 3
 TOKEN_PIECES = 8
 
@@ -593,7 +641,7 @@
     counts = {}
     placed = []
     for number, (kind, start, rows) in enumerate(pieces):
-        order = "lift" if number % 3 == 2 else "side"
+        order = "lift" if number % 4 == 2 else "side"
         key = (kind == "shared", rows, order)
         where = counts.get(key, 0)
         counts[key] = where + 1
@@ -1024,7 +1072,7 @@
         sems((2, TOKEN_PIECES)), sems((2, TOKEN_PIECES)), sems((5,)), sems((5,)), sems((3,)), sems((3,)),
         sems((half_blocks,)), sems((half_blocks,)), sems((5,)), sems((half_blocks,)),
     ]
-    anywhere = pl.BlockSpec(memory_space=pl.ANY)
+    anywhere = pl.BlockSpec(memory_space=pltpu.HBM)
     local = pl.BlockSpec(memory_space=pltpu.VMEM)
     own = jax.ShapeDtypeStruct((own_rows, width), BF16)
     return pl.pallas_call(
@@ -1041,7 +1089,7 @@
         ],
         scratch_shapes=scratch,
         compiler_params=pltpu.CompilerParams(
-            collective_id=0, has_side_effects=True, vmem_limit_bytes=60 << 20
+            collective_id=0, has_side_effects=True, vmem_limit_bytes=VMEM_LIMIT
         ),
         cost_estimate=pl.CostEstimate(
             flops=4 * total * gp.shape[1] * width, bytes_accessed=600 << 20, transcendentals=0
@@ -1143,13 +1191,13 @@
     fused = copies == 8 and size == 4 and sum(IN_ROWS) == 2 * inner
     if fused:
         padded = jnp.pad(small.astype(F32), (0, -small.shape[0] % (8 * LANES))).reshape(-1, LANES)
-        x_all, seg_all, small, w_cols = gather_inputs(
+        scaled_low, seg_all, small, w_cols = gather_inputs(
             size, inner, own_x, segments.reshape(-1, LANES), padded, w_in.T
         )
-        x_all = x_all.reshape(total, width)
         small = small.reshape(size, -1)
         own_cot_later, _ = lax.optimization_barrier((own_cot, seg_all))
         cot_across = swap(own_cot_later, "fsdp", size, 2)
+        cot_beside = swap(own_cot_later, "fsdp", size, 1)
     else:
         small = lax.all_gather(small, "fsdp", axis=0, tiled=False).astype(F32)
         x_all = gather_relative(own_x, "fsdp", size).reshape(total, width)
@@ -1166,7 +1214,8 @@
         wide = inputs.astype(F32)
         return lax.rsqrt(jnp.mean(wide * wide, -1, keepdims=True) + EPS)
 
-    scaled_low = (x_all.astype(F32) * normalise(x_all) * full_norm).astype(BF16)
+    if not fused:
+        scaled_low = norm_rows(x_all, full_norm)
     projected = contract_cols(scaled_low, w_cols)
 
     conv_all = jnp.concatenate([full_cw, full_cb, jnp.zeros((7 - taps, conv_width), F32)], 0)
@@ -1187,11 +1236,10 @@
         me.astype(jnp.int32).reshape(1), projected, seg_all[:, :, None], seg_all[:, None, :], same,
         head_rows, conv_own, chan_rows,
     )
-    gated, squares = mix_forward(dims, operands)
+    gated, squares, scan_out = mix_forward(dims, operands)
     if fused:
         cot_across, squares = lax.optimization_barrier((cot_across, squares))
-        pair = jnp.stack([own_cot, cot_across])
-        cot_all = jnp.concatenate([pair, swap(pair, "fsdp", size, 1)], 0).reshape(total, width)
+        cot_all = jnp.concatenate([own_cot, cot_across, cot_beside, swap(cot_across, "fsdp", size, 1)], 0)
     grad_normed = contract_cols(cot_all, w_out)
     cross = jnp.sum(gated.astype(F32) * grad_normed, 1)
     stats = sum_tokens(jnp.stack([squares[:, 0], cross]), "fsdp", size)
@@ -1200,15 +1248,21 @@
 
     normed_low = (gated.astype(F32) * root[:, None]).astype(BF16)
     if fused:
+        near = total // 2
+        far_out = jnp.dot(gated[near:], w_out, preferred_element_type=F32).astype(BF16)
+        normed_low, far_out = lax.optimization_barrier((normed_low, far_out))
+        far_out = swap(far_out, "fsdp", size, 1)
         grad_out = contract_rows(normed_low, cot_all).astype(BF16)
         head_rows, grad_out = lax.optimization_barrier((head_rows, grad_out))
         operands = operands[:5] + (head_rows,) + operands[6:]
         own_out = lax.psum_scatter(grad_out, "replica", scatter_dimension=0, tiled=True)
+        tok_out = jnp.dot(gated[:near], w_out, preferred_element_type=F32) + far_out.astype(F32)
+        tok_out = tok_out.astype(BF16).reshape(2, own_rows, width)
     gp, grad_conv, grad_chan, grad_head = mix_backward(
-        dims, operands, jnp.stack([root, pull], 1), grad_normed
+        dims, operands, jnp.stack([root, pull], 1), grad_normed, scan_out
     )
     if fused:
-        own_out, grad_head = lax.optimization_barrier((own_out, grad_head))
+        own_out, grad_head, tok_out = lax.optimization_barrier((own_out, grad_head, tok_out))
         grad_w_out = lax.all_gather(own_out, "replica", axis=0, tiled=True).astype(F32)
     own_wide = own_x.astype(F32)
     own_root = normalise(own_x)
@@ -1223,14 +1277,6 @@
     )
 
     if fused:
-        near = total // 2
-
-        def halves(product):
-            sent = swap(product(near, total).astype(BF16), "fsdp", size, 1)
-            kept = product(0, near) + sent.astype(F32)
-            return kept.astype(BF16).reshape(2, own_rows, width)
-
-        tok_out = halves(lambda start, stop: jnp.dot(gated[start:stop], w_out, preferred_element_type=F32))
         spread = lax.dynamic_update_slice(jnp.zeros((size, own_small.shape[0]), F32), own_small[None], (me, 0))
         norm_row = -(-conv_full.shape[0] // LANES)
         conv_padded = jnp.pad(conv_full, (0, norm_row * LANES - conv_full.shape[0]))

time: 662 us -> 619 us (0.935)
  other arithmetic: 52.6 us -> 38.1 us
  Pallas kernels: 464 us -> 450 us
  waiting for transfers between devices: 17.7 us -> 4.7 us
  local copies, waits for them, and re-layouts: 26.4 us -> 18.9 us
    ppermute x5 -> x6, waiting for transfers between devices: 17.7 us -> 3.95 us  [swap(): return lax.ppermute(array, axis, [(i, i ^ bit) for i in range(size)])]
    unnamed x54 -> x29, local copies, waits for them, and re-layouts: 15.4 us -> 2.45 us
    pallas_call x1, Pallas kernels: 269 us -> 258 us  [reduce_gradients(): pl.pallas_call(functools.partial(reduce_kernel, (chunks, counts, inner, d...]
  transfers between devices with their start and end apart: 7 -> 8, of which waited for: 4 -> 3; matrix products, arithmetic and copies ran while one was open for 15% -> 15% of each run, Pallas kernels for 59% -> 60%
where the time goes in v4:
time: 619 us; the launch traced here: 609 us
  Pallas kernels  450 us (73%)
  matrix products  78.3 us (13%)
  other arithmetic  38.1 us (6%)
  local copies, waits for them, and re-layouts  18.9 us (3%)
  between operations  14.9 us (2%)
    pallas_call x1, Pallas kernels, reduce_gradients(): pl.pallas_call(functools.partial(reduce_kernel, (chunks, counts, inner, d...  258 us
    pallas_call x1, Pallas kernels, gather_inputs(): pl.pallas_call(functools.partial(gather_kernel, full_inner, inner), in_sp...  83.6 us
    pallas_call x1, Pallas kernels, mix_backward(): pl.pallas_call(functools.partial(backward_kernel, dims), grid=(total // t...  71.3 us
    dot_general x2, matrix products, contract_cols(): lax.dot_general(left, right, (((1,), (1,)), ((), ())), precision=precisio...  45.5 us
    pallas_call x1, Pallas kernels, mix_forward(): pl.pallas_call(functools.partial(forward_kernel, dims), grid=(total // to...  36.6 us
    dot_general x1, matrix products, contract_rows(): lax.dot_general(left, right, (((0,), (0,)), ((), ())), precision=precisio...  12.8 us
  transfers between devices with their start and end apart: 8, of which 3 were waited for; matrix products, arithmetic and copies ran while one was open for 15% of the time, Pallas kernels for 60%

profile of v4, /device:TPU:0, one launch (start us, length us, event | category | flops | bytes accessed | tf_op | source)
XLA Modules:
  0.0 608.6 jit_solution(11452824462035764378)
XLA Ops:
  7.2 0.8 reshape.187
  8.0 1.3 fusion.19.small_ref
  9.3 83.6 %gather_inputs.1 = (bf16[2048,2048]{1,0:T(8,128)(2,1)}, s32[4,4,128]{2,1,0:T(4,128)}, f32[4,48,128]{2,1,0:T(8,128)}, bf16[2368,2048]{1,0:T(8,128)(2,1)}) custom-call(bf16[512,2048]{1,0:T(8,128)(2,1)} %bitcast.86, s32[4,128]{1,0:T(4,128)} %bitcast.128, f32[48,128]{1,0:T(8,128)} %fusion.19.small_ref, bf16[8512,512]{1,0:T(8,128)(2,1)} %bitcast.87), custom_call_target="tpu_custom_call" | custom-call | bytes 209715200 | tf_op jit(solution)/shard_map/gather_inputs/pallas_call | solution.py:591
  92.9 1.7 collective-permute-start
  95.2 2.5 broadcast_in_dim_reshape.8.seg_col_ref
  98.7 0.9 copy.100
  100.7 28.7 %fusion.31.proj_ref = f32[2048,2368]{1,0:T(8,128)} fusion(bf16[2048,2048]{1,0:T(8,128)(2,1)} %get-tuple-element.40.scaled_ref, bf16[2368,2048]{1,0:T(8,128)(2,1)} %get-tuple-element.41.cols_ref), kind=kOutput, calls=%fused_computation.81 | convolution fusion | flops 19864223744 | bytes 37486592 | tf_op jit(solution)/shard_map/dot_general | solution.py:26
  131.0 1.1 pad_convert_fusion.mask_ref
  132.7 36.6 %mix_forward.1 = (bf16[2048,1024]{1,0:T(8,128)(2,1)}, f32[2048,1]{1,0:T(8,128)}, bf16[2048,1024]{1,0:T(8,128)(2,1)}) custom-call(s32[1]{0:T(128)} %bitcast.5.own_ref, f32[2048,2368]{1,0:T(8,128)} %fusion.31.proj_ref, s32[8,256,1]{2,1,0:T(8,128)} %broadcast_in_dim_reshape.8.seg_col_ref, s32[8,1,256]{2,1,0:T(1,128)} %bitcast.106, ...), custom_call_target="tpu_custom_call" | custom-call | flops 2147483648 | bytes 19398656 | tf_op jit(solution)/shard_map/mix_forward/pallas_call | solution.py:291
  169.4 1.6 reduce.2
  171.0 2.9 collective-permute-done.2
  173.9 16.9 %fusion = (f32[2048]{0:T(1024)S(1)}, f32[2048,1024]{1,0:T(8,128)}) fusion(bf16[2048,1024]{1,0:T(8,128)(2,1)} %get-tuple-element.45, bf16[1024,2048]{1,0:T(8,128)(2,1)} %param.23, bf16[512,2048]{1,0:T(8,128)(2,1)} %collective-permute-done.2, bf16[512,2048]{1,0:T(8,128)(2,1)} %collective-permute-done.1, bf16[512,2048]{1,0:T(8,128)(2,1)} %collective-permute-done, ...), kind=kOutput, calls=%fused_computation.3 | convolution fusion | flops 8629778432 | bytes 25174016 | tf_op jit(solution)/shard_map/dot_general | solution.py:26
  191.0 1.0 collective-permute-done.3
  192.3 1.0 collective-permute-start.4
  193.4 9.3 %convolution_convert_fusion.1 = bf16[1024,2048]{1,0:T(8,128)(2,1)} fusion(bf16[1024,2048]{1,0:T(8,128)(2,1)} %param.23, bf16[2048,1024]{1,0:T(8,128)(2,1)} %get-tuple-element.45), kind=kOutput, calls=%fused_computation.18 | convolution fusion | flops 4297064448 | bytes 10485760 | tf_op jit(solution)/shard_map/dot_general | solution.py:1252
  202.9 2.9 fusion.1
  205.9 12.8 %convolution_convert_fusion = bf16[1024,2048]{1,0:T(8,128)(2,1)} fusion(bf16[2048,1024]{1,0:T(8,128)(2,1)S(1)} %fusion.1, bf16[512,2048]{1,0:T(8,128)(2,1)} %collective-permute-done.2, bf16[512,2048]{1,0:T(8,128)(2,1)} %collective-permute-done.1, bf16[512,2048]{1,0:T(8,128)(2,1)} %collective-permute-done, bf16[512,2048]{1,0:T(8,128)(2,1)S(1)} %bitcast.95), kind=kOutput, calls=%fused_computation.17 | convolution fusion | flops 8625586176 | bytes 16777216 | tf_op jit(solution)/shard_map/dot_general | solution.py:20
  218.9 1.4 copy-done
  220.9 1.4 copy.88.stats_ref
  222.2 71.3 %mix_backward.1 = (bf16[2048,2368]{1,0:T(8,128)(2,1)}, f32[8,1280]{1,0:T(8,128)}, f32[8,1024]{1,0:T(8,128)}, f32[8,128]{1,0:T(8,128)}) custom-call(s32[1]{0:T(128)} %bitcast.5.own_ref, f32[2048,2368]{1,0:T(8,128)} %fusion.31.proj_ref, s32[8,256,1]{2,1,0:T(8,128)} %broadcast_in_dim_reshape.8.seg_col_ref, s32[8,1,256]{2,1,0:T(1,128)} %bitcast.107, ...), custom_call_target="tpu_custom_call" | custom-call | flops 6442450944 | bytes 29097984 | tf_op jit(solution)/shard_map/mix_backward/pallas_call | solution.py:321
  293.6 0.8 fusion.30
  295.3 0.8 slice_dynamic-update-slice_fusion
  296.1 10.7 %add_convert_fusion = bf16[1024,2048]{1,0:T(8,128)(2,1)} fusion(bf16[1024,2048]{1,0:T(8,128)(2,1)} %collective-permute-done.5, bf16[1024,2048]{1,0:T(8,128)(2,1)} %param.23, bf16[2048,1024]{1,0:T(8,128)(2,1)} %get-tuple-element.45), kind=kOutput, calls=%fused_computation.6 | convolution fusion | flops 4301258752 | bytes 14680064 | tf_op jit(solution)/shard_map/dot_general | solution.py:1259
  307.5 0.8 slice_bitcast_fusion.3
  309.3 258.3 %reduce_gradients.1 = (bf16[8,1024,512]{2,1,0:T(8,128)(2,1)}, bf16[320,512]{1,0:T(8,128)(2,1)}, bf16[512,2048]{1,0:T(8,128)(2,1)}, bf16[512,2048]{1,0:T(8,128)(2...) custom-call(bf16[2048,2368]{1,0:T(8,128)(2,1)} %get-tuple-element.54, ...), custom_call_target="tpu_custom_call" | custom-call | flops 39728447488 | bytes 629145600 | tf_op jit(solution)/shard_map/reduce_gradients/pallas_call | solution.py:1078
  567.6 0.9 slice.126
  568.6 1.5 dynamic-slice.5
  570.8 1.4 fusion.29
  573.5 3.2 fusion.3
  577.5 6.9 %fusion.4 = (f32[512,2048]{1,0:T(8,128)}, bf16[512,2048]{1,0:T(8,128)(2,1)}) fusion(bf16[512,2048]{1,0:T(8,128)(2,1)S(1)} %copy-done.2, bf16[512,2048]{1,0:T(8,128)(2,1)S(1)} %copy-done.1, f32[512]{0:T(512)S(1)} %fusion.24, f32[2048]{0:T(1024)S(1)} %bitcast.116, f32[512]{0:T(512)S(1)} %bitcast.124, bf16[2,1,256,2048]{3,2,1,0:T(8,128)(2,1)S(1)} %copy-done.4, ...), kind=kLoop, calls=%fused_computation.12 | loop fusion | flops 16777216 | bytes 18888704 | tf_op jit(solution)/shard_map/sub | solution.py:1312
  584.4 10.3 %convert_bitcast_fusion = f32[512,8512]{0,1:T(8,128)} fusion(bf16[320,512]{1,0:T(8,128)(2,1)S(1)} %copy-done.5, bf16[8192,512]{1,0:T(8,128)(2,1)S(1)} %bitcast.90), kind=kLoop, calls=%fused_computation | loop fusion | flops 17432576 | bytes 26148864 | tf_op jit(solution)/shard_map/transpose | solution.py:1288
  594.7 6.7 %convert_element_type.99 = f32[1024,2048]{1,0:T(8,128)} convert(bf16[1024,2048]{1,0:T(8,128)(2,1)} %all-gather.2.cloned.1.call-done) | non-fusion elementwise | flops 2097152 | bytes 12582912 | tf_op jit(solution)/shard_map/convert_element_type | solution.py:1266
  (101 shorter events, 11.6 us)
Async XLA Ops:
  7.2 300.4 %reduce-scatter.2.cloned.1.call-start = ((), (), s32[]{:S(2)}) async-start(), calls=%async_computation.1 | async-start | bytes 4718592 | tf_op jit(solution)/shard_map/reduce_scatter | solution.py:1258
  9.3 83.6 %copy-start.3 = (bf16[2,1,256,2048]{3,2,1,0:T(8,128)(2,1)S(1)}, bf16[2,1,256,2048]{3,2,1,0:T(8,128)(2,1)}, u32[]{:S(2)}) copy-start(bf16[2,1,256,2048]{3,2,1,0:T(8,128)(2,1)} %param.14) | copy-start | bytes 6291460
  92.9 76.4 %collective-permute-start = (bf16[512,2048]{1,0:T(8,128)(2,1)S(1)}, bf16[512,2048]{1,0:T(8,128)(2,1)}, u32[]{:S(2)}, u32[]{:S(2)}) collective-permute-start(bf16[512,2048]{1,0:T(8,128)(2,1)S(1)} %bitcast.92), channel_id=1, source_target_pairs={{0,2},{1,3},{2,0},{3,1},{4,6},{5,7},{6,4},{7,5},{8,10},{9,11},{10,... | collective-permute-start | bytes 6291464 | tf_op jit(solution)/shard_map/ppermute | solution.py:379
  94.7 76.3 %collective-permute-start.1 = (bf16[512,2048]{1,0:T(8,128)(2,1)S(1)}, bf16[512,2048]{1,0:T(8,128)(2,1)}, u32[]{:S(2)}, u32[]{:S(2)}) collective-permute-start(bf16[512,2048]{1,0:T(8,128)(2,1)S(1)} %bitcast.93), channel_id=1, source_target_pairs={{0,1},{1,0},{2,3},{3,2},{4,5},{5,4},{6,7},{7,6},{8,9},{9,8},{10,11... | collective-permute-start | bytes 6291464 | tf_op jit(solution)/shard_map/ppermute | solution.py:379
  100.7 28.9 %copy-start.6 = (bf16[1024]{0:T(1024)(128)(2,1)S(1)}, bf16[1024]{0:T(1024)(128)(2,1)}, u32[]{:S(2)}) copy-start(bf16[1024]{0:T(1024)(128)(2,1)} %param.22) | copy-start | bytes 6148
  100.7 28.9 %copy-start.7 = (bf16[16]{0:T(256)(128)(2,1)S(1)}, bf16[16]{0:T(256)(128)(2,1)}, u32[]{:S(2)}) copy-start(bf16[16]{0:T(256)(128)(2,1)} %param.21) | copy-start | bytes 100
  100.7 29.1 %copy-start.8 = (bf16[16]{0:T(256)(128)(2,1)S(1)}, bf16[16]{0:T(256)(128)(2,1)}, u32[]{:S(2)}) copy-start(bf16[16]{0:T(256)(128)(2,1)} %param.20) | copy-start | bytes 100
  100.7 29.1 %copy-start.9 = (bf16[16]{0:T(256)(128)(2,1)S(1)}, bf16[16]{0:T(256)(128)(2,1)}, u32[]{:S(2)}) copy-start(bf16[16]{0:T(256)(128)(2,1)} %param.19) | copy-start | bytes 100
  169.3 4.6 collective-permute-start.2
  190.8 1.2 collective-permute-start.3
  192.3 10.3 %collective-permute-start.4 = (f32[2,2048]{1,0:T(2,128)S(1)}, f32[2,2048]{1,0:T(2,128)S(1)}, u32[]{:S(2)}, u32[]{:S(2)}) collective-permute-start(f32[2,2048]{1,0:T(2,128)S(1)} %fusion.27), channel_id=1, source_target_pairs={{0,2},{1,3},{2,0},{3,1},{4,6},{5,7},{6,4},{7,5},{8,10},{9,11},{10,... | collective-permute-start | bytes 49160 | tf_op jit(solution)/shard_map/ppermute | solution.py:379
  218.7 1.6 copy-start
  218.7 375.9 %all-gather.2.cloned.1.call-start = ((), (), s32[]{:S(2)}) async-start(), calls=%async_computation.2 | async-start | bytes 4718592 | tf_op jit(solution)/shard_map/all_gather | solution.py:1266
  218.8 77.3 %collective-permute-start.5 = (bf16[1024,2048]{1,0:T(8,128)(2,1)}, bf16[1024,2048]{1,0:T(8,128)(2,1)}, u32[]{:S(2)}, u32[]{:S(2)}) collective-permute-start(bf16[1024,2048]{1,0:T(8,128)(2,1)} %convolution_convert_fusion.1), channel_id=1, source_target_pairs={{0,1},{1,0},{2,3},{3,2},{4,5},{5,4},{6,7},{7,6},{8,9},{9,8},{10,11... | collective-permute-start | bytes 12582920 | tf_op jit(solution)/shard_map/ppermute | solution.py:379
  568.5 8.9 %copy-start.1 = (bf16[512,2048]{1,0:T(8,128)(2,1)S(1)}, bf16[512,2048]{1,0:T(8,128)(2,1)}, u32[]{:S(2)}) copy-start(bf16[512,2048]{1,0:T(8,128)(2,1)} %get-tuple-element.59) | copy-start | bytes 6291460
  568.5 8.9 %copy-start.2 = (bf16[512,2048]{1,0:T(8,128)(2,1)S(1)}, bf16[512,2048]{1,0:T(8,128)(2,1)}, u32[]{:S(2)}) copy-start(bf16[512,2048]{1,0:T(8,128)(2,1)} %get-tuple-element.60) | copy-start | bytes 6291460
  568.5 8.9 %copy-start.4 = (bf16[2,1,256,2048]{3,2,1,0:T(8,128)(2,1)S(1)}, bf16[2,1,256,2048]{3,2,1,0:T(8,128)(2,1)}, u32[]{:S(2)}) copy-start(bf16[2,1,256,2048]{3,2,1,0:T(8,128)(2,1)} %param.14) | copy-start | bytes 6291460
  577.5 6.9 %slice-start = ((s8[8388608]{0:T(1024)(128)(4,1)}), s8[4194304]{0:T(1024)(128)(4,1)S(1)}, s32[]{:S(2)}) async-start(s8[8388608]{0:T(1024)(128)(4,1)} %bitcast.88), calls=%async_computation.3 | async-start | bytes 8388608
  577.5 6.9 %slice-start.1 = ((s8[8388608]{0:T(1024)(128)(4,1)}), s8[4194304]{0:T(1024)(128)(4,1)S(1)}, s32[]{:S(2)}) async-start(s8[8388608]{0:T(1024)(128)(4,1)} %bitcast.88), calls=%async_computation.4 | async-start | bytes 8388608
  577.5 6.9 %copy-start.5 = (bf16[320,512]{1,0:T(8,128)(2,1)S(1)}, bf16[320,512]{1,0:T(8,128)(2,1)}, u32[]{:S(2)}) copy-start(bf16[320,512]{1,0:T(8,128)(2,1)} %get-tuple-element.63) | copy-start | bytes 983044
Sparse Core Ops, SparseCore 0:
  218.9 88.6 reduce-scatter.1
  309.9 117.5 all-gather.1

commit v5 on v4

--- a/solution.py
+++ b/solution.py
@@ -259,15 +259,15 @@
     gp_ref[:, common + state2 : common + state2 + heads] = placed[:, :heads].astype(BF16)
 
 
-def mixer_specs(dims, width):
+def mixer_specs(dims, width, start=0):
     tokens, inner, state2, heads, local_heads, taps = dims
     fixed = lambda shape: pl.BlockSpec(shape, lambda s: (0,) * len(shape))
     in_specs = [
         pl.BlockSpec(memory_space=pltpu.SMEM),
-        pl.BlockSpec((tokens, width), lambda s: (s, 0)),
-        pl.BlockSpec((None, tokens, 1), lambda s: (s, 0, 0)),
-        pl.BlockSpec((None, 1, tokens), lambda s: (s, 0, 0)),
-        pl.BlockSpec((None, tokens, 8), lambda s: (s, 0, 0)),
+        pl.BlockSpec((tokens, width), lambda s: (s + start, 0)),
+        pl.BlockSpec((None, tokens, 1), lambda s: (s + start, 0, 0)),
+        pl.BlockSpec((None, 1, tokens), lambda s: (s + start, 0, 0)),
+        pl.BlockSpec((None, tokens, 8), lambda s: (s + start, 0, 0)),
         fixed((8, LANES)),
         fixed((8, inner + state2)),
         fixed((8, inner)),
@@ -313,18 +313,18 @@
     )(*operands)
 
 
-def mix_backward(dims, operands, stats, grad_normed, scan_out):
+def mix_backward(dims, operands, stats, grad_normed, scan_out, start, count):
     tokens, inner, state2, heads, local_heads, taps = dims
-    total, width = operands[1].shape
-    in_specs, scratch = mixer_specs(dims, width)
+    total, width = count * tokens, operands[1].shape[1]
+    in_specs, scratch = mixer_specs(dims, width, start)
     fixed = lambda shape: pl.BlockSpec(shape, lambda s: (0,) * len(shape))
     return pl.pallas_call(
         functools.partial(backward_kernel, dims),
-        grid=(total // tokens,),
+        grid=(count,),
         in_specs=in_specs + [
-            pl.BlockSpec((tokens, 2), lambda s: (s, 0)),
-            pl.BlockSpec((tokens, inner), lambda s: (s, 0)),
-            pl.BlockSpec((tokens, inner), lambda s: (s, 0)),
+            pl.BlockSpec((tokens, 2), lambda s: (s + start, 0)),
+            pl.BlockSpec((tokens, inner), lambda s: (s + start, 0)),
+            pl.BlockSpec((tokens, inner), lambda s: (s + start, 0)),
         ],
         out_specs=[
             pl.BlockSpec((tokens, width), lambda s: (s, 0)),
@@ -628,6 +628,7 @@
 ROW_BLOCK = 256
 LANE_TILE = 1024
 PER_TURN = 3
+AGAIN = 1
 TOKEN_PIECES = 8
 
 
@@ -641,7 +642,7 @@
     counts = {}
     placed = []
     for number, (kind, start, rows) in enumerate(pieces):
-        order = "lift" if number % 4 == 2 else "side"
+        order = "lift" if number % 3 == 2 else "side"
         key = (kind == "shared", rows, order)
         where = counts.get(key, 0)
         counts[key] = where + 1
@@ -649,7 +650,7 @@
     return placed, counts
 
 
-def reduce_kernel(plan, gp_ref, scaled_ref, cols_ref, tok_out_ref, small_ref,
+def reduce_kernel(plan, gp_first_ref, gp_last_ref, scaled_ref, cols_ref, tok_out_ref, small_ref,
                   sum_in_ref, sum_shared_ref, got_out_ref, own_grad_ref, got_grad_ref, small_sum_ref,
                   far_land_ref, across_ref, *scratch):
     chunks, counts, inner, depth, common, norm_row = plan
@@ -683,14 +684,25 @@
     column_loads = []
     columns_done = []
 
+    first_rows = gp_first_ref.shape[0]
+    all_rows = first_rows + gp_last_ref.shape[0]
+
     def load_columns(number):
         if number < len(column_blocks):
             start, count = column_blocks[number]
-            copy = pltpu.make_async_copy(
-                gp_ref.at[:, pl.ds(start, count)], gp_cols.at[:, pl.ds(0, count)], load_sems.at[2]
-            )
-            copy.start()
-            column_loads.append(copy)
+            lanes = pl.ds(0, count)
+            copies = [
+                pltpu.make_async_copy(
+                    gp_first_ref.at[:, pl.ds(start, count)], gp_cols.at[pl.ds(0, first_rows), lanes], load_sems.at[2]
+                ),
+                pltpu.make_async_copy(
+                    gp_last_ref.at[:, pl.ds(start, count)],
+                    gp_cols.at[pl.ds(first_rows, all_rows - first_rows), lanes], load_sems.at[5],
+                ),
+            ]
+            for copy in copies:
+                copy.start()
+            column_loads.append(copies)
 
     def next_columns():
         number = len(columns_done)
@@ -698,7 +710,8 @@
             return
         start, count = column_blocks[number]
         need(0)
-        column_loads[number].wait()
+        for copy in column_loads[number]:
+            copy.wait()
         gp_flipped[pl.ds(0, count), :] = gp_cols[:, pl.ds(0, count)].T
         load_columns(number + 1)
 
@@ -757,7 +770,7 @@
             copy.wait()
 
     def row_products():
-        half_blocks = gp_ref.shape[0] // (2 * rows_of_block)
+        half_blocks = all_rows // (2 * rows_of_block)
         quarter_blocks = half_blocks // 2
         later = list(range(quarter_blocks, half_blocks))
         sooner = list(range(quarter_blocks))
@@ -770,7 +783,11 @@
             if number < len(order):
                 far, block = order[number]
                 at = (half_blocks + block if far else block) * rows_of_block
-                copy = pltpu.make_async_copy(gp_ref.at[pl.ds(at, rows_of_block)], gp_rows, load_sems.at[3])
+                if at < first_rows:
+                    source = gp_first_ref.at[pl.ds(at, rows_of_block)]
+                else:
+                    source = gp_last_ref.at[pl.ds(at - first_rows, rows_of_block)]
+                copy = pltpu.make_async_copy(source, gp_rows, load_sems.at[3])
                 copy.start()
                 row_loads.append((copy, at))
 
@@ -961,6 +978,11 @@
             for copy in trade:
                 copy.start()
             own.start()
+
+        yield AGAIN
+
+        @pl.when(inside)
+        def _():
             own.wait()
             for copy in trade:
                 copy.wait_recv()
@@ -1027,13 +1049,16 @@
     active, extra = [], [smalls(), activations()]
 
     def advance(running):
-        still = []
+        still, again = [], []
         for steps in running:
             try:
-                next(steps)
+                if next(steps) == AGAIN:
+                    again.append(steps)
                 still.append(steps)
             except StopIteration:
                 pass
+        for steps in again:
+            next(steps)
         return still
 
     while waiting or active:
@@ -1045,7 +1070,7 @@
         extra = advance(extra)
 
 
-def reduce_gradients(size, depth, inner, common, norm_row, gp, scaled, cols, tok_out, small):
+def reduce_gradients(size, depth, inner, common, norm_row, gp_first, gp_last, scaled, cols, tok_out, small):
     total, width = scaled.shape
     own_rows = tok_out.shape[1]
     chunks, counts = reduce_chunks(inner, common)
@@ -1064,20 +1089,20 @@
         pltpu.VMEM(cols.shape, BF16),
         pltpu.VMEM((total, max(common, COLUMN_BLOCK)), BF16),
         pltpu.VMEM((max(common, COLUMN_BLOCK), total), BF16),
-        pltpu.VMEM((ROW_BLOCK, gp.shape[1]), BF16),
+        pltpu.VMEM((ROW_BLOCK, gp_first.shape[1]), BF16),
         pltpu.VMEM((2, ROW_BLOCK, width), BF16),
         pltpu.VMEM((ROW_BLOCK, width), BF16),
         pltpu.VMEM((1, width), F32),
         sems((len(chunks), SLOTS)), sems((len(chunks), SLOTS)), sems((len(chunks),)),
         sems((2, TOKEN_PIECES)), sems((2, TOKEN_PIECES)), sems((5,)), sems((5,)), sems((3,)), sems((3,)),
-        sems((half_blocks,)), sems((half_blocks,)), sems((5,)), sems((half_blocks,)),
+        sems((half_blocks,)), sems((half_blocks,)), sems((6,)), sems((half_blocks,)),
     ]
     anywhere = pl.BlockSpec(memory_space=pltpu.HBM)
     local = pl.BlockSpec(memory_space=pltpu.VMEM)
     own = jax.ShapeDtypeStruct((own_rows, width), BF16)
     return pl.pallas_call(
         functools.partial(reduce_kernel, (chunks, counts, inner, depth, common, norm_row)),
-        in_specs=[anywhere] * 4 + [local],
+        in_specs=[anywhere] * 5 + [local],
         out_specs=[anywhere] * 5 + [local] + [anywhere] * 2,
         out_shape=[
             jax.ShapeDtypeStruct((2 * size, inner, depth), BF16),
@@ -1092,10 +1117,10 @@
             collective_id=0, has_side_effects=True, vmem_limit_bytes=VMEM_LIMIT
         ),
         cost_estimate=pl.CostEstimate(
-            flops=4 * total * gp.shape[1] * width, bytes_accessed=600 << 20, transcendentals=0
+            flops=total * width, bytes_accessed=1 << 20, transcendentals=0
         ),
         name="reduce_gradients",
-    )(gp, scaled, cols, tok_out, small)
+    )(gp_first, gp_last, scaled, cols, tok_out, small)
 
 
 def small_pieces(size, copies, depth, inner, columns, me, replica, scaled_low, gp, normed_low, cot_all):
@@ -1240,30 +1265,42 @@
     if fused:
         cot_across, squares = lax.optimization_barrier((cot_across, squares))
         cot_all = jnp.concatenate([own_cot, cot_across, cot_beside, swap(cot_across, "fsdp", size, 1)], 0)
-    grad_normed = contract_cols(cot_all, w_out)
-    cross = jnp.sum(gated.astype(F32) * grad_normed, 1)
-    stats = sum_tokens(jnp.stack([squares[:, 0], cross]), "fsdp", size)
-    root = lax.rsqrt(stats[0] / full_inner + EPS)
-    pull = root * root * root * stats[1] / full_inner
-
+    twice = lambda row: jnp.stack([row, row])
+    root = lax.rsqrt(sum_tokens(twice(squares[:, 0]), "fsdp", size)[0] / full_inner + EPS)
     normed_low = (gated.astype(F32) * root[:, None]).astype(BF16)
+    w_later = w_out
     if fused:
         near = total // 2
         far_out = jnp.dot(gated[near:], w_out, preferred_element_type=F32).astype(BF16)
         normed_low, far_out = lax.optimization_barrier((normed_low, far_out))
         far_out = swap(far_out, "fsdp", size, 1)
         grad_out = contract_rows(normed_low, cot_all).astype(BF16)
-        head_rows, grad_out = lax.optimization_barrier((head_rows, grad_out))
-        operands = operands[:5] + (head_rows,) + operands[6:]
+        w_later, grad_out = lax.optimization_barrier((w_out, grad_out))
         own_out = lax.psum_scatter(grad_out, "replica", scatter_dimension=0, tiled=True)
+    grad_normed = contract_cols(cot_all, w_later)
+    cross = jnp.sum(gated.astype(F32) * grad_normed, 1)
+    pull = root * root * root * sum_tokens(twice(cross), "fsdp", size)[0] / full_inner
+
+    sequences = total // tokens
+    stats = jnp.stack([root, pull], 1)
+    if fused:
+        early = sequences * 3 // 4
+        gp_first, *small_first = mix_backward(dims, operands, stats, grad_normed, scan_out, 0, early)
         tok_out = jnp.dot(gated[:near], w_out, preferred_element_type=F32) + far_out.astype(F32)
         tok_out = tok_out.astype(BF16).reshape(2, own_rows, width)
-    gp, grad_conv, grad_chan, grad_head = mix_backward(
-        dims, operands, jnp.stack([root, pull], 1), grad_normed, scan_out
-    )
-    if fused:
-        own_out, grad_head, tok_out = lax.optimization_barrier((own_out, grad_head, tok_out))
+        head_rows, own_out, small_first[2], tok_out = lax.optimization_barrier(
+            (head_rows, own_out, small_first[2], tok_out)
+        )
         grad_w_out = lax.all_gather(own_out, "replica", axis=0, tiled=True).astype(F32)
+        operands = operands[:5] + (head_rows,) + operands[6:]
+        gp_last, *small_last = mix_backward(
+            dims, operands, stats, grad_normed, scan_out, early, sequences - early
+        )
+        grad_conv, grad_chan, grad_head = [first + last for first, last in zip(small_first, small_last)]
+    else:
+        gp, grad_conv, grad_chan, grad_head = mix_backward(
+            dims, operands, stats, grad_normed, scan_out, 0, sequences
+        )
     own_wide = own_x.astype(F32)
     own_root = normalise(own_x)
 
@@ -1283,7 +1320,7 @@
         vector = jnp.concatenate([conv_padded, jnp.zeros((width,), F32), spread.reshape(-1)])
         vector = jnp.pad(vector, (0, -vector.shape[0] % (8 * LANES))).reshape(-1, LANES)
         sum_in, sum_shared, got_out, own_grad, got_grad, vector, _, _ = reduce_gradients(
-            size, depth, inner, common, norm_row, gp, scaled_low, w_cols, tok_out, vector
+            size, depth, inner, common, norm_row, gp_first, gp_last, scaled_low, w_cols, tok_out, vector
         )
         grad_w_in = jnp.concatenate([sum_in.reshape(2 * full_inner, depth), sum_shared], 0).astype(F32).T
         out_sum = tok_out[0].astype(F32) + got_out.astype(F32)

time: 619 us -> 605 us (0.977)
  Pallas kernels: 450 us -> 437 us
    pallas_call x1, Pallas kernels: 258 us -> 242 us  [reduce_gradients(): pl.pallas_call(functools.partial(reduce_kernel, (chunks, counts, inner, d...]
    pallas_call x1 -> x2, Pallas kernels: 71.3 us -> 75.2 us  [mix_backward(): pl.pallas_call(functools.partial(backward_kernel, dims), grid=(count,), i...]
  transfers between devices with their start and end apart: 8 -> 10, of which waited for: 3 -> 3; matrix products, arithmetic and copies ran while one was open for 15% -> 19% of each run, Pallas kernels for 60% -> 59%
where the time goes in v5:
time: 605 us; the launch traced here: 596 us
  Pallas kernels  437 us (72%)
  matrix products  78.4 us (13%)
  other arithmetic  40.6 us (7%)
  local copies, waits for them, and re-layouts  15.1 us (2%)
  between operations  15 us (2%)
    pallas_call x1, Pallas kernels, reduce_gradients(): pl.pallas_call(functools.partial(reduce_kernel, (chunks, counts, inner, d...  242 us
    pallas_call x1, Pallas kernels, gather_inputs(): pl.pallas_call(functools.partial(gather_kernel, full_inner, inner), in_sp...  83.6 us
    pallas_call x2, Pallas kernels, mix_backward(): pl.pallas_call(functools.partial(backward_kernel, dims), grid=(count,), i...  75.2 us
    dot_general x2, matrix products, contract_cols(): lax.dot_general(left, right, (((1,), (1,)), ((), ())), precision=precisio...  45.5 us
    pallas_call x1, Pallas kernels, mix_forward(): pl.pallas_call(functools.partial(forward_kernel, dims), grid=(total // to...  36.6 us
    dot_general x1, matrix products, contract_rows(): lax.dot_general(left, right, (((0,), (0,)), ((), ())), precision=precisio...  12.8 us
  transfers between devices with their start and end apart: 10, of which 3 were waited for; matrix products, arithmetic and copies ran while one was open for 19% of the time, Pallas kernels for 59%

profile of v5, /device:TPU:0, one launch (start us, length us, event | category | flops | bytes accessed | tf_op | source)
XLA Modules:
  0.0 596.1 jit_solution(2664185786801594910)
XLA Ops:
  7.2 0.8 reshape.199
  8.0 1.3 fusion.19.small_ref
  9.3 83.6 %gather_inputs.1 = (bf16[2048,2048]{1,0:T(8,128)(2,1)}, s32[4,4,128]{2,1,0:T(4,128)}, f32[4,48,128]{2,1,0:T(8,128)}, bf16[2368,2048]{1,0:T(8,128)(2,1)}) custom-call(bf16[512,2048]{1,0:T(8,128)(2,1)} %bitcast.90, s32[4,128]{1,0:T(4,128)} %bitcast.132, f32[48,128]{1,0:T(8,128)} %fusion.19.small_ref, bf16[8512,512]{1,0:T(8,128)(2,1)} %bitcast.93), custom_call_target="tpu_custom_call" | custom-call | bytes 209715200 | tf_op jit(solution)/shard_map/gather_inputs/pallas_call | solution.py:591
  93.0 1.7 collective-permute-start
  95.4 0.9 copy.116
  96.3 2.6 broadcast_in_dim_reshape.8.seg_col_ref
  99.7 28.7 %fusion.31.proj_ref = f32[2048,2368]{1,0:T(8,128)} fusion(bf16[2048,2048]{1,0:T(8,128)(2,1)} %get-tuple-element.45.scaled_ref, bf16[2368,2048]{1,0:T(8,128)(2,1)} %get-tuple-element.46.cols_ref), kind=kOutput, calls=%fused_computation.84 | convolution fusion | flops 19864223744 | bytes 37486592 | tf_op jit(solution)/shard_map/dot_general | solution.py:26
  130.4 1.1 pad_convert_fusion.mask_ref
  132.1 36.6 %mix_forward.1 = (bf16[2048,1024]{1,0:T(8,128)(2,1)}, f32[2048,1]{1,0:T(8,128)}, bf16[2048,1024]{1,0:T(8,128)(2,1)}) custom-call(s32[1]{0:T(128)} %bitcast.5.own_ref, f32[2048,2368]{1,0:T(8,128)} %fusion.31.proj_ref, s32[8,256,1]{2,1,0:T(8,128)} %broadcast_in_dim_reshape.8.seg_col_ref, s32[8,1,256]{2,1,0:T(1,128)} %bitcast.108, ...), custom_call_target="tpu_custom_call" | custom-call | flops 2147483648 | bytes 19398656 | tf_op jit(solution)/shard_map/mix_forward/pallas_call | solution.py:291
  168.7 1.6 reduce.2
  172.3 1.1 collective-permute-start.2
  173.3 9.3 %convolution_convert_fusion.1 = bf16[1024,2048]{1,0:T(8,128)(2,1)} fusion(bf16[1024,2048]{1,0:T(8,128)(2,1)} %param.23, bf16[2048,1024]{1,0:T(8,128)(2,1)} %get-tuple-element.50), kind=kOutput, calls=%fused_computation.18 | convolution fusion | flops 4297064448 | bytes 10485760 | tf_op jit(solution)/shard_map/dot_general | solution.py:1274
  182.9 2.9 fusion
  185.8 12.8 %convolution_convert_fusion = bf16[1024,2048]{1,0:T(8,128)(2,1)} fusion(bf16[2048,1024]{1,0:T(8,128)(2,1)S(1)} %fusion, bf16[512,2048]{1,0:T(8,128)(2,1)} %collective-permute-done.4, bf16[512,2048]{1,0:T(8,128)(2,1)} %collective-permute-done.3, bf16[512,2048]{1,0:T(8,128)(2,1)} %collective-permute-done, bf16[512,2048]{1,0:T(8,128)(2,1)S(1)} %bitcast.100), kind=kOutput, calls=%fused_computation.17 | convolution fusion | flops 8625586176 | bytes 16777216 | tf_op jit(solution)/shard_map/dot_general | solution.py:20
  198.8 16.9 %fusion.1 = (f32[2048]{0:T(1024)S(1)}, f32[2048,1024]{1,0:T(8,128)}) fusion(bf16[2048,1024]{1,0:T(8,128)(2,1)} %get-tuple-element.50, bf16[1024,2048]{1,0:T(8,128)(2,1)} %param.23, bf16[512,2048]{1,0:T(8,128)(2,1)} %collective-permute-done.4, bf16[512,2048]{1,0:T(8,128)(2,1)} %collective-permute-done.3, bf16[512,2048]{1,0:T(8,128)(2,1)} %collective-permute-done, ...), kind=kOutput, calls=%fused_computation.4 | convolution fusion | flops 8629778432 | bytes 25174016 | tf_op jit(solution)/shard_map/dot_general | solution.py:26
  216.2 0.8 collective-permute-done.5
  217.4 1.1 collective-permute-start.6
  218.5 2.7 collective-permute-done.6
  221.5 1.4 copy.99.stats_ref
  222.9 54.7 %mix_backward.2 = (bf16[1536,2368]{1,0:T(8,128)(2,1)}, f32[8,1280]{1,0:T(8,128)}, f32[8,1024]{1,0:T(8,128)}, f32[8,128]{1,0:T(8,128)}) custom-call(s32[1]{0:T(128)} %bitcast.5.own_ref, f32[2048,2368]{1,0:T(8,128)} %fusion.31.proj_ref, s32[8,256,1]{2,1,0:T(8,128)} %broadcast_in_dim_reshape.8.seg_col_ref, s32[8,1,256]{2,1,0:T(1,128)} %bitcast.109, ...), custom_call_target="tpu_custom_call" | custom-call | flops 4831838208 | bytes 21823488 | tf_op jit(solution)/shard_map/mix_backward/pallas_call | solution.py:321
  277.6 10.8 %add_convert_fusion = bf16[1024,2048]{1,0:T(8,128)(2,1)} fusion(bf16[1024,2048]{1,0:T(8,128)(2,1)} %collective-permute-done.7, bf16[1024,2048]{1,0:T(8,128)(2,1)} %param.23, bf16[2048,1024]{1,0:T(8,128)(2,1)} %get-tuple-element.50), kind=kOutput, calls=%fused_computation.6 | convolution fusion | flops 4301258752 | bytes 14680064 | tf_op jit(solution)/shard_map/dot_general | solution.py:1289
  289.0 20.5 %mix_backward.3 = (bf16[512,2368]{1,0:T(8,128)(2,1)}, f32[8,1280]{1,0:T(8,128)}, f32[8,1024]{1,0:T(8,128)}, f32[8,128]{1,0:T(8,128)}) custom-call(s32[1]{0:T(128)} %bitcast.5.own_ref, f32[2048,2368]{1,0:T(8,128)} %fusion.31.proj_ref, s32[8,256,1]{2,1,0:T(8,128)} %broadcast_in_dim_reshape.8.seg_col_ref, s32[8,1,256]{2,1,0:T(1,128)} %bitcast.110, ...), custom_call_target="tpu_custom_call" | custom-call | flops 1610612736 | bytes 7274496 | tf_op jit(solution)/shard_map/mix_backward/pallas_call | solution.py:321
  309.5 0.8 add.113
  310.3 0.8 add.115
  312.9 242.0 %reduce_gradients.1 = (bf16[8,1024,512]{2,1,0:T(8,128)(2,1)}, bf16[320,512]{1,0:T(8,128)(2,1)}, bf16[512,2048]{1,0:T(8,128)(2,1)}, bf16[512,2048]{1,0:T(8,128)(2...) custom-call(bf16[1536,2368]{1,0:T(8,128)(2,1)} %get-tuple-element.59, ...), custom_call_target="tpu_custom_call" | custom-call | flops 4194304 | bytes 1048576 | tf_op jit(solution)/shard_map/reduce_gradients/pallas_call | solution.py:1103
  554.9 0.9 slice.126
  555.9 1.5 dynamic-slice.5
  558.1 1.4 fusion.29
  560.8 3.2 fusion.3
  564.8 7.1 %fusion.4 = (f32[512,2048]{1,0:T(8,128)}, bf16[512,2048]{1,0:T(8,128)(2,1)}) fusion(bf16[512,2048]{1,0:T(8,128)(2,1)} %get-tuple-element.70, bf16[512,2048]{1,0:T(8,128)(2,1)S(1)} %copy-done.2, f32[512]{0:T(512)S(1)} %fusion.24, f32[2048]{0:T(1024)S(1)} %bitcast.118, f32[512]{0:T(512)S(1)} %bitcast.128, bf16[2,1,256,2048]{3,2,1,0:T(8,128)(2,1)} %param.14, ...), kind=kLoop, calls=%fused_computation.12 | loop fusion | flops 16777216 | bytes 18888704 | tf_op jit(solution)/shard_map/sub | solution.py:1349
  571.9 10.3 %convert_bitcast_fusion = f32[512,8512]{0,1:T(8,128)} fusion(bf16[320,512]{1,0:T(8,128)(2,1)S(1)} %copy-done.4, bf16[8192,512]{1,0:T(8,128)(2,1)S(1)} %bitcast.96), kind=kLoop, calls=%fused_computation | loop fusion | flops 17432576 | bytes 26148864 | tf_op jit(solution)/shard_map/transpose | solution.py:1325
  582.2 6.7 %convert_element_type.99 = f32[1024,2048]{1,0:T(8,128)} convert(bf16[1024,2048]{1,0:T(8,128)(2,1)} %all-gather.2.cloned.1.call-done) | non-fusion elementwise | flops 2097152 | bytes 12582912 | tf_op jit(solution)/shard_map/convert_element_type | solution.py:1294
  (121 shorter events, 12.9 us)
Async XLA Ops:
  7.2 281.2 %reduce-scatter.2.cloned.1.call-start = ((), (), s32[]{:S(2)}) async-start(), calls=%async_computation.1 | async-start | bytes 4718592 | tf_op jit(solution)/shard_map/reduce_scatter | solution.py:1279
  9.3 83.7 %copy-start.3 = (bf16[2,1,256,2048]{3,2,1,0:T(8,128)(2,1)S(1)}, bf16[2,1,256,2048]{3,2,1,0:T(8,128)(2,1)}, u32[]{:S(2)}) copy-start(bf16[2,1,256,2048]{3,2,1,0:T(8,128)(2,1)} %param.14) | copy-start | bytes 6291460
  9.3 89.6 %copy-start.8 = (bf16[1024]{0:T(1024)(128)(2,1)S(1)}, bf16[1024]{0:T(1024)(128)(2,1)}, u32[]{:S(2)}) copy-start(bf16[1024]{0:T(1024)(128)(2,1)} %param.22) | copy-start | bytes 6148
  9.3 89.6 %copy-start.9 = (bf16[16]{0:T(256)(128)(2,1)S(1)}, bf16[16]{0:T(256)(128)(2,1)}, u32[]{:S(2)}) copy-start(bf16[16]{0:T(256)(128)(2,1)} %param.21) | copy-start | bytes 100
  93.0 75.7 %collective-permute-start = (bf16[512,2048]{1,0:T(8,128)(2,1)S(1)}, bf16[512,2048]{1,0:T(8,128)(2,1)}, u32[]{:S(2)}, u32[]{:S(2)}) collective-permute-start(bf16[512,2048]{1,0:T(8,128)(2,1)S(1)} %bitcast.98), channel_id=1, source_target_pairs={{0,2},{1,3},{2,0},{3,1},{4,6},{5,7},{6,4},{7,5},{8,10},{9,11},{10,... | collective-permute-start | bytes 6291464 | tf_op jit(solution)/shard_map/ppermute | solution.py:379
  99.7 29.5 %copy-start.10 = (bf16[16]{0:T(256)(128)(2,1)S(1)}, bf16[16]{0:T(256)(128)(2,1)}, u32[]{:S(2)}) copy-start(bf16[16]{0:T(256)(128)(2,1)} %param.19) | copy-start | bytes 100
  99.7 29.5 %copy-start.11 = (bf16[16]{0:T(256)(128)(2,1)S(1)}, bf16[16]{0:T(256)(128)(2,1)}, u32[]{:S(2)}) copy-start(bf16[16]{0:T(256)(128)(2,1)} %param.20) | copy-start | bytes 100
  170.3 1.5 collective-permute-start.1
  170.9 14.9 %collective-permute-start.3 = (bf16[512,2048]{1,0:T(8,128)(2,1)S(1)}, bf16[512,2048]{1,0:T(8,128)(2,1)}, u32[]{:S(2)}, u32[]{:S(2)}) collective-permute-start(bf16[512,2048]{1,0:T(8,128)(2,1)S(1)} %bitcast.99), channel_id=1, source_target_pairs={{0,1},{1,0},{2,3},{3,2},{4,5},{5,4},{6,7},{7,6},{8,9},{9,8},{10,11... | collective-permute-start | bytes 6291464 | tf_op jit(solution)/shard_map/ppermute | solution.py:379
  171.0 14.8 %collective-permute-start.4 = (bf16[512,2048]{1,0:T(8,128)(2,1)}, bf16[512,2048]{1,0:T(8,128)(2,1)}, u32[]{:S(2)}, u32[]{:S(2)}) collective-permute-start(bf16[512,2048]{1,0:T(8,128)(2,1)} %collective-permute-done), channel_id=1, source_target_pairs={{0,1},{1,0},{2,3},{3,2},{4,5},{5,4},{6,7},{7,6},{8,9},{9,8},{10,11... | collective-permute-start | bytes 6291464 | tf_op jit(solution)/shard_map/ppermute | solution.py:379
  172.3 10.3 %collective-permute-start.2 = (f32[2,2048]{1,0:T(2,128)S(1)}, f32[2,2048]{1,0:T(2,128)S(1)}, u32[]{:S(2)}, u32[]{:S(2)}) collective-permute-start(f32[2,2048]{1,0:T(2,128)S(1)} %fusion.28), channel_id=1, source_target_pairs={{0,2},{1,3},{2,0},{3,1},{4,6},{5,7},{6,4},{7,5},{8,10},{9,11},{10,... | collective-permute-start | bytes 49160 | tf_op jit(solution)/shard_map/ppermute | solution.py:379
  198.7 383.5 %all-gather.2.cloned.1.call-start = ((), (), s32[]{:S(2)}) async-start(), calls=%async_computation.2 | async-start | bytes 4718592 | tf_op jit(solution)/shard_map/all_gather | solution.py:1294
  198.7 78.9 %collective-permute-start.7 = (bf16[1024,2048]{1,0:T(8,128)(2,1)}, bf16[1024,2048]{1,0:T(8,128)(2,1)}, u32[]{:S(2)}, u32[]{:S(2)}) collective-permute-start(bf16[1024,2048]{1,0:T(8,128)(2,1)} %convolution_convert_fusion.1), channel_id=1, source_target_pairs={{0,1},{1,0},{2,3},{3,2},{4,5},{5,4},{6,7},{7,6},{8,9},{9,8},{10,11... | collective-permute-start | bytes 12582920 | tf_op jit(solution)/shard_map/ppermute | solution.py:379
  215.7 1.4 collective-permute-start.5
  217.4 3.8 collective-permute-start.6
  277.6 10.9 %copy-start = (bf16[2,1,256,2048]{3,2,1,0:T(8,128)(2,1)S(1)}, bf16[2,1,256,2048]{3,2,1,0:T(8,128)(2,1)}, u32[]{:S(2)}) copy-start(bf16[2,1,256,2048]{3,2,1,0:T(8,128)(2,1)} %param.12) | copy-start | bytes 6291460
  289.0 20.5 %copy-start.5 = (f32[8,1280]{1,0:T(8,128)S(1)}, f32[8,1280]{1,0:T(8,128)}, u32[]{:S(2)}) copy-start(f32[8,1280]{1,0:T(8,128)} %get-tuple-element.62) | copy-start | bytes 122884
  289.0 21.3 %copy-start.6 = (f32[8,1024]{1,0:T(8,128)S(1)}, f32[8,1024]{1,0:T(8,128)}, u32[]{:S(2)}) copy-start(f32[8,1024]{1,0:T(8,128)} %get-tuple-element.66) | copy-start | bytes 98308
  289.0 22.2 %copy-start.7 = (f32[8,128]{1,0:T(8,128)S(1)}, f32[8,128]{1,0:T(8,128)}, u32[]{:S(2)}) copy-start(f32[8,128]{1,0:T(8,128)} %get-tuple-element.64) | copy-start | bytes 12292
  555.8 8.9 %copy-start.1 = (bf16[1024,2048]{1,0:T(8,128)(2,1)S(1)}, bf16[1024,2048]{1,0:T(8,128)(2,1)}, u32[]{:S(2)}) copy-start(bf16[1024,2048]{1,0:T(8,128)(2,1)} %add_convert_fusion) | copy-start | bytes 12582916
  555.8 8.9 %copy-start.2 = (bf16[512,2048]{1,0:T(8,128)(2,1)S(1)}, bf16[512,2048]{1,0:T(8,128)(2,1)}, u32[]{:S(2)}) copy-start(bf16[512,2048]{1,0:T(8,128)(2,1)} %get-tuple-element.69) | copy-start | bytes 6291460
  564.8 7.1 %slice-start = ((s8[8388608]{0:T(1024)(128)(4,1)}), s8[4194304]{0:T(1024)(128)(4,1)S(1)}, s32[]{:S(2)}) async-start(s8[8388608]{0:T(1024)(128)(4,1)} %bitcast.94), calls=%async_computation.3 | async-start | bytes 8388608
  564.8 7.1 %slice-start.1 = ((s8[8388608]{0:T(1024)(128)(4,1)}), s8[4194304]{0:T(1024)(128)(4,1)S(1)}, s32[]{:S(2)}) async-start(s8[8388608]{0:T(1024)(128)(4,1)} %bitcast.94), calls=%async_computation.4 | async-start | bytes 8388608
  564.8 7.1 %copy-start.4 = (bf16[320,512]{1,0:T(8,128)(2,1)S(1)}, bf16[320,512]{1,0:T(8,128)(2,1)}, u32[]{:S(2)}) copy-start(bf16[320,512]{1,0:T(8,128)(2,1)} %get-tuple-element.73) | copy-start | bytes 983044
Sparse Core Ops, SparseCore 0:
  198.8 88.6 reduce-scatter.1
  289.8 100.5 all-gather.1

commit v6 on v5

--- a/solution.py
+++ b/solution.py
@@ -42,14 +42,14 @@
     return total, shifted
 
 
-def prepare(dims, own_ref, proj_ref, seg_col_ref, seg_row_ref, mask_ref, head_ref, cw_ref,
+def prepare(dims, own_ref, proj_ref, seg_row_ref, mask_ref, head_ref, cw_ref,
             mask_wide, visible_bias, step_wide, cum_wide, cum_rows, state_act, affinity):
     tokens, inner, state2, heads, local_heads, taps = dims
     for offset in range(taps - 1):
         mask_wide[offset] = jnp.broadcast_to(mask_ref[:, offset : offset + 1], (tokens, LANES))
     rows = lax.broadcasted_iota(jnp.int32, (tokens, tokens), 0)
     cols = lax.broadcasted_iota(jnp.int32, (tokens, tokens), 1)
-    visible = (rows >= cols) & (seg_col_ref[...] == seg_row_ref[...])
+    visible = (rows >= cols) & (mask_ref[:, taps - 1 : taps] == seg_row_ref[...])
     visible_bias[...] = jnp.where(visible, 0.0, -1e30)
     common = 2 * inner
     raw = proj_ref[:, common + state2 : common + state2 + heads]
@@ -94,11 +94,11 @@
     return lax.fori_loop(0, count // group, turn, carry)
 
 
-def forward_kernel(dims, own_ref, proj_ref, seg_col_ref, seg_row_ref, mask_ref, head_ref, cw_ref, chan_ref,
+def forward_kernel(dims, own_ref, proj_ref, seg_row_ref, mask_ref, head_ref, cw_ref, chan_ref,
                    gated_ref, square_ref, out_ref,
                    mask_wide, visible_bias, step_wide, cum_wide, cum_rows, state_act, affinity):
     tokens, inner, state2, heads, local_heads, taps = dims
-    prepare(dims, own_ref, proj_ref, seg_col_ref, seg_row_ref, mask_ref, head_ref, cw_ref,
+    prepare(dims, own_ref, proj_ref, seg_row_ref, mask_ref, head_ref, cw_ref,
             mask_wide, visible_bias, step_wide, cum_wide, cum_rows, state_act, affinity)
     lane = lax.broadcasted_iota(jnp.int32, (tokens, LANES), 1)
     first = lane < LANES // 2
@@ -139,7 +139,7 @@
     square_ref[...] = jnp.sum(squares, 1, keepdims=True)
 
 
-def backward_kernel(dims, own_ref, proj_ref, seg_col_ref, seg_row_ref, mask_ref, head_ref, cw_ref, chan_ref,
+def backward_kernel(dims, own_ref, proj_ref, seg_row_ref, mask_ref, head_ref, cw_ref, chan_ref,
                     stats_ref, gn_ref, out_ref,
                     gp_ref, grad_cw_ref, grad_chan_ref, grad_head_ref,
                     mask_wide, visible_bias, step_wide, cum_wide, cum_rows, state_act, affinity,
@@ -153,7 +153,7 @@
         grad_head_ref[...] = jnp.zeros_like(grad_head_ref)
 
     raw, step, log_decay, rows, cols = prepare(
-        dims, own_ref, proj_ref, seg_col_ref, seg_row_ref, mask_ref, head_ref, cw_ref,
+        dims, own_ref, proj_ref, seg_row_ref, mask_ref, head_ref, cw_ref,
         mask_wide, visible_bias, step_wide, cum_wide, cum_rows, state_act, affinity)
     grad_affinity[...] = jnp.zeros_like(grad_affinity)
     row_sums[...] = jnp.zeros_like(row_sums)
@@ -265,7 +265,6 @@
     in_specs = [
         pl.BlockSpec(memory_space=pltpu.SMEM),
         pl.BlockSpec((tokens, width), lambda s: (s + start, 0)),
-        pl.BlockSpec((None, tokens, 1), lambda s: (s + start, 0, 0)),
         pl.BlockSpec((None, 1, tokens), lambda s: (s + start, 0, 0)),
         pl.BlockSpec((None, tokens, 8), lambda s: (s + start, 0, 0)),
         fixed((8, LANES)),
@@ -1256,9 +1255,11 @@
     for offset in range(1, taps):
         equal = (seg_all[:, offset:] == seg_all[:, :-offset]).astype(F32)
         same.append(jnp.pad(equal, ((0, 0), (offset, 0))))
-    same = jnp.pad(jnp.stack(same, 2), ((0, 0), (0, 0), (0, 9 - taps)))
+    seg_wide = seg_all.astype(F32)
+    same.append(seg_wide)
+    same = jnp.pad(jnp.stack(same, 2), ((0, 0), (0, 0), (0, 8 - taps)))
     operands = (
-        me.astype(jnp.int32).reshape(1), projected, seg_all[:, :, None], seg_all[:, None, :], same,
+        me.astype(jnp.int32).reshape(1), projected, seg_wide[:, None, :], same,
         head_rows, conv_own, chan_rows,
     )
     gated, squares, scan_out = mix_forward(dims, operands)
@@ -1292,7 +1293,7 @@
             (head_rows, own_out, small_first[2], tok_out)
         )
         grad_w_out = lax.all_gather(own_out, "replica", axis=0, tiled=True).astype(F32)
-        operands = operands[:5] + (head_rows,) + operands[6:]
+        operands = operands[:4] + (head_rows,) + operands[5:]
         gp_last, *small_last = mix_backward(
             dims, operands, stats, grad_normed, scan_out, early, sequences - early
         )

time: 605 us -> 602 us (level)
  transfers between devices with their start and end apart: 10 -> 10, of which waited for: 3 -> 3; matrix products, arithmetic and copies ran while one was open for 19% -> 18% of each run, Pallas kernels for 59% -> 60%
where the time goes in v6:
time: 602 us; the launch traced here: 593 us
  Pallas kernels  436 us (72%)
  matrix products  78.6 us (13%)
  other arithmetic  39.7 us (7%)
  between operations  15 us (2%)
  local copies, waits for them, and re-layouts  13.4 us (2%)
    pallas_call x1, Pallas kernels, reduce_gradients(): pl.pallas_call(functools.partial(reduce_kernel, (chunks, counts, inner, d...  242 us
    pallas_call x1, Pallas kernels, gather_inputs(): pl.pallas_call(functools.partial(gather_kernel, full_inner, inner), in_sp...  83.6 us
    pallas_call x2, Pallas kernels, mix_backward(): pl.pallas_call(functools.partial(backward_kernel, dims), grid=(count,), i...  74.4 us
    dot_general x2, matrix products, contract_cols(): lax.dot_general(left, right, (((1,), (1,)), ((), ())), precision=precisio...  45.7 us
    pallas_call x1, Pallas kernels, mix_forward(): pl.pallas_call(functools.partial(forward_kernel, dims), grid=(total // to...  36.6 us
    dot_general x1, matrix products, contract_rows(): lax.dot_general(left, right, (((0,), (0,)), ((), ())), precision=precisio...  12.8 us
  transfers between devices with their start and end apart: 10, of which 3 were waited for; matrix products, arithmetic and copies ran while one was open for 18% of the time, Pallas kernels for 60%

profile of v6, /device:TPU:0, one launch (start us, length us, event | category | flops | bytes accessed | tf_op | source)
XLA Modules:
  0.0 592.7 jit_solution(12063067044439269166)
XLA Ops:
  7.2 0.8 reshape.221
  8.0 1.3 fusion.19.small_ref
  9.3 83.6 %gather_inputs.1 = (bf16[2048,2048]{1,0:T(8,128)(2,1)}, s32[4,4,128]{2,1,0:T(4,128)}, f32[4,48,128]{2,1,0:T(8,128)}, bf16[2368,2048]{1,0:T(8,128)(2,1)}) custom-call(bf16[512,2048]{1,0:T(8,128)(2,1)} %bitcast.90, s32[4,128]{1,0:T(4,128)} %bitcast.132, f32[48,128]{1,0:T(8,128)} %fusion.19.small_ref, bf16[8512,512]{1,0:T(8,128)(2,1)} %bitcast.93), custom_call_target="tpu_custom_call" | custom-call | bytes 209715200 | tf_op jit(solution)/shard_map/gather_inputs/pallas_call | solution.py:590
  92.9 1.7 collective-permute-start
  95.3 0.9 copy.107
  96.8 28.8 %fusion.31.proj_ref = f32[2048,2368]{1,0:T(8,128)} fusion(bf16[2048,2048]{1,0:T(8,128)(2,1)} %get-tuple-element.45.scaled_ref, bf16[2368,2048]{1,0:T(8,128)(2,1)} %get-tuple-element.46.cols_ref), kind=kOutput, calls=%fused_computation.83 | convolution fusion | flops 19864223744 | bytes 37486592 | tf_op jit(solution)/shard_map/dot_general | solution.py:26
  126.7 1.1 pad.49.mask_ref
  129.6 36.6 %mix_forward.1 = (bf16[2048,1024]{1,0:T(8,128)(2,1)}, f32[2048,1]{1,0:T(8,128)}, bf16[2048,1024]{1,0:T(8,128)(2,1)}) custom-call(s32[1]{0:T(128)} %bitcast.5.own_ref, f32[2048,2368]{1,0:T(8,128)} %fusion.31.proj_ref, f32[8,1,256]{2,1,0:T(1,128)} %bitcast.108, f32[8,256,8]{2,1,0:T(8,128)} %pad.49.mask_ref, f32[8,128]{1,0:T(8,128)} %select_maximum_fusion.3.head_ref, ...), custom_call_target="tpu_custom_call" | custom-call | flops 2147483648 | bytes 19398656 | tf_op jit(solution)/shard_map/mix_forward/pallas_call | solution.py:290
  166.2 1.6 reduce.2
  169.8 1.0 collective-permute-start.2
  170.8 9.3 %convolution_convert_fusion.1 = bf16[1024,2048]{1,0:T(8,128)(2,1)} fusion(bf16[1024,2048]{1,0:T(8,128)(2,1)} %param.23, bf16[2048,1024]{1,0:T(8,128)(2,1)} %get-tuple-element.50), kind=kOutput, calls=%fused_computation.18 | convolution fusion | flops 4297064448 | bytes 10485760 | tf_op jit(solution)/shard_map/dot_general | solution.py:1275
  180.4 2.9 fusion
  183.3 12.8 %convolution_convert_fusion = bf16[1024,2048]{1,0:T(8,128)(2,1)} fusion(bf16[2048,1024]{1,0:T(8,128)(2,1)S(1)} %fusion, bf16[512,2048]{1,0:T(8,128)(2,1)} %collective-permute-done.4, bf16[512,2048]{1,0:T(8,128)(2,1)} %collective-permute-done.3, bf16[512,2048]{1,0:T(8,128)(2,1)} %collective-permute-done, bf16[512,2048]{1,0:T(8,128)(2,1)S(1)} %bitcast.100), kind=kOutput, calls=%fused_computation.17 | convolution fusion | flops 8625586176 | bytes 16777216 | tf_op jit(solution)/shard_map/dot_general | solution.py:20
  196.4 16.9 %fusion.1 = (f32[2048]{0:T(1024)S(1)}, f32[2048,1024]{1,0:T(8,128)}) fusion(bf16[2048,1024]{1,0:T(8,128)(2,1)} %get-tuple-element.50, bf16[1024,2048]{1,0:T(8,128)(2,1)} %param.23, bf16[512,2048]{1,0:T(8,128)(2,1)} %collective-permute-done.4, bf16[512,2048]{1,0:T(8,128)(2,1)} %collective-permute-done.3, bf16[512,2048]{1,0:T(8,128)(2,1)} %collective-permute-done, ...), kind=kOutput, calls=%fused_computation.4 | convolution fusion | flops 8629778432 | bytes 25174016 | tf_op jit(solution)/shard_map/dot_general | solution.py:26
  213.7 0.8 collective-permute-done.5
  214.9 1.1 collective-permute-start.6
  216.0 2.7 collective-permute-done.6
  219.0 1.4 copy.91.stats_ref
  220.4 54.3 %mix_backward.2 = (bf16[1536,2368]{1,0:T(8,128)(2,1)}, f32[8,1280]{1,0:T(8,128)}, f32[8,1024]{1,0:T(8,128)}, f32[8,128]{1,0:T(8,128)}) custom-call(s32[1]{0:T(128)} %bitcast.5.own_ref, f32[2048,2368]{1,0:T(8,128)} %fusion.31.proj_ref, f32[8,1,256]{2,1,0:T(1,128)} %bitcast.109, f32[8,256,8]{2,1,0:T(8,128)} %pad.49.mask_ref, ...), custom_call_target="tpu_custom_call" | custom-call | flops 4831838208 | bytes 21823488 | tf_op jit(solution)/shard_map/mix_backward/pallas_call | solution.py:320
  274.7 10.8 %add_convert_fusion = bf16[1024,2048]{1,0:T(8,128)(2,1)} fusion(bf16[1024,2048]{1,0:T(8,128)(2,1)} %collective-permute-done.7, bf16[1024,2048]{1,0:T(8,128)(2,1)} %param.23, bf16[2048,1024]{1,0:T(8,128)(2,1)} %get-tuple-element.50), kind=kOutput, calls=%fused_computation.6 | convolution fusion | flops 4301258752 | bytes 14680064 | tf_op jit(solution)/shard_map/dot_general | solution.py:1290
  286.1 20.1 %mix_backward.3 = (bf16[512,2368]{1,0:T(8,128)(2,1)}, f32[8,1280]{1,0:T(8,128)}, f32[8,1024]{1,0:T(8,128)}, f32[8,128]{1,0:T(8,128)}) custom-call(s32[1]{0:T(128)} %bitcast.5.own_ref, f32[2048,2368]{1,0:T(8,128)} %fusion.31.proj_ref, f32[8,1,256]{2,1,0:T(1,128)} %bitcast.110, f32[8,256,8]{2,1,0:T(8,128)} %pad.49.mask_ref, ...), custom_call_target="tpu_custom_call" | custom-call | flops 1610612736 | bytes 7274496 | tf_op jit(solution)/shard_map/mix_backward/pallas_call | solution.py:320
  306.2 0.8 add.115
  307.0 0.8 add.117
  309.7 241.9 %reduce_gradients.1 = (bf16[8,1024,512]{2,1,0:T(8,128)(2,1)}, bf16[320,512]{1,0:T(8,128)(2,1)}, bf16[512,2048]{1,0:T(8,128)(2,1)}, bf16[512,2048]{1,0:T(8,128)(2...) custom-call(bf16[1536,2368]{1,0:T(8,128)(2,1)} %get-tuple-element.59, ...), custom_call_target="tpu_custom_call" | custom-call | flops 4194304 | bytes 1048576 | tf_op jit(solution)/shard_map/reduce_gradients/pallas_call | solution.py:1102
  551.5 0.9 slice.126
  552.5 1.5 dynamic-slice.5
  554.7 1.4 fusion.29
  556.1 0.7 slice_bitcast_fusion.1
  557.4 3.2 fusion.3
  561.4 7.1 %fusion.4 = (f32[512,2048]{1,0:T(8,128)}, bf16[512,2048]{1,0:T(8,128)(2,1)}) fusion(bf16[512,2048]{1,0:T(8,128)(2,1)} %get-tuple-element.70, bf16[512,2048]{1,0:T(8,128)(2,1)S(1)} %copy-done.2, f32[512]{0:T(512)S(1)} %fusion.24, f32[2048]{0:T(1024)S(1)} %bitcast.118, f32[512]{0:T(512)S(1)} %bitcast.128, bf16[2,1,256,2048]{3,2,1,0:T(8,128)(2,1)} %param.14, ...), kind=kLoop, calls=%fused_computation.12 | loop fusion | flops 16777216 | bytes 18888704 | tf_op jit(solution)/shard_map/sub | solution.py:1350
  568.5 10.3 %convert_bitcast_fusion = f32[512,8512]{0,1:T(8,128)} fusion(bf16[320,512]{1,0:T(8,128)(2,1)S(1)} %copy-done.4, bf16[8192,512]{1,0:T(8,128)(2,1)S(1)} %bitcast.96), kind=kLoop, calls=%fused_computation | loop fusion | flops 17432576 | bytes 26148864 | tf_op jit(solution)/shard_map/transpose | solution.py:1326
  578.8 6.7 %convert_element_type.125 = f32[1024,2048]{1,0:T(8,128)} convert(bf16[1024,2048]{1,0:T(8,128)(2,1)} %all-gather.2.cloned.1.call-done) | non-fusion elementwise | flops 2097152 | bytes 12582912 | tf_op jit(solution)/shard_map/convert_element_type | solution.py:1295
  (126 shorter events, 12.0 us)
Async XLA Ops:
  7.2 278.3 %reduce-scatter.2.cloned.1.call-start = ((), (), s32[]{:S(2)}) async-start(), calls=%async_computation.1 | async-start | bytes 4718592 | tf_op jit(solution)/shard_map/reduce_scatter | solution.py:1280
  9.3 83.6 %copy-start.3 = (bf16[2,1,256,2048]{3,2,1,0:T(8,128)(2,1)S(1)}, bf16[2,1,256,2048]{3,2,1,0:T(8,128)(2,1)}, u32[]{:S(2)}) copy-start(bf16[2,1,256,2048]{3,2,1,0:T(8,128)(2,1)} %param.14) | copy-start | bytes 6291460
  92.9 73.3 %collective-permute-start = (bf16[512,2048]{1,0:T(8,128)(2,1)S(1)}, bf16[512,2048]{1,0:T(8,128)(2,1)}, u32[]{:S(2)}, u32[]{:S(2)}) collective-permute-start(bf16[512,2048]{1,0:T(8,128)(2,1)S(1)} %bitcast.98), channel_id=1, source_target_pairs={{0,2},{1,3},{2,0},{3,1},{4,6},{5,7},{6,4},{7,5},{8,10},{9,11},{10,... | collective-permute-start | bytes 6291464 | tf_op jit(solution)/shard_map/ppermute | solution.py:378
  96.8 29.0 %copy-start.8 = (s32[4,4,128]{2,1,0:T(4,128)S(1)}, s32[4,4,128]{2,1,0:T(4,128)}, u32[]{:S(2)}) copy-start(s32[4,4,128]{2,1,0:T(4,128)} %get-tuple-element.43) | copy-start | bytes 24580
  96.8 29.0 %copy-start.10 = (bf16[1024]{0:T(1024)(128)(2,1)S(1)}, bf16[1024]{0:T(1024)(128)(2,1)}, u32[]{:S(2)}) copy-start(bf16[1024]{0:T(1024)(128)(2,1)} %param.22) | copy-start | bytes 6148
  96.8 29.0 %copy-start.11 = (bf16[16]{0:T(256)(128)(2,1)S(1)}, bf16[16]{0:T(256)(128)(2,1)}, u32[]{:S(2)}) copy-start(bf16[16]{0:T(256)(128)(2,1)} %param.21) | copy-start | bytes 100
  96.8 31.0 %copy-start.12 = (bf16[16]{0:T(256)(128)(2,1)S(1)}, bf16[16]{0:T(256)(128)(2,1)}, u32[]{:S(2)}) copy-start(bf16[16]{0:T(256)(128)(2,1)} %param.19) | copy-start | bytes 100
  96.8 31.0 %copy-start.13 = (bf16[16]{0:T(256)(128)(2,1)S(1)}, bf16[16]{0:T(256)(128)(2,1)}, u32[]{:S(2)}) copy-start(bf16[16]{0:T(256)(128)(2,1)} %param.20) | copy-start | bytes 100
  125.8 3.8 copy-start.5
  167.8 1.4 collective-permute-start.1
  168.4 14.9 %collective-permute-start.3 = (bf16[512,2048]{1,0:T(8,128)(2,1)S(1)}, bf16[512,2048]{1,0:T(8,128)(2,1)}, u32[]{:S(2)}, u32[]{:S(2)}) collective-permute-start(bf16[512,2048]{1,0:T(8,128)(2,1)S(1)} %bitcast.99), channel_id=1, source_target_pairs={{0,1},{1,0},{2,3},{3,2},{4,5},{5,4},{6,7},{7,6},{8,9},{9,8},{10,11... | collective-permute-start | bytes 6291464 | tf_op jit(solution)/shard_map/ppermute | solution.py:378
  168.5 14.8 %collective-permute-start.4 = (bf16[512,2048]{1,0:T(8,128)(2,1)}, bf16[512,2048]{1,0:T(8,128)(2,1)}, u32[]{:S(2)}, u32[]{:S(2)}) collective-permute-start(bf16[512,2048]{1,0:T(8,128)(2,1)} %collective-permute-done), channel_id=1, source_target_pairs={{0,1},{1,0},{2,3},{3,2},{4,5},{5,4},{6,7},{7,6},{8,9},{9,8},{10,11... | collective-permute-start | bytes 6291464 | tf_op jit(solution)/shard_map/ppermute | solution.py:378
  169.8 10.3 %collective-permute-start.2 = (f32[2,2048]{1,0:T(2,128)S(1)}, f32[2,2048]{1,0:T(2,128)S(1)}, u32[]{:S(2)}, u32[]{:S(2)}) collective-permute-start(f32[2,2048]{1,0:T(2,128)S(1)} %fusion.28), channel_id=1, source_target_pairs={{0,2},{1,3},{2,0},{3,1},{4,6},{5,7},{6,4},{7,5},{8,10},{9,11},{10,... | collective-permute-start | bytes 49160 | tf_op jit(solution)/shard_map/ppermute | solution.py:378
  196.2 382.6 %all-gather.2.cloned.1.call-start = ((), (), s32[]{:S(2)}) async-start(), calls=%async_computation.2 | async-start | bytes 4718592 | tf_op jit(solution)/shard_map/all_gather | solution.py:1295
  196.2 78.4 %collective-permute-start.7 = (bf16[1024,2048]{1,0:T(8,128)(2,1)}, bf16[1024,2048]{1,0:T(8,128)(2,1)}, u32[]{:S(2)}, u32[]{:S(2)}) collective-permute-start(bf16[1024,2048]{1,0:T(8,128)(2,1)} %convolution_convert_fusion.1), channel_id=1, source_target_pairs={{0,1},{1,0},{2,3},{3,2},{4,5},{5,4},{6,7},{7,6},{8,9},{9,8},{10,11... | collective-permute-start | bytes 12582920 | tf_op jit(solution)/shard_map/ppermute | solution.py:378
  213.2 1.3 collective-permute-start.5
  214.9 3.8 collective-permute-start.6
  274.6 10.8 %copy-start = (bf16[2,1,256,2048]{3,2,1,0:T(8,128)(2,1)S(1)}, bf16[2,1,256,2048]{3,2,1,0:T(8,128)(2,1)}, u32[]{:S(2)}) copy-start(bf16[2,1,256,2048]{3,2,1,0:T(8,128)(2,1)} %param.12) | copy-start | bytes 6291460
  286.0 20.2 %copy-start.6 = (f32[8,1280]{1,0:T(8,128)S(1)}, f32[8,1280]{1,0:T(8,128)}, u32[]{:S(2)}) copy-start(f32[8,1280]{1,0:T(8,128)} %get-tuple-element.62) | copy-start | bytes 122884
  286.0 21.0 %copy-start.7 = (f32[8,1024]{1,0:T(8,128)S(1)}, f32[8,1024]{1,0:T(8,128)}, u32[]{:S(2)}) copy-start(f32[8,1024]{1,0:T(8,128)} %get-tuple-element.66) | copy-start | bytes 98308
  286.0 21.9 %copy-start.9 = (f32[8,128]{1,0:T(8,128)S(1)}, f32[8,128]{1,0:T(8,128)}, u32[]{:S(2)}) copy-start(f32[8,128]{1,0:T(8,128)} %get-tuple-element.64) | copy-start | bytes 12292
  552.5 8.9 %copy-start.1 = (bf16[1024,2048]{1,0:T(8,128)(2,1)S(1)}, bf16[1024,2048]{1,0:T(8,128)(2,1)}, u32[]{:S(2)}) copy-start(bf16[1024,2048]{1,0:T(8,128)(2,1)} %add_convert_fusion) | copy-start | bytes 12582916
  552.5 8.9 %copy-start.2 = (bf16[512,2048]{1,0:T(8,128)(2,1)S(1)}, bf16[512,2048]{1,0:T(8,128)(2,1)}, u32[]{:S(2)}) copy-start(bf16[512,2048]{1,0:T(8,128)(2,1)} %get-tuple-element.69) | copy-start | bytes 6291460
  561.4 7.1 %slice-start = ((s8[8388608]{0:T(1024)(128)(4,1)}), s8[4194304]{0:T(1024)(128)(4,1)S(1)}, s32[]{:S(2)}) async-start(s8[8388608]{0:T(1024)(128)(4,1)} %bitcast.94), calls=%async_computation.3 | async-start | bytes 8388608
  561.4 7.1 %slice-start.1 = ((s8[8388608]{0:T(1024)(128)(4,1)}), s8[4194304]{0:T(1024)(128)(4,1)S(1)}, s32[]{:S(2)}) async-start(s8[8388608]{0:T(1024)(128)(4,1)} %bitcast.94), calls=%async_computation.4 | async-start | bytes 8388608
  561.4 7.1 %copy-start.4 = (bf16[320,512]{1,0:T(8,128)(2,1)S(1)}, bf16[320,512]{1,0:T(8,128)(2,1)}, u32[]{:S(2)}) copy-start(bf16[320,512]{1,0:T(8,128)(2,1)} %get-tuple-element.73) | copy-start | bytes 983044
Sparse Core Ops, SparseCore 0:
  196.3 88.8 reduce-scatter.1
  287.5 100.8 all-gather.1

commit v7 on v6

--- a/solution.py
+++ b/solution.py
@@ -625,7 +625,7 @@
 SHARED_AT = 4
 COLUMN_BLOCK = 256
 ROW_BLOCK = 256
-LANE_TILE = 1024
+LANE_TILE = 2048
 PER_TURN = 3
 AGAIN = 1
 TOKEN_PIECES = 8

time: 602 us -> 601 us (level)
  transfers between devices with their start and end apart: 10 -> 10, of which waited for: 3 -> 3; matrix products, arithmetic and copies ran while one was open for 18% -> 18% of each run, Pallas kernels for 60% -> 59%
where the time goes in v7:
time: 601 us; the launch traced here: 592 us
  Pallas kernels  436 us (73%)
  matrix products  78.7 us (13%)
  other arithmetic  39.7 us (7%)
  between operations  15 us (2%)
  local copies, waits for them, and re-layouts  13.6 us (2%)
    pallas_call x1, Pallas kernels, reduce_gradients(): pl.pallas_call(functools.partial(reduce_kernel, (chunks, counts, inner, d...  241 us
    pallas_call x1, Pallas kernels, gather_inputs(): pl.pallas_call(functools.partial(gather_kernel, full_inner, inner), in_sp...  83.6 us
    pallas_call x2, Pallas kernels, mix_backward(): pl.pallas_call(functools.partial(backward_kernel, dims), grid=(count,), i...  74.2 us
    dot_general x2, matrix products, contract_cols(): lax.dot_general(left, right, (((1,), (1,)), ((), ())), precision=precisio...  45.9 us
    pallas_call x1, Pallas kernels, mix_forward(): pl.pallas_call(functools.partial(forward_kernel, dims), grid=(total // to...  36.6 us
    dot_general x1, matrix products, contract_rows(): lax.dot_general(left, right, (((0,), (0,)), ((), ())), precision=precisio...  12.8 us
  transfers between devices with their start and end apart: 10, of which 3 were waited for; matrix products, arithmetic and copies ran while one was open for 18% of the time, Pallas kernels for 59%

profile of v7, /device:TPU:0, one launch (start us, length us, event | category | flops | bytes accessed | tf_op | source)
XLA Modules:
  0.0 592.4 jit_solution(15610734272410856984)
XLA Ops:
  7.2 0.8 reshape.221
  8.0 1.3 fusion.19.small_ref
  9.3 83.6 %gather_inputs.1 = (bf16[2048,2048]{1,0:T(8,128)(2,1)}, s32[4,4,128]{2,1,0:T(4,128)}, f32[4,48,128]{2,1,0:T(8,128)}, bf16[2368,2048]{1,0:T(8,128)(2,1)}) custom-call(bf16[512,2048]{1,0:T(8,128)(2,1)} %bitcast.90, s32[4,128]{1,0:T(4,128)} %bitcast.132, f32[48,128]{1,0:T(8,128)} %fusion.19.small_ref, bf16[8512,512]{1,0:T(8,128)(2,1)} %bitcast.93), custom_call_target="tpu_custom_call" | custom-call | bytes 209715200 | tf_op jit(solution)/shard_map/gather_inputs/pallas_call | solution.py:590
  92.9 1.7 collective-permute-start
  95.3 0.9 copy.107
  96.8 28.8 %fusion.31.proj_ref = f32[2048,2368]{1,0:T(8,128)} fusion(bf16[2048,2048]{1,0:T(8,128)(2,1)} %get-tuple-element.45.scaled_ref, bf16[2368,2048]{1,0:T(8,128)(2,1)} %get-tuple-element.46.cols_ref), kind=kOutput, calls=%fused_computation.83 | convolution fusion | flops 19864223744 | bytes 37486592 | tf_op jit(solution)/shard_map/dot_general | solution.py:26
  126.7 1.1 pad.49.mask_ref
  129.6 36.6 %mix_forward.1 = (bf16[2048,1024]{1,0:T(8,128)(2,1)}, f32[2048,1]{1,0:T(8,128)}, bf16[2048,1024]{1,0:T(8,128)(2,1)}) custom-call(s32[1]{0:T(128)} %bitcast.5.own_ref, f32[2048,2368]{1,0:T(8,128)} %fusion.31.proj_ref, f32[8,1,256]{2,1,0:T(1,128)} %bitcast.108, f32[8,256,8]{2,1,0:T(8,128)} %pad.49.mask_ref, f32[8,128]{1,0:T(8,128)} %select_maximum_fusion.3.head_ref, ...), custom_call_target="tpu_custom_call" | custom-call | flops 2147483648 | bytes 19398656 | tf_op jit(solution)/shard_map/mix_forward/pallas_call | solution.py:290
  166.2 1.6 reduce.2
  169.8 1.0 collective-permute-start.2
  170.9 9.3 %convolution_convert_fusion.1 = bf16[1024,2048]{1,0:T(8,128)(2,1)} fusion(bf16[1024,2048]{1,0:T(8,128)(2,1)} %param.23, bf16[2048,1024]{1,0:T(8,128)(2,1)} %get-tuple-element.50), kind=kOutput, calls=%fused_computation.18 | convolution fusion | flops 4297064448 | bytes 10485760 | tf_op jit(solution)/shard_map/dot_general | solution.py:1275
  180.4 2.9 fusion
  183.4 12.8 %convolution_convert_fusion = bf16[1024,2048]{1,0:T(8,128)(2,1)} fusion(bf16[2048,1024]{1,0:T(8,128)(2,1)S(1)} %fusion, bf16[512,2048]{1,0:T(8,128)(2,1)} %collective-permute-done.4, bf16[512,2048]{1,0:T(8,128)(2,1)} %collective-permute-done.3, bf16[512,2048]{1,0:T(8,128)(2,1)} %collective-permute-done, bf16[512,2048]{1,0:T(8,128)(2,1)S(1)} %bitcast.100), kind=kOutput, calls=%fused_computation.17 | convolution fusion | flops 8625586176 | bytes 16777216 | tf_op jit(solution)/shard_map/dot_general | solution.py:20
  196.4 17.1 %fusion.1 = (f32[2048]{0:T(1024)S(1)}, f32[2048,1024]{1,0:T(8,128)}) fusion(bf16[2048,1024]{1,0:T(8,128)(2,1)} %get-tuple-element.50, bf16[1024,2048]{1,0:T(8,128)(2,1)} %param.23, bf16[512,2048]{1,0:T(8,128)(2,1)} %collective-permute-done.4, bf16[512,2048]{1,0:T(8,128)(2,1)} %collective-permute-done.3, bf16[512,2048]{1,0:T(8,128)(2,1)} %collective-permute-done, ...), kind=kOutput, calls=%fused_computation.4 | convolution fusion | flops 8629778432 | bytes 25174016 | tf_op jit(solution)/shard_map/dot_general | solution.py:26
  214.0 0.8 collective-permute-done.5
  215.1 1.1 collective-permute-start.6
  216.3 2.7 collective-permute-done.6
  219.2 1.4 copy.91.stats_ref
  220.6 54.1 %mix_backward.2 = (bf16[1536,2368]{1,0:T(8,128)(2,1)}, f32[8,1280]{1,0:T(8,128)}, f32[8,1024]{1,0:T(8,128)}, f32[8,128]{1,0:T(8,128)}) custom-call(s32[1]{0:T(128)} %bitcast.5.own_ref, f32[2048,2368]{1,0:T(8,128)} %fusion.31.proj_ref, f32[8,1,256]{2,1,0:T(1,128)} %bitcast.109, f32[8,256,8]{2,1,0:T(8,128)} %pad.49.mask_ref, ...), custom_call_target="tpu_custom_call" | custom-call | flops 4831838208 | bytes 21823488 | tf_op jit(solution)/shard_map/mix_backward/pallas_call | solution.py:320
  274.7 10.8 %add_convert_fusion = bf16[1024,2048]{1,0:T(8,128)(2,1)} fusion(bf16[1024,2048]{1,0:T(8,128)(2,1)} %collective-permute-done.7, bf16[1024,2048]{1,0:T(8,128)(2,1)} %param.23, bf16[2048,1024]{1,0:T(8,128)(2,1)} %get-tuple-element.50), kind=kOutput, calls=%fused_computation.6 | convolution fusion | flops 4301258752 | bytes 14680064 | tf_op jit(solution)/shard_map/dot_general | solution.py:1290
  286.1 20.1 %mix_backward.3 = (bf16[512,2368]{1,0:T(8,128)(2,1)}, f32[8,1280]{1,0:T(8,128)}, f32[8,1024]{1,0:T(8,128)}, f32[8,128]{1,0:T(8,128)}) custom-call(s32[1]{0:T(128)} %bitcast.5.own_ref, f32[2048,2368]{1,0:T(8,128)} %fusion.31.proj_ref, f32[8,1,256]{2,1,0:T(1,128)} %bitcast.110, f32[8,256,8]{2,1,0:T(8,128)} %pad.49.mask_ref, ...), custom_call_target="tpu_custom_call" | custom-call | flops 1610612736 | bytes 7274496 | tf_op jit(solution)/shard_map/mix_backward/pallas_call | solution.py:320
  306.3 0.8 add.115
  307.0 0.8 add.117
  309.9 241.3 %reduce_gradients.1 = (bf16[8,1024,512]{2,1,0:T(8,128)(2,1)}, bf16[320,512]{1,0:T(8,128)(2,1)}, bf16[512,2048]{1,0:T(8,128)(2,1)}, bf16[512,2048]{1,0:T(8,128)(2...) custom-call(bf16[1536,2368]{1,0:T(8,128)(2,1)} %get-tuple-element.59, ...), custom_call_target="tpu_custom_call" | custom-call | flops 4194304 | bytes 1048576 | tf_op jit(solution)/shard_map/reduce_gradients/pallas_call | solution.py:1102
  551.2 0.9 slice.126
  552.2 1.5 dynamic-slice.5
  554.4 1.4 fusion.29
  555.8 0.7 slice_bitcast_fusion.1
  557.1 3.2 fusion.3
  561.1 7.1 %fusion.4 = (f32[512,2048]{1,0:T(8,128)}, bf16[512,2048]{1,0:T(8,128)(2,1)}) fusion(bf16[512,2048]{1,0:T(8,128)(2,1)} %get-tuple-element.70, bf16[512,2048]{1,0:T(8,128)(2,1)S(1)} %copy-done.2, f32[512]{0:T(512)S(1)} %fusion.24, f32[2048]{0:T(1024)S(1)} %bitcast.118, f32[512]{0:T(512)S(1)} %bitcast.128, bf16[2,1,256,2048]{3,2,1,0:T(8,128)(2,1)} %param.14, ...), kind=kLoop, calls=%fused_computation.12 | loop fusion | flops 16777216 | bytes 18888704 | tf_op jit(solution)/shard_map/sub | solution.py:1350
  568.2 10.3 %convert_bitcast_fusion = f32[512,8512]{0,1:T(8,128)} fusion(bf16[320,512]{1,0:T(8,128)(2,1)S(1)} %copy-done.4, bf16[8192,512]{1,0:T(8,128)(2,1)S(1)} %bitcast.96), kind=kLoop, calls=%fused_computation | loop fusion | flops 17432576 | bytes 26148864 | tf_op jit(solution)/shard_map/transpose | solution.py:1326
  578.5 6.7 %convert_element_type.125 = f32[1024,2048]{1,0:T(8,128)} convert(bf16[1024,2048]{1,0:T(8,128)(2,1)} %all-gather.2.cloned.1.call-done) | non-fusion elementwise | flops 2097152 | bytes 12582912 | tf_op jit(solution)/shard_map/convert_element_type | solution.py:1295
  (126 shorter events, 12.3 us)
Async XLA Ops:
  7.2 278.3 %reduce-scatter.2.cloned.1.call-start = ((), (), s32[]{:S(2)}) async-start(), calls=%async_computation.1 | async-start | bytes 4718592 | tf_op jit(solution)/shard_map/reduce_scatter | solution.py:1280
  9.3 83.6 %copy-start.3 = (bf16[2,1,256,2048]{3,2,1,0:T(8,128)(2,1)S(1)}, bf16[2,1,256,2048]{3,2,1,0:T(8,128)(2,1)}, u32[]{:S(2)}) copy-start(bf16[2,1,256,2048]{3,2,1,0:T(8,128)(2,1)} %param.14) | copy-start | bytes 6291460
  92.9 73.3 %collective-permute-start = (bf16[512,2048]{1,0:T(8,128)(2,1)S(1)}, bf16[512,2048]{1,0:T(8,128)(2,1)}, u32[]{:S(2)}, u32[]{:S(2)}) collective-permute-start(bf16[512,2048]{1,0:T(8,128)(2,1)S(1)} %bitcast.98), channel_id=1, source_target_pairs={{0,2},{1,3},{2,0},{3,1},{4,6},{5,7},{6,4},{7,5},{8,10},{9,11},{10,... | collective-permute-start | bytes 6291464 | tf_op jit(solution)/shard_map/ppermute | solution.py:378
  96.8 29.0 %copy-start.8 = (s32[4,4,128]{2,1,0:T(4,128)S(1)}, s32[4,4,128]{2,1,0:T(4,128)}, u32[]{:S(2)}) copy-start(s32[4,4,128]{2,1,0:T(4,128)} %get-tuple-element.43) | copy-start | bytes 24580
  96.8 29.0 %copy-start.10 = (bf16[1024]{0:T(1024)(128)(2,1)S(1)}, bf16[1024]{0:T(1024)(128)(2,1)}, u32[]{:S(2)}) copy-start(bf16[1024]{0:T(1024)(128)(2,1)} %param.22) | copy-start | bytes 6148
  96.8 29.0 %copy-start.11 = (bf16[16]{0:T(256)(128)(2,1)S(1)}, bf16[16]{0:T(256)(128)(2,1)}, u32[]{:S(2)}) copy-start(bf16[16]{0:T(256)(128)(2,1)} %param.21) | copy-start | bytes 100
  96.8 31.0 %copy-start.12 = (bf16[16]{0:T(256)(128)(2,1)S(1)}, bf16[16]{0:T(256)(128)(2,1)}, u32[]{:S(2)}) copy-start(bf16[16]{0:T(256)(128)(2,1)} %param.19) | copy-start | bytes 100
  96.8 31.0 %copy-start.13 = (bf16[16]{0:T(256)(128)(2,1)S(1)}, bf16[16]{0:T(256)(128)(2,1)}, u32[]{:S(2)}) copy-start(bf16[16]{0:T(256)(128)(2,1)} %param.20) | copy-start | bytes 100
  125.8 3.8 copy-start.5
  167.8 1.5 collective-permute-start.1
  168.4 14.9 %collective-permute-start.3 = (bf16[512,2048]{1,0:T(8,128)(2,1)S(1)}, bf16[512,2048]{1,0:T(8,128)(2,1)}, u32[]{:S(2)}, u32[]{:S(2)}) collective-permute-start(bf16[512,2048]{1,0:T(8,128)(2,1)S(1)} %bitcast.99), channel_id=1, source_target_pairs={{0,1},{1,0},{2,3},{3,2},{4,5},{5,4},{6,7},{7,6},{8,9},{9,8},{10,11... | collective-permute-start | bytes 6291464 | tf_op jit(solution)/shard_map/ppermute | solution.py:378
  168.5 14.8 %collective-permute-start.4 = (bf16[512,2048]{1,0:T(8,128)(2,1)}, bf16[512,2048]{1,0:T(8,128)(2,1)}, u32[]{:S(2)}, u32[]{:S(2)}) collective-permute-start(bf16[512,2048]{1,0:T(8,128)(2,1)} %collective-permute-done), channel_id=1, source_target_pairs={{0,1},{1,0},{2,3},{3,2},{4,5},{5,4},{6,7},{7,6},{8,9},{9,8},{10,11... | collective-permute-start | bytes 6291464 | tf_op jit(solution)/shard_map/ppermute | solution.py:378
  169.8 10.3 %collective-permute-start.2 = (f32[2,2048]{1,0:T(2,128)S(1)}, f32[2,2048]{1,0:T(2,128)S(1)}, u32[]{:S(2)}, u32[]{:S(2)}) collective-permute-start(f32[2,2048]{1,0:T(2,128)S(1)} %fusion.28), channel_id=1, source_target_pairs={{0,2},{1,3},{2,0},{3,1},{4,6},{5,7},{6,4},{7,5},{8,10},{9,11},{10,... | collective-permute-start | bytes 49160 | tf_op jit(solution)/shard_map/ppermute | solution.py:378
  196.2 382.3 %all-gather.2.cloned.1.call-start = ((), (), s32[]{:S(2)}) async-start(), calls=%async_computation.2 | async-start | bytes 4718592 | tf_op jit(solution)/shard_map/all_gather | solution.py:1295
  196.2 78.4 %collective-permute-start.7 = (bf16[1024,2048]{1,0:T(8,128)(2,1)}, bf16[1024,2048]{1,0:T(8,128)(2,1)}, u32[]{:S(2)}, u32[]{:S(2)}) collective-permute-start(bf16[1024,2048]{1,0:T(8,128)(2,1)} %convolution_convert_fusion.1), channel_id=1, source_target_pairs={{0,1},{1,0},{2,3},{3,2},{4,5},{5,4},{6,7},{7,6},{8,9},{9,8},{10,11... | collective-permute-start | bytes 12582920 | tf_op jit(solution)/shard_map/ppermute | solution.py:378
  213.5 1.4 collective-permute-start.5
  215.1 3.8 collective-permute-start.6
  274.7 10.8 %copy-start = (bf16[2,1,256,2048]{3,2,1,0:T(8,128)(2,1)S(1)}, bf16[2,1,256,2048]{3,2,1,0:T(8,128)(2,1)}, u32[]{:S(2)}) copy-start(bf16[2,1,256,2048]{3,2,1,0:T(8,128)(2,1)} %param.12) | copy-start | bytes 6291460
  286.1 20.2 %copy-start.6 = (f32[8,1280]{1,0:T(8,128)S(1)}, f32[8,1280]{1,0:T(8,128)}, u32[]{:S(2)}) copy-start(f32[8,1280]{1,0:T(8,128)} %get-tuple-element.62) | copy-start | bytes 122884
  286.1 21.0 %copy-start.7 = (f32[8,1024]{1,0:T(8,128)S(1)}, f32[8,1024]{1,0:T(8,128)}, u32[]{:S(2)}) copy-start(f32[8,1024]{1,0:T(8,128)} %get-tuple-element.66) | copy-start | bytes 98308
  286.1 21.9 %copy-start.9 = (f32[8,128]{1,0:T(8,128)S(1)}, f32[8,128]{1,0:T(8,128)}, u32[]{:S(2)}) copy-start(f32[8,128]{1,0:T(8,128)} %get-tuple-element.64) | copy-start | bytes 12292
  552.2 8.9 %copy-start.1 = (bf16[1024,2048]{1,0:T(8,128)(2,1)S(1)}, bf16[1024,2048]{1,0:T(8,128)(2,1)}, u32[]{:S(2)}) copy-start(bf16[1024,2048]{1,0:T(8,128)(2,1)} %add_convert_fusion) | copy-start | bytes 12582916
  552.2 8.9 %copy-start.2 = (bf16[512,2048]{1,0:T(8,128)(2,1)S(1)}, bf16[512,2048]{1,0:T(8,128)(2,1)}, u32[]{:S(2)}) copy-start(bf16[512,2048]{1,0:T(8,128)(2,1)} %get-tuple-element.69) | copy-start | bytes 6291460
  561.1 7.1 %slice-start = ((s8[8388608]{0:T(1024)(128)(4,1)}), s8[4194304]{0:T(1024)(128)(4,1)S(1)}, s32[]{:S(2)}) async-start(s8[8388608]{0:T(1024)(128)(4,1)} %bitcast.94), calls=%async_computation.3 | async-start | bytes 8388608
  561.1 7.1 %slice-start.1 = ((s8[8388608]{0:T(1024)(128)(4,1)}), s8[4194304]{0:T(1024)(128)(4,1)S(1)}, s32[]{:S(2)}) async-start(s8[8388608]{0:T(1024)(128)(4,1)} %bitcast.94), calls=%async_computation.4 | async-start | bytes 8388608
  561.1 7.1 %copy-start.4 = (bf16[320,512]{1,0:T(8,128)(2,1)S(1)}, bf16[320,512]{1,0:T(8,128)(2,1)}, u32[]{:S(2)}) copy-start(bf16[320,512]{1,0:T(8,128)(2,1)} %get-tuple-element.73) | copy-start | bytes 983044
Sparse Core Ops, SparseCore 0:
  196.3 88.8 reduce-scatter.1
  287.6 100.8 all-gather.1
